TPU v7x, 32 devices: a whole 2x2x4 slice. The times are simulated.
32 devices in a mesh: dp: 8 (over z, x), segment: 4 (over y, core).
Axes of the slice: x: 2, y: 2, z: 4, core: 2. Of those that a mesh axis runs over, the one named last changes fastest.
Arguments:
- query_cache: bfloat16 [256, 4096], P(('dp', 'segment')), may hold values from -0.125 to 0.125, as said below
- passage_cache: bfloat16 [256, 4096], P(('dp', 'segment')), may hold values from -0.125 to 0.125, as said below
- hard_offsets: int32 [256, 1], P(('dp', 'segment')), may hold values from 0 to 127
- passage_lengths: int32 [8], replicated, may hold values from 1 to 64, 128 in all
- segment_inputs: bfloat16 [4, 128, 4096], P('segment', 'dp'), may hold values from -6 to 6
- segment_cotangents: bfloat16 [4, 128, 4096], P('segment', 'dp'), may hold values from -6 to 6
- norm_gain: float32 [4, 4096], P('segment'), may hold values from 0.5 to 1.5
- gate_weight: bfloat16 [4, 4096, 14336], P('segment', None, 'dp'), may hold values from -0.09375 to 0.09375
- up_weight: bfloat16 [4, 4096, 14336], P('segment', None, 'dp'), may hold values from -0.09375 to 0.09375
- down_weight: bfloat16 [4, 14336, 4096], P('segment', 'dp'), may hold values from -0.046875 to 0.046875
Outputs:
- query_grads: bfloat16 [256, 4096], P(('dp', 'segment'))
- passage_grads: bfloat16 [256, 4096], P(('dp', 'segment'))
- input_grads: bfloat16 [4, 128, 4096], P('segment', 'dp')
- gate_grads: bfloat16 [4, 4096, 14336], P('segment', None, 'dp')
- up_grads: bfloat16 [4, 4096, 14336], P('segment', None, 'dp')
- down_grads: bfloat16 [4, 14336, 4096], P('segment', 'dp')
- gain_grads: float32 [4, 4096], P('segment')
Inputs may be any that keep to these rules, and one draw needn't show every extreme that they name: Query i's hard negative k is passage (i // 128) * 128 + hard_offsets[i, k]. `passage_lengths`: the lengths sum to 128; the longest is exactly 64. `query_cache`: cached query embeddings, no row zero. `passage_cache`: cached passage embeddings, no row zero.
All inputs are finite; a program needn't handle non-finite values.
Results may differ from a plain program's by a relative error of at most 0.0071.
Values may be sent and summed in bfloat16 or wider, within the bound.
No kernel may reach another device: no remote copies, remote signals or barrier semaphores. Data moves between devices by JAX's collectives and lax.ppermute only.
A program may use at most 192 MiB of HBM per device.

v0:
```python
import jax
import jax.numpy as jnp
from jax import lax
from jax.sharding import PartitionSpec as P

HN_BLOCK = 128


TAU = 0.02
HN_WEIGHT = 64.0
EPS_NORM = 1e-06
EPS_RMS = 1e-05


def from_root(block, axis, holder):
    block = jnp.where(lax.axis_index(axis) == holder, block, jnp.zeros_like(block))
    return lax.psum(block, axis)


def unit_rows(values):
    widened = values.astype(jnp.float32)
    inverse = lax.rsqrt(jnp.sum(widened * widened, axis=-1, keepdims=True) + EPS_NORM)
    return (widened * inverse, inverse)


def unit_back(gradient, unit_value, inverse):
    return inverse * (
        gradient - unit_value * jnp.sum(gradient * unit_value, axis=-1, keepdims=True)
    )


def hard_weights(hard_offsets, first_row, column_index):
    row_index = first_row + jnp.arange(hard_offsets.shape[0], dtype=jnp.int32)
    picked = row_index // HN_BLOCK * HN_BLOCK
    picked = picked[:, None] + hard_offsets
    tallies = (picked == column_index[None, :]).astype(jnp.float32)
    return 1.0 + HN_WEIGHT * tallies


def mean_pool_back(passage_lengths, token_index, rows):
    last_tokens = jnp.cumsum(passage_lengths) - 1
    first_tokens = last_tokens - passage_lengths + 1
    member = (token_index[:, None] >= first_tokens[None, :]) & (
        token_index[:, None] <= last_tokens[None, :]
    )
    selector = member.astype(jnp.float32) / passage_lengths.astype(jnp.float32)[None, :]
    return jnp.dot(selector, rows.astype(jnp.float32), precision=lax.Precision.HIGHEST).astype(
        jnp.bfloat16
    )


def rms_rows(values):
    widened = values.astype(jnp.float32)
    inverse = lax.rsqrt(jnp.mean(widened * widened, axis=-1, keepdims=True) + EPS_RMS)
    return (widened * inverse, inverse)


def local(
    query_cache,
    passage_cache,
    hard_offsets,
    passage_lengths,
    segment_inputs,
    segment_cotangents,
    norm_gain,
    gate_weight,
    up_weight,
    down_weight,
):
    rows_here = query_cache.shape[0]
    first_row = lax.axis_index(("dp", "segment")) * rows_here
    query_unit, query_inverse = unit_rows(query_cache)
    passage_unit, passage_inverse = unit_rows(passage_cache)
    query_low = query_unit.astype(jnp.bfloat16)
    passage_low = passage_unit.astype(jnp.bfloat16)
    all_passages = lax.all_gather(passage_low, ("dp", "segment"), axis=0, tiled=True)
    column_index = jnp.arange(all_passages.shape[0], dtype=jnp.int32)
    scores = jnp.dot(query_low, all_passages.T, preferred_element_type=jnp.float32) / TAU
    weights = hard_weights(hard_offsets, first_row, column_index)
    weighted = weights * jnp.exp(scores)
    totals = jnp.sum(weighted, axis=1, keepdims=True)
    own_index = first_row + jnp.arange(rows_here, dtype=jnp.int32)
    positive = (own_index[:, None] == column_index[None, :]).astype(jnp.float32)
    dscore = (weighted / totals - positive).astype(jnp.bfloat16)
    query_dir = jnp.dot(dscore, all_passages, preferred_element_type=jnp.float32) / TAU
    query_grads = unit_back(query_dir, query_unit, query_inverse).astype(jnp.bfloat16)
    offsets_wide = hard_offsets.astype(jnp.float32)
    all_totals, all_offsets = (
        lax.all_gather(totals[:, 0], ("dp", "segment"), axis=0, tiled=True),
        lax.all_gather(offsets_wide, ("dp", "segment"), axis=0, tiled=True),
    )
    block_rows = lax.all_gather(query_low, ("dp", "segment"), axis=0, tiled=True)
    length = block_rows.shape[0]
    block_scores = jnp.dot(block_rows, passage_low.T, preferred_element_type=jnp.float32) / TAU
    block_offsets = all_offsets.astype(jnp.int32)
    block_weights = hard_weights(block_offsets, jnp.int32(0), own_index)
    block_weighted = block_weights * jnp.exp(block_scores)
    block_index = jnp.arange(length, dtype=jnp.int32)
    block_positive = (block_index[:, None] == own_index[None, :]).astype(jnp.float32)
    block_dscore = (block_weighted / all_totals[:, None] - block_positive).astype(jnp.bfloat16)
    passage_dir = jnp.dot(block_dscore.T, block_rows, preferred_element_type=jnp.float32) / TAU
    passage_grads = unit_back(passage_dir, passage_unit, passage_inverse).astype(jnp.bfloat16)
    batch_rows = from_root(passage_grads, "dp", 0)
    section = lax.axis_index("segment")
    last_section = lax.axis_size("segment") - 1
    token_count = segment_inputs.shape[1]
    inputs = segment_inputs[0]
    cotangent_given = segment_cotangents[0]
    gain_row = norm_gain[0]
    gate_matrix = gate_weight[0]
    up_matrix = up_weight[0]
    down_matrix = down_weight[0]
    token_index = lax.axis_index("dp") * token_count + jnp.arange(token_count, dtype=jnp.int32)
    pooled = mean_pool_back(passage_lengths, token_index, batch_rows)
    cotangent = jnp.where(section == last_section, pooled, cotangent_given)
    unit_local, inverse = rms_rows(inputs)
    normed_local = (unit_local * gain_row).astype(jnp.bfloat16)
    normed = lax.all_gather(normed_local, "dp", axis=0, tiled=True)
    gate_value = jnp.dot(normed, gate_matrix, preferred_element_type=jnp.float32)
    up_value = jnp.dot(normed, up_matrix, preferred_element_type=jnp.float32)
    sigmoid_gate = jax.nn.sigmoid(gate_value)
    activation = gate_value * sigmoid_gate
    hidden = (activation * up_value).astype(jnp.bfloat16)
    full_cotangent = lax.all_gather(cotangent, "dp", axis=0, tiled=True)
    hidden_delta = jnp.dot(full_cotangent, down_matrix.T, preferred_element_type=jnp.float32)
    up_delta = (hidden_delta * activation).astype(jnp.bfloat16)
    gate_delta = (
        hidden_delta * up_value * sigmoid_gate * (1.0 + gate_value * (1.0 - sigmoid_gate))
    ).astype(jnp.bfloat16)
    down_grads = jnp.dot(hidden.T, full_cotangent, preferred_element_type=jnp.float32).astype(
        jnp.bfloat16
    )
    gate_grads = jnp.dot(normed.T, gate_delta, preferred_element_type=jnp.float32).astype(
        jnp.bfloat16
    )
    up_grads = jnp.dot(normed.T, up_delta, preferred_element_type=jnp.float32).astype(jnp.bfloat16)
    normed_delta = lax.psum_scatter(
        jnp.dot(gate_delta, gate_matrix.T, preferred_element_type=jnp.float32)
        + jnp.dot(up_delta, up_matrix.T, preferred_element_type=jnp.float32),
        "dp",
        scatter_dimension=0,
        tiled=True,
    )
    gain_total = lax.psum(jnp.sum(normed_delta * unit_local, axis=0), "dp")
    scaled_delta = normed_delta * gain_row
    input_grad = cotangent.astype(jnp.float32) + inverse * (
        scaled_delta - unit_local * jnp.mean(scaled_delta * unit_local, axis=-1, keepdims=True)
    )
    return (
        query_grads,
        passage_grads,
        input_grad.astype(jnp.bfloat16)[None],
        gate_grads[None],
        up_grads[None],
        down_grads[None],
        gain_total[None],
    )


def solution(mesh):
    placed = (
        P(("dp", "segment"), None),
        P(("dp", "segment"), None),
        P(("dp", "segment"), None),
        P(),
        P("segment", "dp", None),
        P("segment", "dp", None),
        P("segment", None),
        P("segment", None, "dp"),
        P("segment", None, "dp"),
        P("segment", "dp", None),
    )
    return jax.shard_map(
        local,
        mesh=mesh,
        in_specs=placed,
        out_specs=(
            P(("dp", "segment"), None),
            P(("dp", "segment"), None),
            P("segment", "dp", None),
            P("segment", None, "dp"),
            P("segment", None, "dp"),
            P("segment", "dp", None),
            P("segment", None),
        ),
        check_vma=False,
    )
```

profile of v0, /device:TPU:0, one launch (start us, length us, event | category | flops | bytes accessed | tf_op | source)
XLA Modules:
  0.0 430.7 jit_solution(1563937213957629825)
XLA Ops:
  8.2 1.6 fusion.39
  10.8 1.6 fusion.42
  15.0 55.6 %all-gather.5.cloned.1.call-done = bf16[256,4096]{1,0:T(8,128)(2,1)} async-done(((bf16[8,4096]{1,0:T(8,128)(2,1)}), bf16[256,4096]{1,0:T(8,128)(2,1)}) %all-gather.5.cloned.1.call-update) | async-done | bytes 2097168 | tf_op jit(solution)/shard_map/all_gather | solution.py:76
  70.6 2.4 fusion.85
  73.2 38.6 %all-reduce.2 = (f32[256]{0:T(256)S(1)}, f32[256]{0:T(256)S(1)}) all-reduce(f32[256]{0:T(256)S(1)} %dynamic-update-slice.1, f32[256]{0:T(256)S(1)} %bitcast_dynamic-update-slice_fusion), channel_id=1, replica_groups=mesh['dp'=8,'segment'=4] {'dp','segment'}, use_global_device_ids=true, to_apply=%add.1 | all-reduce | flops 512 | bytes 4096
  111.8 17.5 %all-gather.7.cloned.1.call-done = bf16[256,4096]{1,0:T(8,128)(2,1)} async-done(((bf16[8,4096]{1,0:T(8,128)(2,1)}), bf16[256,4096]{1,0:T(8,128)(2,1)}) %all-gather.7.cloned.1.call-update) | async-done | bytes 2097168 | tf_op jit(solution)/shard_map/all_gather | solution.py:92
  129.3 3.9 fusion.49
  133.2 1.6 broadcast_select_fusion
  134.9 1.7 fusion.29
  138.2 64.1 %all-reduce.5.cloned.1.call-done = bf16[8,4096]{1,0:T(8,128)(2,1)} async-done(((bf16[8,4096]{1,0:T(8,128)(2,1)}), bf16[8,4096]{1,0:T(8,128)(2,1)}) %all-reduce.5.cloned.1.call-update) | async-done | bytes 65552 | tf_op jit(solution)/shard_map/psum | solution.py:17
  202.4 1.9 fusion.16
  204.5 40.5 %all-gather.11.cloned.1.call-done = bf16[128,4096]{1,0:T(8,128)(2,1)} async-done(((bf16[16,4096]{1,0:T(8,128)(2,1)}), bf16[128,4096]{1,0:T(8,128)(2,1)}) %all-gather.11.cloned.1.call-update) | async-done | bytes 1048592 | tf_op jit(solution)/shard_map/all_gather | solution.py:118
  245.0 7.6 %fusion.2 = f32[128,1792]{1,0:T(8,128)S(1)} fusion(bf16[128,4096]{1,0:T(8,128)(2,1)} %all-gather.11.cloned.1.call-done, bf16[1,4096,1792]{2,1,0:T(8,128)(2,1)} %param.17), kind=kOutput, calls=%fused_computation.5 | convolution fusion | flops 1879048192 | bytes 16646144 | tf_op jit(solution)/shard_map/dot_general | solution.py:119
  252.7 7.6 %fusion.6 = f32[128,1792]{1,0:T(8,128)S(1)} fusion(bf16[128,4096]{1,0:T(8,128)(2,1)S(1)} %copy-done, bf16[1,4096,1792]{2,1,0:T(8,128)(2,1)} %param.18), kind=kOutput, calls=%fused_computation.9 | convolution fusion | flops 1879048192 | bytes 16646144 | tf_op jit(solution)/shard_map/dot_general | solution.py:120
  260.4 25.6 %all-gather.9.cloned.1.call-done = bf16[128,4096]{1,0:T(8,128)(2,1)} async-done(((bf16[16,4096]{1,0:T(8,128)(2,1)}), bf16[128,4096]{1,0:T(8,128)(2,1)}) %all-gather.9.cloned.1.call-update) | async-done | bytes 1048592 | tf_op jit(solution)/shard_map/all_gather | solution.py:124
  286.0 10.6 %multiply_convert_fusion.1 = (bf16[128,1792]{1,0:T(8,128)(2,1)S(1)}, bf16[128,1792]{1,0:T(8,128)(2,1)S(1)}) fusion(f32[128,1792]{1,0:T(8,128)S(1)} %fusion.2, f32[128,1792]{1,0:T(8,128)S(1)} %fusion.6, bf16[128,4096]{1,0:T(8,128)(2,1)} %all-gather.9.cloned.1.call-done, bf16[1,1792,4096]{2,1,0:T(8,128)(2,1)} %param.19), kind=kOutput, calls=%fused_computation.31 | convolution fusion | flops 1882030080 | bytes 18481152 | tf_op jit(solution)/shard_map/dot_general | solution.py:125
  296.6 10.3 %fusion = f32[128,4096]{1,0:T(8,128)S(1)} fusion(bf16[128,1792]{1,0:T(8,128)(2,1)S(1)} %get-tuple-element.14, bf16[1,4096,1792]{2,1,0:T(8,128)(2,1)} %param.17), kind=kOutput, calls=%fused_computation.3 | convolution fusion | flops 1879048192 | bytes 17235968 | tf_op jit(solution)/shard_map/dot_general | solution.py:138
  307.0 11.6 %fusion.13 = f32[128,4096]{1,0:T(8,128)} fusion(f32[128,4096]{1,0:T(8,128)S(1)} %fusion, bf16[128,1792]{1,0:T(8,128)(2,1)S(1)} %get-tuple-element.13, bf16[1,4096,1792]{2,1,0:T(8,128)(2,1)} %param.18), kind=kOutput, calls=%fused_computation.16 | convolution fusion | flops 1879572480 | bytes 19333120 | tf_op jit(solution)/shard_map/dot_general | solution.py:139
  319.9 8.8 %fusion.11 = bf16[1,4096,1792]{2,1,0:T(8,128)(2,1)} fusion(bf16[128,4096]{1,0:T(8,128)(2,1)S(1)} %copy-done, bf16[128,1792]{1,0:T(8,128)(2,1)} %copy-done.9), kind=kOutput, calls=%fused_computation.14 | convolution fusion | flops 1886388224 | bytes 16187392 | tf_op jit(solution)/shard_map/dot_general | solution.py:136
  328.7 7.6 %fusion.10 = bf16[1,4096,1792]{2,1,0:T(8,128)(2,1)} fusion(bf16[128,4096]{1,0:T(8,128)(2,1)S(1)} %copy-done, bf16[128,1792]{1,0:T(8,128)(2,1)S(1)} %copy-done.8), kind=kOutput, calls=%fused_computation.13 | convolution fusion | flops 1886388224 | bytes 16187392 | tf_op jit(solution)/shard_map/dot_general | solution.py:133
  336.3 7.6 %fusion.12 = bf16[1,1792,4096]{2,1,0:T(8,128)(2,1)} fusion(bf16[128,4096]{1,0:T(8,128)(2,1)S(1)} %copy-done.11, f32[128,1792]{1,0:T(8,128)S(1)} %copy-done.5, f32[128,1792]{1,0:T(8,128)S(1)} %copy-done.3), kind=kOutput, calls=%fused_computation.15 | convolution fusion | flops 1887764480 | bytes 17563648 | tf_op jit(solution)/shard_map/dot_general | solution.py:130
  343.9 41.4 %reduce-scatter.2.cloned.1.call-done = f32[16,4096]{1,0:T(8,128)} async-done(((f32[128,4096]{1,0:T(8,128)}), f32[16,4096]{1,0:T(8,128)}) %reduce-scatter.2.cloned.1.call-update) | async-done | bytes 262160 | tf_op jit(solution)/shard_map/reduce_scatter | solution.py:137
  386.5 35.6 %psum.15 = f32[1,4096]{1,0:T(1,128)} all-reduce(f32[1,4096]{1,0:T(1,128)S(1)} %bitcast.66), channel_id=1, replica_groups=mesh['dp'=8,'segment'=4] {'dp'}, use_global_device_ids=true, to_apply=%region_11.12 | all-reduce | flops 4096 | bytes 32768 | tf_op jit(solution)/shard_map/psum | solution.py:144
  422.1 1.7 fusion.54
  (62 shorter events, 9.4 us)
Async XLA Ops:
  7.2 63.4 %all-gather.5.cloned.1.call-start = ((), (), s32[]{:S(2)}) async-start(), calls=%async_computation.1 | async-start | bytes 2162688 | tf_op jit(solution)/shard_map/all_gather | solution.py:76
  9.8 119.5 %all-gather.7.cloned.1.call-start = ((), (), s32[]{:S(2)}) async-start(), calls=%async_computation.2 | async-start | bytes 2162688 | tf_op jit(solution)/shard_map/all_gather | solution.py:92
  12.4 189.9 %all-reduce.5.cloned.1.call-start = ((), (), s32[]{:S(2)}) async-start(), calls=%async_computation.3 | async-start | bytes 131072 | tf_op jit(solution)/shard_map/psum | solution.py:17
  134.9 110.2 %all-gather.11.cloned.1.call-start = ((), (), s32[]{:S(2)}) async-start(), calls=%async_computation.5 | async-start | bytes 1179648 | tf_op jit(solution)/shard_map/all_gather | solution.py:118
  136.6 149.4 %all-gather.9.cloned.1.call-start = ((), (), s32[]{:S(2)}) async-start(), calls=%async_computation.4 | async-start | bytes 1179648 | tf_op jit(solution)/shard_map/all_gather | solution.py:124
  204.3 181.0 %reduce-scatter.2.cloned.1.call-start = ((), (), s32[]{:S(2)}) async-start(), calls=%async_computation.6 | async-start | bytes 2359296 | tf_op jit(solution)/shard_map/reduce_scatter | solution.py:137
  245.0 7.7 %copy-start = (bf16[128,4096]{1,0:T(8,128)(2,1)S(1)}, bf16[128,4096]{1,0:T(8,128)(2,1)}, u32[]{:S(2)}) copy-start(bf16[128,4096]{1,0:T(8,128)(2,1)} %all-gather.11.cloned.1.call-done) | copy-start | bytes 3145732
  252.7 43.9 %copy-start.2 = (f32[128,1792]{1,0:T(8,128)}, f32[128,1792]{1,0:T(8,128)S(1)}, u32[]{:S(2)}) copy-start(f32[128,1792]{1,0:T(8,128)S(1)} %fusion.2) | copy-start | bytes 2752516
  260.4 36.3 %copy-start.4 = (f32[128,1792]{1,0:T(8,128)}, f32[128,1792]{1,0:T(8,128)S(1)}, u32[]{:S(2)}) copy-start(f32[128,1792]{1,0:T(8,128)S(1)} %fusion.6) | copy-start | bytes 2752516
  296.6 10.3 %copy-start.7 = (bf16[128,1792]{1,0:T(8,128)(2,1)}, bf16[128,1792]{1,0:T(8,128)(2,1)S(1)}, u32[]{:S(2)}) copy-start(bf16[128,1792]{1,0:T(8,128)(2,1)S(1)} %get-tuple-element.14) | copy-start | bytes 1376260
  296.6 10.3 %copy-start.9 = (bf16[128,1792]{1,0:T(8,128)(2,1)}, bf16[128,1792]{1,0:T(8,128)(2,1)S(1)}, u32[]{:S(2)}) copy-start(bf16[128,1792]{1,0:T(8,128)(2,1)S(1)} %get-tuple-element.13) | copy-start | bytes 1376260
  306.9 11.7 %copy-start.1 = (bf16[256,4096]{1,0:T(8,128)(2,1)S(1)}, bf16[256,4096]{1,0:T(8,128)(2,1)}, u32[]{:S(2)}) copy-start(bf16[256,4096]{1,0:T(8,128)(2,1)} %all-gather.5.cloned.1.call-done) | copy-start | bytes 6291460
  306.9 11.7 %copy-start.12 = (bf16[8,4096]{1,0:T(8,128)(2,1)S(1)}, bf16[8,4096]{1,0:T(8,128)(2,1)}, u32[]{:S(2)}) copy-start(bf16[8,4096]{1,0:T(8,128)(2,1)} %param.10) | copy-start | bytes 196612
  318.6 10.1 %copy-start.8 = (bf16[128,1792]{1,0:T(8,128)(2,1)S(1)}, bf16[128,1792]{1,0:T(8,128)(2,1)}, u32[]{:S(2)}) copy-start(bf16[128,1792]{1,0:T(8,128)(2,1)} %copy-done.7) | copy-start | bytes 1376260
  319.9 16.4 %copy-start.3 = (f32[128,1792]{1,0:T(8,128)S(1)}, f32[128,1792]{1,0:T(8,128)}, u32[]{:S(2)}) copy-start(f32[128,1792]{1,0:T(8,128)} %copy-done.2) | copy-start | bytes 2752516
  319.9 16.4 %copy-start.5 = (f32[128,1792]{1,0:T(8,128)S(1)}, f32[128,1792]{1,0:T(8,128)}, u32[]{:S(2)}) copy-start(f32[128,1792]{1,0:T(8,128)} %copy-done.4) | copy-start | bytes 2752516
  319.9 16.4 %copy-start.11 = (bf16[128,4096]{1,0:T(8,128)(2,1)S(1)}, bf16[128,4096]{1,0:T(8,128)(2,1)}, u32[]{:S(2)}) copy-start(bf16[128,4096]{1,0:T(8,128)(2,1)} %all-gather.9.cloned.1.call-done) | copy-start | bytes 3145732
  328.7 56.6 %copy-start.6 = (bf16[1,16,4096]{2,1,0:T(8,128)(2,1)S(1)}, bf16[1,16,4096]{2,1,0:T(8,128)(2,1)}, u32[]{:S(2)}) copy-start(bf16[1,16,4096]{2,1,0:T(8,128)(2,1)} %param.14) | copy-start | bytes 393220
  328.7 56.6 %copy-start.13 = (f32[1,4096]{1,0:T(1,128)S(1)}, f32[1,4096]{1,0:T(1,128)}, u32[]{:S(2)}) copy-start(f32[1,4096]{1,0:T(1,128)} %param.16) | copy-start | bytes 49156
  328.7 93.4 %copy-start.10 = (bf16[16,4096]{1,0:T(8,128)(2,1)S(1)}, bf16[16,4096]{1,0:T(8,128)(2,1)}, u32[]{:S(2)}) copy-start(bf16[16,4096]{1,0:T(8,128)(2,1)} %fusion.16) | copy-start | bytes 393220
Sparse Core Ops, SparseCore 0:
  11.4 59.0 all-gather.4
  74.0 55.2 all-gather.6
  135.0 67.3 all-reduce.4
  204.9 40.0 all-gather.10
  247.0 38.9 all-gather.8
  318.7 66.5 reduce-scatter.1
where the time goes:
time: 431 us
  waiting for transfers between devices  245 us (57%)
  matrix products  80.5 us (19%)
  blocking collectives  74.1 us (17%)
  other arithmetic  16.1 us (4%)
  between operations  14.3 us (3%)
    psum x1, waiting for transfers between devices, from_root(): return lax.psum(block, axis)  64.1 us
    all_gather x1, waiting for transfers between devices, local(): lax.all_gather(passage_low, ('dp', 'segment'), axis=0, tiled=True)  55.6 us
    reduce_scatter x1, waiting for transfers between devices, local(): lax.psum_scatter(jnp.dot(gate_delta, gate_matrix.T, preferred_element_typ...  41.4 us
    all_gather x1, waiting for transfers between devices, local(): normed = lax.all_gather(normed_local, 'dp', axis=0, tiled=True)  40.5 us
    unnamed x1, blocking collectives  38.6 us
    psum x1, blocking collectives, local(): gain_total = lax.psum(jnp.sum(normed_delta * unit_local, axis=0), 'dp')  35.6 us
    all_gather x1, waiting for transfers between devices, local(): full_cotangent = lax.all_gather(cotangent, 'dp', axis=0, tiled=True)  25.6 us
    all_gather x1, waiting for transfers between devices, local(): lax.all_gather(query_low, ('dp', 'segment'), axis=0, tiled=True)  17.5 us
  transfers between devices with their start and end apart: 6, of which 6 were waited for; matrix products, arithmetic and copies ran while one was open for 12% of the time, Pallas kernels for 0%

commit v1 on v0

v1 whole, which is shorter than its diff:
```python
import jax
import jax.numpy as jnp
from jax import lax
from jax.experimental import pallas as pl
from jax.experimental.pallas import tpu as pltpu
from jax.sharding import PartitionSpec as P

HN_BLOCK = 128
TAU = 0.02
HN_WEIGHT = 64.0
EPS_NORM = 1e-06
EPS_RMS = 1e-05

F32 = jnp.float32
BF16 = jnp.bfloat16
MIB = 2**20
NT = (((1,), (1,)), ((), ()))
TN = (((0,), (0,)), ((), ()))


def vmem():
    return pl.BlockSpec(memory_space=pltpu.VMEM)


def smem():
    return pl.BlockSpec(memory_space=pltpu.SMEM)


def anywhere():
    return pl.BlockSpec(memory_space=pl.ANY)


def params(mib):
    return pltpu.CompilerParams(vmem_limit_bytes=mib * MIB)


def iota(shape, axis):
    return lax.broadcasted_iota(jnp.int32, shape, axis)


def split3(value):
    high = value.astype(BF16).astype(F32)
    rest = value - high
    middle = rest.astype(BF16).astype(F32)
    return high, middle, (rest - middle).astype(BF16).astype(F32)


def to_row(column, width):
    n = column.shape[0]
    pick = iota((n, width), 0) == iota((n, width), 1)
    return jnp.sum(jnp.where(pick, column, 0.0), axis=0, keepdims=True)


def to_columns(rows, n):
    shape = rows.shape[:-2] + (n, rows.shape[-1])
    pick = iota(shape, len(shape) - 2) == iota(shape, len(shape) - 1)
    return jnp.sum(jnp.where(pick, rows, 0.0), axis=-1, keepdims=True)


def row_inverse(ref, rows, mean, eps):
    total = jnp.zeros((rows, 1), F32)
    width = ref.shape[1]
    step = min(width, 1024)
    for at in range(0, width, step):
        part = ref[:, at : at + step].astype(F32)
        total += jnp.sum(part * part, axis=1, keepdims=True)
    if mean:
        total = total / width
    return lax.rsqrt(total + eps)


def pack_rows(query_ref, passage_ref, out_ref):
    count, block, cols = out_ref.shape
    rows = query_ref.shape[0]
    inverse = jnp.concatenate(
        [
            row_inverse(query_ref, rows, False, EPS_NORM),
            row_inverse(passage_ref, rows, False, EPS_NORM),
        ],
        axis=0,
    )
    terms = [to_row(term, cols) for term in split3(inverse)]
    extra = jnp.concatenate(
        terms + [jnp.zeros((block - 2 * rows - 3, cols), F32)], axis=0
    )
    for peer in range(count):
        cut = slice(peer * cols, (peer + 1) * cols)
        both = jnp.concatenate(
            [
                query_ref[:, cut].astype(F32),
                passage_ref[:, cut].astype(F32),
                extra,
            ],
            axis=0,
        )
        out_ref[peer] = both.astype(BF16)


def partial_scores(rows_ref, out_ref, unit_ref, inverse_ref):
    count, block, cols = rows_ref.shape
    rows = out_ref.shape[1]
    pairs = count * rows
    values = rows_ref[...].astype(F32)
    lines = values[:, 2 * rows : 2 * rows + 1]
    lines = lines + values[:, 2 * rows + 1 : 2 * rows + 2]
    lines = lines + values[:, 2 * rows + 2 : 2 * rows + 3]
    inverse = to_columns(lines, 2 * rows)
    unit = values[:, : 2 * rows] * inverse
    query_unit = unit[:, :rows].reshape(pairs, cols)
    passage_unit = unit[:, rows:].reshape(pairs, cols)
    unit_ref[0] = query_unit
    unit_ref[1] = passage_unit
    inverse_ref[0] = inverse[:, :rows].reshape(pairs, 1)
    inverse_ref[1] = inverse[:, rows:].reshape(pairs, 1)
    scores = lax.dot_general(
        query_unit.astype(BF16), passage_unit.astype(BF16), NT, preferred_element_type=F32
    )
    out_ref[...] = scores.reshape(out_ref.shape)


def softmax_rows(first_ref, parts_ref, offsets_ref, out_ref):
    count, block, pairs = out_ref.shape
    rows = parts_ref.shape[1]
    scores = jnp.sum(parts_ref[...], axis=0) / TAU
    row = first_ref[0] + iota((rows, pairs), 0)
    column = iota((rows, pairs), 1)
    base = row // HN_BLOCK * HN_BLOCK
    tallies = jnp.zeros((rows, pairs), F32)
    for k in range(offsets_ref.shape[1]):
        tallies += (base + offsets_ref[:, k : k + 1] == column).astype(F32)
    weighted = (1.0 + HN_WEIGHT * tallies) * jnp.exp(scores)
    totals = jnp.sum(weighted, axis=1, keepdims=True)
    dscore = weighted / totals - (row == column).astype(F32)
    dscore = dscore.astype(BF16).astype(F32)
    product = dscore * scores
    lines = list(split3(jnp.sum(product, axis=0, keepdims=True)))
    lines += [
        to_row(term, pairs) for term in split3(jnp.sum(product, axis=1, keepdims=True))
    ]
    lines.append(jnp.zeros((block - rows - 6, pairs), F32))
    message = jnp.concatenate([dscore] + lines, axis=0).astype(BF16)
    for peer in range(count):
        out_ref[peer] = message


def pair_grads(first, take, rows_ref, unit_ref, inverse_ref, out_ref):
    count, block, pairs = rows_ref.shape
    rows = pairs // count
    cols = unit_ref.shape[2]
    values = rows_ref[...].astype(F32)
    dscore = values[:, :rows].reshape(pairs, pairs).astype(BF16)
    column_line = jnp.sum(
        values[:, rows] + values[:, rows + 1] + values[:, rows + 2], axis=0, keepdims=True
    )
    column_dots = to_columns(column_line, pairs)
    row_lines = (
        values[:, rows + 3 : rows + 4]
        + values[:, rows + 4 : rows + 5]
        + values[:, rows + 5 : rows + 6]
    )
    row_dots = to_columns(row_lines, rows).reshape(pairs, 1)
    query_unit, passage_unit = unit_ref[0], unit_ref[1]
    query_dir = (
        jnp.dot(dscore, passage_unit.astype(BF16), preferred_element_type=F32) / TAU
    )
    passage_dir = (
        lax.dot_general(dscore, query_unit.astype(BF16), TN, preferred_element_type=F32) / TAU
    )
    query_grad = inverse_ref[0] * (query_dir - query_unit * row_dots)
    passage_grad = inverse_ref[1] * (passage_dir - passage_unit * column_dots)
    pieces = [
        query_grad.reshape(count, rows, cols),
        passage_grad.reshape(count, rows, cols),
    ]
    picked = passage_grad[first : first + take]
    spare = out_ref.shape[1] - 2 * rows - take
    if spare:
        picked = jnp.concatenate([picked, jnp.zeros((spare, cols), F32)], axis=0)
    pieces.append(jnp.broadcast_to(picked[None], (count,) + picked.shape))
    out_ref[...] = jnp.concatenate(pieces, axis=1).astype(BF16)


def layer(
    cuts,
    deep_cuts,
    place_ref,
    lengths_ref,
    back_ref,
    x_ref,
    given_ref,
    gain_ref,
    gate_hbm,
    up_hbm,
    down_hbm,
    query_out,
    passage_out,
    delta_out,
    hidden_out,
    d_up_out,
    d_gate_out,
    normed_out,
    cot_out,
    gate_w,
    up_w,
    down_w,
    gate_s,
    up_s,
    inverse_s,
    gain_s,
    gate_sem,
    up_sem,
    down_sem,
):
    tokens, width = x_ref.shape
    units = gate_s.shape[1]
    owners, own, _ = delta_out.shape
    step = width // cuts
    copies = []
    for c in range(cuts):
        part = pl.ds(c * step, step)
        a = pltpu.make_async_copy(gate_hbm.at[part], gate_w.at[part], gate_sem.at[c])
        b = pltpu.make_async_copy(up_hbm.at[part], up_w.at[part], up_sem.at[c])
        a.start()
        b.start()
        copies.append((a, b))
    deep = units // deep_cuts
    deep_copies = []
    for c in range(deep_cuts):
        part = pl.ds(c * deep, deep)
        a = pltpu.make_async_copy(down_hbm.at[part], down_w.at[part], down_sem.at[c])
        a.start()
        deep_copies.append(a)

    inverse = row_inverse(x_ref, tokens, True, EPS_RMS)
    inverse_s[...] = inverse
    for c in range(cuts):
        cut = slice(c * step, (c + 1) * step)
        normed_out[:, cut] = (
            x_ref[:, cut].astype(F32) * inverse * gain_ref[:, cut]
        ).astype(BF16)

    count, block, cols = back_ref.shape
    rows = query_out.shape[0]
    passages = block - 2 * rows
    token = iota((tokens, 1), 0)
    lane = iota((tokens, passages), 1)
    start = jnp.int32(0)
    member = jnp.zeros((tokens, passages), F32)
    scale = jnp.zeros((tokens, 1), F32)
    for m in range(lengths_ref.shape[0]):
        length = lengths_ref[m]
        inside = jnp.logical_and(token >= start, token < start + length)
        member = jnp.where(jnp.logical_and(inside, lane == m), 1.0, member)
        scale = jnp.where(inside, 1.0 / (jnp.zeros((tokens, 1), F32) + length.astype(F32)), scale)
        start = start + length
    member = member.astype(BF16)
    last = place_ref[0] == 1
    for peer in range(count):
        cut = slice(peer * cols, (peer + 1) * cols)
        piece = back_ref[peer].astype(F32)
        query_out[:, cut] = piece[:rows].astype(BF16)
        passage_out[:, cut] = piece[rows : 2 * rows].astype(BF16)
        spread = jnp.dot(member, piece[2 * rows :].astype(BF16), preferred_element_type=F32)
        pooled = (spread * scale).astype(BF16)
        cot_out[:, cut] = jnp.where(last, pooled, given_ref[:, cut])

    for c in range(cuts):
        cut = slice(c * step, (c + 1) * step)
        copies[c][0].wait()
        copies[c][1].wait()
        gate = jnp.dot(normed_out[:, cut], gate_w[cut, :], preferred_element_type=F32)
        up = jnp.dot(normed_out[:, cut], up_w[cut, :], preferred_element_type=F32)
        if c == 0:
            gate_s[...] = gate
            up_s[...] = up
        else:
            gate_s[...] += gate
            up_s[...] += up
    for c in range(deep_cuts):
        cut = slice(c * deep, (c + 1) * deep)
        deep_copies[c].wait()
        d_hidden = lax.dot_general(cot_out[...], down_w[cut, :], NT, preferred_element_type=F32)
        gate, up = gate_s[:, cut], up_s[:, cut]
        sigmoid = jax.nn.sigmoid(gate)
        active = gate * sigmoid
        hidden_out[:, cut] = (active * up).astype(BF16)
        d_up_out[:, cut] = (d_hidden * active).astype(BF16)
        d_gate_out[:, cut] = (
            d_hidden * up * sigmoid * (1.0 + gate * (1.0 - sigmoid))
        ).astype(BF16)
    inverse = inverse_s[...]
    for c in range(cuts):
        cut = slice(c * step, (c + 1) * step)
        delta = lax.dot_general(
            d_gate_out[...], gate_w[cut, :], NT, preferred_element_type=F32
        ) + lax.dot_general(d_up_out[...], up_w[cut, :], NT, preferred_element_type=F32)
        delta_out[:, :, cut] = delta.astype(BF16).reshape(owners, own, step)
        gain_s[:, cut] = jnp.sum(
            delta * (x_ref[:, cut].astype(F32) * inverse), axis=0, keepdims=True
        )
    fold = width // own
    gain = jnp.concatenate(
        [gain_s[:, r * fold : (r + 1) * fold] for r in range(own)], axis=0
    )
    high, low, _ = split3(gain)
    tail = jnp.concatenate([high, low], axis=1).astype(BF16)
    for owner in range(owners):
        delta_out[owner, :, width:] = tail


def weight_grads(
    normed_ref, d_gate_ref, d_up_ref, hidden_ref, cot_ref, gate_out, up_out, down_out, hidden_t
):
    @pl.when(pl.program_id(0) == 0)
    def _():
        hidden_t[...] = hidden_ref[...].T

    gate_out[...] = lax.dot_general(
        normed_ref[...], d_gate_ref[...], TN, preferred_element_type=F32
    ).astype(BF16)
    up_out[...] = lax.dot_general(
        normed_ref[...], d_up_ref[...], TN, preferred_element_type=F32
    ).astype(BF16)
    down_out[...] = jnp.dot(
        hidden_t[...], cot_ref[...], preferred_element_type=F32
    ).astype(BF16)


def finish(parts_ref, x_ref, cot_ref, gain_ref, input_out, gain_out):
    owners, own, total = parts_ref.shape
    width = x_ref.shape[1]
    fold = width // own
    gain = jnp.zeros((own, fold), F32)
    for p in range(owners):
        gain += parts_ref[p, :, width : width + fold].astype(F32)
        gain += parts_ref[p, :, width + fold : width + 2 * fold].astype(F32)
    for r in range(own):
        gain_out[:, r * fold : (r + 1) * fold] = gain[r : r + 1]
    delta = parts_ref[0, :, :width].astype(F32)
    for p in range(1, owners):
        delta += parts_ref[p, :, :width].astype(F32)
    inverse = row_inverse(x_ref, own, True, EPS_RMS)
    unit = x_ref[...].astype(F32) * inverse
    scaled = delta * gain_ref[...]
    mean = jnp.sum(scaled * unit, axis=1, keepdims=True) / width
    input_out[...] = (
        cot_ref[...].astype(F32) + inverse * (scaled - unit * mean)
    ).astype(BF16)


def shape(dims, dtype):
    return jax.ShapeDtypeStruct(dims, dtype)


def local(
    query_cache,
    passage_cache,
    hard_offsets,
    passage_lengths,
    segment_inputs,
    segment_cotangents,
    norm_gain,
    gate_weight,
    up_weight,
    down_weight,
):
    everyone = ("dp", "segment")
    count = lax.axis_size(everyone)
    owners = lax.axis_size("dp")
    sections = lax.axis_size("segment")
    rows, width = query_cache.shape
    pairs = rows * count
    cols = width // count
    passages = passage_lengths.shape[0]
    own = segment_inputs.shape[1]
    tokens = own * owners
    units = gate_weight.shape[2]
    section = lax.axis_index("segment")
    dp = lax.axis_index("dp")
    first_row = (lax.axis_index(everyone) * rows).astype(jnp.int32).reshape(1)
    is_last = (section == sections - 1).astype(jnp.int32).reshape(1)

    x_own, cot_own, gain = segment_inputs[0], segment_cotangents[0], norm_gain
    x_all = lax.all_gather(x_own, "dp", axis=0, tiled=True)
    cot_all = lax.all_gather(cot_own, "dp", axis=0, tiled=True)

    block1 = 4 * rows
    message = pl.pallas_call(
        pack_rows,
        out_shape=shape((count, block1, cols), BF16),
        in_specs=[vmem(), vmem()],
        out_specs=vmem(),
        compiler_params=params(16),
        name="pack_rows",
    )(query_cache, passage_cache)
    message = lax.all_to_all(message, everyone, 0, 0, tiled=True)
    parts, unit, inverse = pl.pallas_call(
        partial_scores,
        out_shape=(
            shape((count, rows, pairs), F32),
            shape((2, pairs, cols), F32),
            shape((2, pairs, 1), F32),
        ),
        in_specs=[vmem()],
        out_specs=(vmem(), vmem(), vmem()),
        compiler_params=params(32),
        name="partial_scores",
    )(message)
    parts = lax.all_to_all(parts, everyone, 0, 0, tiled=True)
    message = pl.pallas_call(
        softmax_rows,
        out_shape=shape((count, 2 * rows, pairs), BF16),
        in_specs=[smem(), vmem(), vmem()],
        out_specs=vmem(),
        compiler_params=params(32),
        name="softmax_rows",
    )(first_row, parts, hard_offsets)
    message = lax.all_to_all(message, everyone, 0, 0, tiled=True)
    back = -(-(2 * rows + passages) // 16) * 16
    message = pl.pallas_call(
        lambda *refs: pair_grads((sections - 1) * rows, passages, *refs),
        out_shape=shape((count, back, cols), BF16),
        in_specs=[vmem(), vmem(), vmem()],
        out_specs=vmem(),
        compiler_params=params(48),
        name="pair_grads",
    )(message, unit, inverse)
    message = lax.all_to_all(message, everyone, 0, 0, tiled=True)

    cuts = 8
    deep_cuts = units // 256 if units % 256 == 0 else 1
    fold = width // own
    outs = pl.pallas_call(
        lambda *refs: layer(cuts, deep_cuts, *refs),
        out_shape=(
            shape((rows, width), BF16),
            shape((rows, width), BF16),
            shape((owners, own, width + 2 * fold), BF16),
            shape((tokens, units), BF16),
            shape((tokens, units), BF16),
            shape((tokens, units), BF16),
            shape((tokens, width), BF16),
            shape((tokens, width), BF16),
        ),
        in_specs=[smem(), smem()] + [vmem()] * 4 + [anywhere()] * 3,
        out_specs=tuple(vmem() for _ in range(8)),
        scratch_shapes=[
            pltpu.VMEM((width, units), BF16),
            pltpu.VMEM((width, units), BF16),
            pltpu.VMEM((units, width), BF16),
            pltpu.VMEM((tokens, units), F32),
            pltpu.VMEM((tokens, units), F32),
            pltpu.VMEM((tokens, 1), F32),
            pltpu.VMEM((1, width), F32),
            pltpu.SemaphoreType.DMA((cuts,)),
            pltpu.SemaphoreType.DMA((cuts,)),
            pltpu.SemaphoreType.DMA((deep_cuts,)),
        ],
        compiler_params=params(60),
        cost_estimate=pl.CostEstimate(
            flops=10 * tokens * width * units,
            bytes_accessed=6 * width * units,
            transcendentals=tokens * units,
        ),
        name="layer",
    )(
        is_last,
        passage_lengths,
        message,
        x_all,
        cot_all,
        gain,
        gate_weight[0],
        up_weight[0],
        down_weight[0],
    )
    query_grads, passage_grads, delta, hidden, d_up, d_gate, normed, cot = outs
    delta = lax.all_to_all(delta, "dp", 0, 0, tiled=True)

    step = 256
    whole = lambda shape_: pl.BlockSpec(shape_, lambda i: (0, 0))
    gate_grads, up_grads, down_grads = pl.pallas_call(
        weight_grads,
        grid=(width // step,),
        out_shape=(
            shape((width, units), BF16),
            shape((width, units), BF16),
            shape((units, width), BF16),
        ),
        in_specs=[
            pl.BlockSpec((tokens, step), lambda i: (0, i)),
            whole((tokens, units)),
            whole((tokens, units)),
            whole((tokens, units)),
            pl.BlockSpec((tokens, step), lambda i: (0, i)),
        ],
        out_specs=(
            pl.BlockSpec((step, units), lambda i: (i, 0)),
            pl.BlockSpec((step, units), lambda i: (i, 0)),
            pl.BlockSpec((units, step), lambda i: (0, i)),
        ),
        scratch_shapes=[pltpu.VMEM((units, tokens), BF16)],
        compiler_params=params(40),
        cost_estimate=pl.CostEstimate(
            flops=6 * tokens * width * units,
            bytes_accessed=6 * width * units,
            transcendentals=0,
        ),
        name="weight_grads",
    )(normed, d_gate, d_up, hidden, cot)

    cot_rows = lax.dynamic_slice_in_dim(cot, dp * own, own, axis=0)
    input_grads, gain_grads = pl.pallas_call(
        finish,
        out_shape=(shape((own, width), BF16), shape((1, width), F32)),
        in_specs=[vmem()] * 4,
        out_specs=(vmem(), vmem()),
        compiler_params=params(32),
        name="finish",
    )(delta, x_own, cot_rows, gain)
    return (
        query_grads,
        passage_grads,
        input_grads[None],
        gate_grads[None],
        up_grads[None],
        down_grads[None],
        gain_grads,
    )


def solution(mesh):
    pair = P(("dp", "segment"), None)
    token = P("segment", "dp", None)
    wide = P("segment", None, "dp")
    return jax.shard_map(
        local,
        mesh=mesh,
        in_specs=(pair, pair, pair, P(), token, token, P("segment", None), wide, wide, token),
        out_specs=(pair, pair, token, wide, wide, token, P("segment", None)),
        check_vma=False,
    )
```

time: 431 us -> 176 us (0.41)
  waiting for transfers between devices: 245 us -> 64.4 us
  matrix products: 80.5 us -> 0 us
  blocking collectives: 74.1 us -> 15.3 us
  Pallas kernels: 0 us -> 55.1 us
  starting transfers between devices: 0.43 us -> 16.8 us
  other arithmetic: 16.1 us -> 0 us
  local copies, waits for them, and re-layouts: 0.31 us -> 9.54 us
    all_gather x4 -> x2, waiting for transfers between devices: 139 us -> 37.6 us  [the longest x1 37.5 us: local(): x_all = lax.all_gather(x_own, 'dp', axis=0, tiled=True)]
    dot_general x12 -> x0, matrix products: 80.5 us -> none  [the longest x1 11.6 us: local(): jnp.dot(up_delta, up_matrix.T, preferred_element_type=jnp.float32)]
    psum x1 -> x0, waiting for transfers between devices: 64.1 us -> none  [from_root(): return lax.psum(block, axis)]
    pallas_call x0 -> x7, Pallas kernels: none -> 55.1 us  [the longest x1 33.9 us: local(): pl.pallas_call(lambda *refs: layer(cuts, deep_cuts, *refs), out_shape=(sh...]
    reduce_scatter x1 -> x0, waiting for transfers between devices: 41.4 us -> none  [local(): lax.psum_scatter(jnp.dot(gate_delta, gate_matrix.T, preferred_element_typ...]
    unnamed x1 -> x0, blocking collectives: 38.6 us -> none
    psum x1 -> x0, blocking collectives: 35.6 us -> none  [local(): gain_total = lax.psum(jnp.sum(normed_delta * unit_local, axis=0), 'dp')]
    all_to_all x0 -> x4, waiting for transfers between devices: none -> 25.5 us  [the longest x2 11.2 us: local(): message = lax.all_to_all(message, everyone, 0, 0, tiled=True)]
  transfers between devices with their start and end apart: 6 -> 6, of which waited for: 6 -> 4; matrix products, arithmetic and copies ran while one was open for 12% -> 1% of each run, Pallas kernels for 0% -> 12%
where the time goes in v1:
time: 176 us; the launch traced here: 175 us
  waiting for transfers between devices  64.4 us (37%)
  Pallas kernels  55.1 us (31%)
  starting transfers between devices  16.8 us (10%)
  blocking collectives  15.3 us (9%)
  between operations  14.2 us (8%)
  local copies, waits for them, and re-layouts  9.54 us (5%)
    all_gather x1, waiting for transfers between devices, local(): x_all = lax.all_gather(x_own, 'dp', axis=0, tiled=True)  37.5 us
    pallas_call x1, Pallas kernels, local(): pl.pallas_call(lambda *refs: layer(cuts, deep_cuts, *refs), out_shape=(sh...  33.9 us
    pallas_call x1, Pallas kernels, local(): pl.pallas_call(weight_grads, grid=(width // step,), out_shape=(shape((wid...  17.1 us
    all_to_all x1, blocking collectives, local(): message = lax.all_to_all(message, everyone, 0, 0, tiled=True)  15.3 us
    all_to_all x2, waiting for transfers between devices, local(): message = lax.all_to_all(message, everyone, 0, 0, tiled=True)  11.2 us
    all_to_all x2, starting transfers between devices, local(): message = lax.all_to_all(message, everyone, 0, 0, tiled=True)  10.2 us
    all_to_all x1, waiting for transfers between devices, local(): parts = lax.all_to_all(parts, everyone, 0, 0, tiled=True)  9.88 us
    unnamed x21, local copies, waits for them, and re-layouts  8.62 us
  transfers between devices with their start and end apart: 6, of which 4 were waited for; matrix products, arithmetic and copies ran while one was open for 1% of the time, Pallas kernels for 12%

profile of v1, /device:TPU:0, one launch (start us, length us, event | category | flops | bytes accessed | tf_op | source)
XLA Modules:
  0.0 175.4 jit_solution(10262801596755381660)
XLA Ops:
  7.9 0.8 copy-done.2
  8.7 0.8 copy-done.3
  9.6 0.9 pack_rows.1
  10.5 7.3 %all-to-all-start = ((bf16[32,32,128]{2,1,0:T(8,128)(2,1)}), bf16[32,32,128]{2,1,0:T(8,128)(2,1)S(1)}, u32[]{:S(2)}, u32[]{:S(2)}) async-start(bf16[32,32,128]{2,1,0:T(8,128)(2,1)} %pack_rows.1), calls=%async_computation | async-start | bytes 524288 | tf_op jit(solution)/shard_map/all_to_all | solution.py:396
  18.6 11.2 %all-to-all-done.rows_ref = bf16[32,32,128]{2,1,0:T(8,128)(2,1)S(1)} async-done(((bf16[32,32,128]{2,1,0:T(8,128)(2,1)}), bf16[32,32,128]{2,1,0:T(8,128)(2,1)S(1)}, u32[]{:S(2)}, u32[]{:S(2)}) %all-to-all-start) | async-done | bytes 262176 | tf_op jit(solution)/shard_map/all_to_all | solution.py:396
  29.7 1.0 partial_scores.1
  30.7 2.8 %all-to-all-start.1 = ((f32[32,8,256]{2,1,0:T(8,128)}), f32[32,8,256]{2,1,0:T(8,128)S(1)}, u32[]{:S(2)}, u32[]{:S(2)}) async-start(f32[32,8,256]{2,1,0:T(8,128)} %get-tuple-element.23), calls=%async_computation.1 | async-start | bytes 524288 | tf_op jit(solution)/shard_map/all_to_all | solution.py:409
  33.5 0.7 copy.17.offsets_ref
  34.2 9.9 %all-to-all-done.1.parts_ref = f32[32,8,256]{2,1,0:T(8,128)S(1)} async-done(((f32[32,8,256]{2,1,0:T(8,128)}), f32[32,8,256]{2,1,0:T(8,128)S(1)}, u32[]{:S(2)}, u32[]{:S(2)}) %all-to-all-start.1) | async-done | bytes 262176 | tf_op jit(solution)/shard_map/all_to_all | solution.py:409
  44.4 15.3 %all_to_all.25.refs_0_ = bf16[32,16,256]{2,1,0:T(8,128)(2,1)S(1)} all-to-all(bf16[32,16,256]{2,1,0:T(8,128)(2,1)S(1)} %softmax_rows.1), channel_id=1, replica_groups=mesh['dp'=8,'segment'=4] {'dp','segment'}, dimensions={0} | all-to-all | bytes 524288 | tf_op jit(solution)/shard_map/all_to_all | solution.py:418
  59.7 1.0 pair_grads.1
  60.7 2.9 %all-to-all-start.3 = ((bf16[32,32,128]{2,1,0:T(8,128)(2,1)}), bf16[32,32,128]{2,1,0:T(8,128)(2,1)S(1)}, u32[]{:S(2)}, u32[]{:S(2)}) async-start(bf16[32,32,128]{2,1,0:T(8,128)(2,1)} %pair_grads.1), calls=%async_computation.3 | async-start | bytes 524288 | tf_op jit(solution)/shard_map/all_to_all | solution.py:428
  63.7 37.5 %all-gather.5.cloned.1.call-done = bf16[1,128,4096]{2,1,0:T(8,128)(2,1)} async-done(((bf16[1,16,4096]{2,1,0:T(8,128)(2,1)}), bf16[1,128,4096]{2,1,0:T(8,128)(2,1)}) %all-gather.5.cloned.1.call-update) | async-done | bytes 1048592 | tf_op jit(solution)/shard_map/all_gather | solution.py:384
  102.0 33.9 %layer.1 = (bf16[8,4096]{1,0:T(8,128)(2,1)}, bf16[8,4096]{1,0:T(8,128)(2,1)}, bf16[8,16,4608]{2,1,0:T(8,128)(2,1)}, bf16[128,1792]{1,0:T(8,128)(2,1)}, bf16[128,...) custom-call(s32[1]{0:T(128)} %bitcast.refs_0_, ...), custom_call_target="tpu_custom_call" | custom-call | flops 9395240960 | bytes 44040192 | tf_op jit(solution)/shard_map/layer/pallas_call | solution.py:433
  135.9 3.7 %all-to-all-start.4 = ((bf16[8,16,4608]{2,1,0:T(8,128)(2,1)}), bf16[8,16,4608]{2,1,0:T(8,128)(2,1)S(1)}, u32[]{:S(2)}, u32[]{:S(2)}) async-start(bf16[8,16,4608]{2,1,0:T(8,128)(2,1)} %get-tuple-element.28), calls=%async_computation.4 | async-start | bytes 2359296 | tf_op jit(solution)/shard_map/all_to_all | solution.py:478
  139.6 0.9 constant_dynamic-slice_fusion.cot_ref
  140.5 1.2 copy-done.4
  141.7 1.2 copy-done.5
  142.9 1.0 copy-done.6
  144.0 1.0 copy-done.7
  145.0 1.0 copy-done.8
  146.0 17.1 %weight_grads.1 = (bf16[4096,1792]{1,0:T(8,128)(2,1)}, bf16[4096,1792]{1,0:T(8,128)(2,1)}, bf16[1792,4096]{1,0:T(8,128)(2,1)}) custom-call(bf16[128,4096]{1,0:T(8,128)(2,1)S(1)} %copy-done.5, bf16[128,1792]{1,0:T(8,128)(2,1)S(1)} %copy-done.8, bf16[128,1792]{1,0:T(8,128)(2,1)S(1)} %copy-done.7, bf16[128,1792]{1,0:T(8,128)(2,1)S(1)} %copy-done.6, ...), custom_call_target="tpu_custom_call" | custom-call | flops 5637144576 | bytes 44040192 | tf_op jit(solution)/shard_map/weight_grads/pallas_call | solution.py:482
  163.1 4.4 %all-to-all-done.4.parts_ref = bf16[8,16,4608]{2,1,0:T(8,128)(2,1)S(1)} async-done(((bf16[8,16,4608]{2,1,0:T(8,128)(2,1)}), bf16[8,16,4608]{2,1,0:T(8,128)(2,1)S(1)}, u32[]{:S(2)}, u32[]{:S(2)}) %all-to-all-start.4) | async-done | bytes 1179680 | tf_op jit(solution)/shard_map/all_to_all | solution.py:478
  167.5 1.0 finish.1
  (20 shorter events, 2.5 us)
Async XLA Ops:
  7.2 56.6 %all-gather.7.cloned.1.call-start = ((), (), s32[]{:S(2)}) async-start(), calls=%async_computation.6 | async-start | bytes 1179648 | tf_op jit(solution)/shard_map/all_gather | solution.py:385
  7.9 0.8 copy-start.2
  8.7 0.8 copy-start.3
  10.5 19.2 %all-to-all-start = ((bf16[32,32,128]{2,1,0:T(8,128)(2,1)}), bf16[32,32,128]{2,1,0:T(8,128)(2,1)S(1)}, u32[]{:S(2)}, u32[]{:S(2)}) async-start(bf16[32,32,128]{2,1,0:T(8,128)(2,1)} %pack_rows.1), calls=%async_computation | async-start | bytes 524288 | tf_op jit(solution)/shard_map/all_to_all | solution.py:396
  17.8 83.4 %all-gather.5.cloned.1.call-start = ((), (), s32[]{:S(2)}) async-start(), calls=%async_computation.5 | async-start | bytes 1179648 | tf_op jit(solution)/shard_map/all_gather | solution.py:384
  30.7 13.4 %all-to-all-start.1 = ((f32[32,8,256]{2,1,0:T(8,128)}), f32[32,8,256]{2,1,0:T(8,128)S(1)}, u32[]{:S(2)}, u32[]{:S(2)}) async-start(f32[32,8,256]{2,1,0:T(8,128)} %get-tuple-element.23), calls=%async_computation.1 | async-start | bytes 524288 | tf_op jit(solution)/shard_map/all_to_all | solution.py:409
  60.7 40.5 %all-to-all-start.3 = ((bf16[32,32,128]{2,1,0:T(8,128)(2,1)}), bf16[32,32,128]{2,1,0:T(8,128)(2,1)S(1)}, u32[]{:S(2)}, u32[]{:S(2)}) async-start(bf16[32,32,128]{2,1,0:T(8,128)(2,1)} %pair_grads.1), calls=%async_computation.3 | async-start | bytes 524288 | tf_op jit(solution)/shard_map/all_to_all | solution.py:428
  101.3 0.7 copy-start.9
  135.8 31.7 %copy-start = (bf16[1,16,4096]{2,1,0:T(8,128)(2,1)S(1)}, bf16[1,16,4096]{2,1,0:T(8,128)(2,1)}, u32[]{:S(2)}) copy-start(bf16[1,16,4096]{2,1,0:T(8,128)(2,1)} %param.14) | copy-start | bytes 393220
  135.8 31.7 %copy-start.1 = (f32[1,4096]{1,0:T(1,128)S(1)}, f32[1,4096]{1,0:T(1,128)}, u32[]{:S(2)}) copy-start(f32[1,4096]{1,0:T(1,128)} %gain_ref.1) | copy-start | bytes 49156
  135.9 31.7 %all-to-all-start.4 = ((bf16[8,16,4608]{2,1,0:T(8,128)(2,1)}), bf16[8,16,4608]{2,1,0:T(8,128)(2,1)S(1)}, u32[]{:S(2)}, u32[]{:S(2)}) async-start(bf16[8,16,4608]{2,1,0:T(8,128)(2,1)} %get-tuple-element.28), calls=%async_computation.4 | async-start | bytes 2359296 | tf_op jit(solution)/shard_map/all_to_all | solution.py:478
  140.5 1.2 copy-start.4
  141.7 1.2 copy-start.5
  142.9 1.0 copy-start.6
  144.0 1.0 copy-start.7
  145.0 1.0 copy-start.8
Sparse Core Ops, SparseCore 0:
  10.1 48.6 all-gather.6
  60.9 40.2 all-gather.4

commit v2 on v1

--- a/solution.py
+++ b/solution.py
@@ -14,6 +14,8 @@
 F32 = jnp.float32
 BF16 = jnp.bfloat16
 MIB = 2**20
+WINDOW = 3
+BIG = 62
 NT = (((1,), (1,)), ((), ()))
 TN = (((0,), (0,)), ((), ()))
 
@@ -180,15 +182,27 @@
     out_ref[...] = jnp.concatenate(pieces, axis=1).astype(BF16)
 
 
-def layer(
+def forward(tokens_ref, gain_ref, gate_ref, up_ref, normed_out, gate_out, up_out):
+    @pl.when(pl.program_id(0) == 0)
+    def _():
+        tokens, width = normed_out.shape
+        x = tokens_ref[...].reshape(tokens, width).astype(F32)
+        inverse = lax.rsqrt(jnp.sum(x * x, axis=1, keepdims=True) / width + EPS_RMS)
+        normed_out[...] = (x * inverse * gain_ref[...]).astype(BF16)
+
+    gate_out[...] = jnp.dot(normed_out[...], gate_ref[...], preferred_element_type=F32)
+    up_out[...] = jnp.dot(normed_out[...], up_ref[...], preferred_element_type=F32)
+
+
+def backward(
     cuts,
     deep_cuts,
     place_ref,
     lengths_ref,
     back_ref,
-    x_ref,
-    given_ref,
-    gain_ref,
+    both_ref,
+    gate_ref,
+    up_ref,
     gate_hbm,
     up_hbm,
     down_hbm,
@@ -198,46 +212,47 @@
     hidden_out,
     d_up_out,
     d_gate_out,
-    normed_out,
     cot_out,
     gate_w,
     up_w,
     down_w,
-    gate_s,
-    up_s,
+    gain_s,
+    x_s,
     inverse_s,
-    gain_s,
+    d_gate_t,
+    d_up_t,
     gate_sem,
     up_sem,
     down_sem,
 ):
-    tokens, width = x_ref.shape
-    units = gate_s.shape[1]
+    tokens, width = cot_out.shape
+    units = gate_ref.shape[1]
     owners, own, _ = delta_out.shape
+    deep = units // deep_cuts
     step = width // cuts
-    copies = []
-    for c in range(cuts):
+
+    def down_copy(c):
+        slot = lax.rem(c, WINDOW)
+        return pltpu.make_async_copy(
+            down_hbm.at[pl.ds(c * deep, deep)], down_w.at[slot], down_sem.at[slot]
+        )
+
+    def wide_copies(c):
+        slot = lax.rem(c, WINDOW)
         part = pl.ds(c * step, step)
-        a = pltpu.make_async_copy(gate_hbm.at[part], gate_w.at[part], gate_sem.at[c])
-        b = pltpu.make_async_copy(up_hbm.at[part], up_w.at[part], up_sem.at[c])
-        a.start()
-        b.start()
-        copies.append((a, b))
-    deep = units // deep_cuts
-    deep_copies = []
-    for c in range(deep_cuts):
-        part = pl.ds(c * deep, deep)
-        a = pltpu.make_async_copy(down_hbm.at[part], down_w.at[part], down_sem.at[c])
-        a.start()
-        deep_copies.append(a)
-
-    inverse = row_inverse(x_ref, tokens, True, EPS_RMS)
-    inverse_s[...] = inverse
-    for c in range(cuts):
-        cut = slice(c * step, (c + 1) * step)
-        normed_out[:, cut] = (
-            x_ref[:, cut].astype(F32) * inverse * gain_ref[:, cut]
-        ).astype(BF16)
+        return (
+            pltpu.make_async_copy(gate_hbm.at[part], gate_w.at[slot], gate_sem.at[slot]),
+            pltpu.make_async_copy(up_hbm.at[part], up_w.at[slot], up_sem.at[slot]),
+        )
+
+    def start_wide(c):
+        for copy in wide_copies(c):
+            copy.start()
+
+    for c in range(min(WINDOW, deep_cuts)):
+        down_copy(c).start()
+    for c in range(WINDOW - deep_cuts):
+        start_wide(c)
 
     count, block, cols = back_ref.shape
     rows = query_out.shape[0]
@@ -262,25 +277,14 @@
         passage_out[:, cut] = piece[rows : 2 * rows].astype(BF16)
         spread = jnp.dot(member, piece[2 * rows :].astype(BF16), preferred_element_type=F32)
         pooled = (spread * scale).astype(BF16)
-        cot_out[:, cut] = jnp.where(last, pooled, given_ref[:, cut])
-
-    for c in range(cuts):
-        cut = slice(c * step, (c + 1) * step)
-        copies[c][0].wait()
-        copies[c][1].wait()
-        gate = jnp.dot(normed_out[:, cut], gate_w[cut, :], preferred_element_type=F32)
-        up = jnp.dot(normed_out[:, cut], up_w[cut, :], preferred_element_type=F32)
-        if c == 0:
-            gate_s[...] = gate
-            up_s[...] = up
-        else:
-            gate_s[...] += gate
-            up_s[...] += up
-    for c in range(deep_cuts):
-        cut = slice(c * deep, (c + 1) * deep)
-        deep_copies[c].wait()
-        d_hidden = lax.dot_general(cot_out[...], down_w[cut, :], NT, preferred_element_type=F32)
-        gate, up = gate_s[:, cut], up_s[:, cut]
+        given = both_ref[:, 1, :, cut].reshape(tokens, cols)
+        cot_out[:, cut] = jnp.where(last, pooled, given)
+
+    def down_step(c, carry):
+        down_copy(c).wait()
+        cut = pl.ds(pl.multiple_of(c * deep, deep), deep)
+        d_hidden = lax.dot_general(cot_out[...], down_w[lax.rem(c, WINDOW)], NT, preferred_element_type=F32)
+        gate, up = gate_ref[:, cut], up_ref[:, cut]
         sigmoid = jax.nn.sigmoid(gate)
         active = gate * sigmoid
         hidden_out[:, cut] = (active * up).astype(BF16)
@@ -288,16 +292,47 @@
         d_gate_out[:, cut] = (
             d_hidden * up * sigmoid * (1.0 + gate * (1.0 - sigmoid))
         ).astype(BF16)
-    inverse = inverse_s[...]
-    for c in range(cuts):
-        cut = slice(c * step, (c + 1) * step)
-        delta = lax.dot_general(
-            d_gate_out[...], gate_w[cut, :], NT, preferred_element_type=F32
-        ) + lax.dot_general(d_up_out[...], up_w[cut, :], NT, preferred_element_type=F32)
+        ahead = c + WINDOW
+
+        @pl.when(ahead < deep_cuts)
+        def _():
+            down_copy(ahead).start()
+
+        @pl.when(jnp.logical_and(ahead >= deep_cuts, ahead - deep_cuts < cuts))
+        def _():
+            start_wide(ahead - deep_cuts)
+
+        return carry
+
+    lax.fori_loop(0, deep_cuts, down_step, 0)
+
+    x = both_ref[:, 0].reshape(tokens, width).astype(F32)
+    x_s[...] = x
+    inverse_s[...] = lax.rsqrt(jnp.sum(x * x, axis=1, keepdims=True) / width + EPS_RMS)
+    d_gate_t[...] = d_gate_out[...].T
+    d_up_t[...] = d_up_out[...].T
+
+    def wide_step(c, carry):
+        for copy in wide_copies(c):
+            copy.wait()
+        cut = pl.ds(pl.multiple_of(c * step, step), step)
+        delta = (
+            jnp.dot(gate_w[lax.rem(c, WINDOW)], d_gate_t[...], preferred_element_type=F32)
+            + jnp.dot(up_w[lax.rem(c, WINDOW)], d_up_t[...], preferred_element_type=F32)
+        ).T
         delta_out[:, :, cut] = delta.astype(BF16).reshape(owners, own, step)
         gain_s[:, cut] = jnp.sum(
-            delta * (x_ref[:, cut].astype(F32) * inverse), axis=0, keepdims=True
+            delta * (x_s[:, cut] * inverse_s[...]), axis=0, keepdims=True
         )
+
+        @pl.when(c + WINDOW < cuts)
+        def _():
+            start_wide(c + WINDOW)
+
+        return carry
+
+    lax.fori_loop(0, cuts, wide_step, 0)
+
     fold = width // own
     gain = jnp.concatenate(
         [gain_s[:, r * fold : (r + 1) * fold] for r in range(own)], axis=0
@@ -381,8 +416,7 @@
     is_last = (section == sections - 1).astype(jnp.int32).reshape(1)
 
     x_own, cot_own, gain = segment_inputs[0], segment_cotangents[0], norm_gain
-    x_all = lax.all_gather(x_own, "dp", axis=0, tiled=True)
-    cot_all = lax.all_gather(cot_own, "dp", axis=0, tiled=True)
+    both = lax.all_gather(jnp.stack([x_own, cot_own]), "dp", axis=0, tiled=False)
 
     block1 = 4 * rows
     message = pl.pallas_call(
@@ -427,11 +461,39 @@
     )(message, unit, inverse)
     message = lax.all_to_all(message, everyone, 0, 0, tiled=True)
 
+    whole = lambda dims: pl.BlockSpec(dims, lambda i: (0,) * len(dims))
+    step = 256 if units % 256 == 0 else units
+    weight = pl.BlockSpec((width, step), lambda i: (0, i))
+    part = pl.BlockSpec((tokens, step), lambda i: (0, i))
+    normed, gate, up = pl.pallas_call(
+        forward,
+        grid=(units // step,),
+        out_shape=(
+            shape((tokens, width), BF16),
+            shape((tokens, units), F32),
+            shape((tokens, units), F32),
+        ),
+        in_specs=[
+            pl.BlockSpec((owners, None, own, width), lambda i: (0, 0, 0, 0)),
+            whole((1, width)),
+            weight,
+            weight,
+        ],
+        out_specs=(whole((tokens, width)), part, part),
+        compiler_params=params(BIG),
+        cost_estimate=pl.CostEstimate(
+            flops=4 * tokens * width * units,
+            bytes_accessed=4 * width * units,
+            transcendentals=0,
+        ),
+        name="forward",
+    )(both, gain, gate_weight[0], up_weight[0])
+
     cuts = 8
     deep_cuts = units // 256 if units % 256 == 0 else 1
     fold = width // own
     outs = pl.pallas_call(
-        lambda *refs: layer(cuts, deep_cuts, *refs),
+        lambda *refs: backward(cuts, deep_cuts, *refs),
         out_shape=(
             shape((rows, width), BF16),
             shape((rows, width), BF16),
@@ -440,45 +502,44 @@
             shape((tokens, units), BF16),
             shape((tokens, units), BF16),
             shape((tokens, width), BF16),
-            shape((tokens, width), BF16),
         ),
         in_specs=[smem(), smem()] + [vmem()] * 4 + [anywhere()] * 3,
-        out_specs=tuple(vmem() for _ in range(8)),
+        out_specs=tuple(vmem() for _ in range(7)),
         scratch_shapes=[
-            pltpu.VMEM((width, units), BF16),
-            pltpu.VMEM((width, units), BF16),
-            pltpu.VMEM((units, width), BF16),
-            pltpu.VMEM((tokens, units), F32),
-            pltpu.VMEM((tokens, units), F32),
+            pltpu.VMEM((WINDOW, width // cuts, units), BF16),
+            pltpu.VMEM((WINDOW, width // cuts, units), BF16),
+            pltpu.VMEM((WINDOW, units // deep_cuts, width), BF16),
+            pltpu.VMEM((1, width), F32),
+            pltpu.VMEM((tokens, width), F32),
             pltpu.VMEM((tokens, 1), F32),
-            pltpu.VMEM((1, width), F32),
-            pltpu.SemaphoreType.DMA((cuts,)),
-            pltpu.SemaphoreType.DMA((cuts,)),
-            pltpu.SemaphoreType.DMA((deep_cuts,)),
+            pltpu.VMEM((units, tokens), BF16),
+            pltpu.VMEM((units, tokens), BF16),
+            pltpu.SemaphoreType.DMA((WINDOW,)),
+            pltpu.SemaphoreType.DMA((WINDOW,)),
+            pltpu.SemaphoreType.DMA((WINDOW,)),
         ],
-        compiler_params=params(60),
+        compiler_params=params(BIG),
         cost_estimate=pl.CostEstimate(
-            flops=10 * tokens * width * units,
+            flops=6 * tokens * width * units,
             bytes_accessed=6 * width * units,
             transcendentals=tokens * units,
         ),
-        name="layer",
+        name="backward",
     )(
         is_last,
         passage_lengths,
         message,
-        x_all,
-        cot_all,
-        gain,
+        both,
+        gate,
+        up,
         gate_weight[0],
         up_weight[0],
         down_weight[0],
     )
-    query_grads, passage_grads, delta, hidden, d_up, d_gate, normed, cot = outs
+    query_grads, passage_grads, delta, hidden, d_up, d_gate, cot = outs
     delta = lax.all_to_all(delta, "dp", 0, 0, tiled=True)
 
-    step = 256
-    whole = lambda shape_: pl.BlockSpec(shape_, lambda i: (0, 0))
+    step = min(512, width)
     gate_grads, up_grads, down_grads = pl.pallas_call(
         weight_grads,
         grid=(width // step,),
@@ -500,7 +561,7 @@
             pl.BlockSpec((units, step), lambda i: (0, i)),
         ),
         scratch_shapes=[pltpu.VMEM((units, tokens), BF16)],
-        compiler_params=params(40),
+        compiler_params=params(BIG),
         cost_estimate=pl.CostEstimate(
             flops=6 * tokens * width * units,
             bytes_accessed=6 * width * units,

time: 176 us -> 150 us (0.85)
  waiting for transfers between devices: 64.4 us -> 21.2 us
  blocking collectives: 15.3 us -> 37.5 us
  local copies, waits for them, and re-layouts: 9.54 us -> 4.03 us
  starting transfers between devices: 16.8 us -> 14.6 us
    all_gather x2 -> x1, waiting for transfers between devices: 37.6 us -> 0.02 us  [local(): lax.all_gather(jnp.stack([x_own, cot_own]), 'dp', axis=0, tiled=False)]
    all_to_all x1 -> x2, blocking collectives: 15.3 us -> 37.5 us  [local(): message = lax.all_to_all(message, everyone, 0, 0, tiled=True)]
    all_to_all x2 -> x1, waiting for transfers between devices: 11.2 us -> 0.01 us  [local(): message = lax.all_to_all(message, everyone, 0, 0, tiled=True)]
    all_to_all x1, waiting for transfers between devices: 4.44 us -> 11.2 us  [local(): delta = lax.all_to_all(delta, 'dp', 0, 0, tiled=True)]
    all_to_all x2 -> x1, starting transfers between devices: 10.2 us -> 4.34 us  [local(): message = lax.all_to_all(message, everyone, 0, 0, tiled=True)]
    unnamed x21 -> x11, local copies, waits for them, and re-layouts: 8.62 us -> 3.12 us
    all_to_all x1, starting transfers between devices: 3.71 us -> 5.95 us  [local(): delta = lax.all_to_all(delta, 'dp', 0, 0, tiled=True)]
    pallas_call x1 -> x2, Pallas kernels: 33.9 us -> 35.7 us  [the longest x1 21.5 us: local(): pl.pallas_call(lambda *refs: backward(cuts, deep_cuts, *refs), out_shape=...]
  transfers between devices with their start and end apart: 6 -> 4, of which waited for: 4 -> 2; matrix products, arithmetic and copies ran while one was open for 1% -> 1% of each run, Pallas kernels for 12% -> 22%
where the time goes in v2:
time: 150 us; the launch traced here: 149 us
  Pallas kernels  55.9 us (37%)
  blocking collectives  37.5 us (25%)
  waiting for transfers between devices  21.2 us (14%)
  starting transfers between devices  14.6 us (10%)
  between operations  14.1 us (9%)
  local copies, waits for them, and re-layouts  4.03 us (3%)
  other arithmetic  1.7 us (1%)
    all_to_all x2, blocking collectives, local(): message = lax.all_to_all(message, everyone, 0, 0, tiled=True)  37.5 us
    pallas_call x1, Pallas kernels, local(): pl.pallas_call(lambda *refs: backward(cuts, deep_cuts, *refs), out_shape=...  21.5 us
    pallas_call x1, Pallas kernels, local(): pl.pallas_call(weight_grads, grid=(width // step,), out_shape=(shape((wid...  16.7 us
    pallas_call x1, Pallas kernels, local(): pl.pallas_call(forward, grid=(units // step,), out_shape=(shape((tokens,...  14.1 us
    all_to_all x1, waiting for transfers between devices, local(): delta = lax.all_to_all(delta, 'dp', 0, 0, tiled=True)  11.2 us
    all_to_all x1, waiting for transfers between devices, local(): parts = lax.all_to_all(parts, everyone, 0, 0, tiled=True)  9.96 us
    all_to_all x1, starting transfers between devices, local(): delta = lax.all_to_all(delta, 'dp', 0, 0, tiled=True)  5.95 us
    all_to_all x1, starting transfers between devices, local(): message = lax.all_to_all(message, everyone, 0, 0, tiled=True)  4.34 us
  transfers between devices with their start and end apart: 4, of which 2 were waited for; matrix products, arithmetic and copies ran while one was open for 1% of the time, Pallas kernels for 22%

profile of v2, /device:TPU:0, one launch (start us, length us, event | category | flops | bytes accessed | tf_op | source)
XLA Modules:
  0.0 149.1 jit_solution(10653481946869476335)
XLA Ops:
  7.2 0.0 all-gather.3.cloned.1.call-start
  7.2 1.7 %pad_maximum_fusion = bf16[2,16,4096]{2,1,0:T(8,128)(2,1)} fusion(bf16[1,16,4096]{2,1,0:T(8,128)(2,1)} %param.15, bf16[1,16,4096]{2,1,0:T(8,128)(2,1)} %param.14), kind=kLoop, calls=%fused_computation | loop fusion | flops 131072 | bytes 524288 | tf_op jit(solution)/shard_map/stack | solution.py:419
  8.9 0.0 all-gather.3.cloned.1.call-update
  8.9 0.8 copy-done.2
  9.8 0.8 copy-done.3
  10.6 0.2 pack_rows.1
  10.9 19.3 %all_to_all.25.rows_ref = bf16[32,32,128]{2,1,0:T(8,128)(2,1)S(1)} all-to-all(bf16[32,32,128]{2,1,0:T(8,128)(2,1)S(1)} %pack_rows.1), channel_id=1, replica_groups=mesh['dp'=8,'segment'=4] {'dp','segment'}, dimensions={0} | all-to-all | bytes 524288 | tf_op jit(solution)/shard_map/all_to_all | solution.py:430
  30.2 1.0 partial_scores.1
  31.2 4.3 %all-to-all-start.1 = ((f32[32,8,256]{2,1,0:T(8,128)}), f32[32,8,256]{2,1,0:T(8,128)S(1)}, u32[]{:S(2)}, u32[]{:S(2)}) async-start(f32[32,8,256]{2,1,0:T(8,128)} %get-tuple-element.25), calls=%async_computation.1 | async-start | bytes 524288 | tf_op jit(solution)/shard_map/all_to_all | solution.py:443
  35.5 0.7 copy.18.offsets_ref
  36.2 10.0 %all-to-all-done.1.parts_ref = f32[32,8,256]{2,1,0:T(8,128)S(1)} async-done(((f32[32,8,256]{2,1,0:T(8,128)}), f32[32,8,256]{2,1,0:T(8,128)S(1)}, u32[]{:S(2)}, u32[]{:S(2)}) %all-to-all-start.1) | async-done | bytes 262176 | tf_op jit(solution)/shard_map/all_to_all | solution.py:443
  46.2 0.3 softmax_rows.1
  46.4 18.1 %all_to_all.26.refs_0_ = bf16[32,16,256]{2,1,0:T(8,128)(2,1)S(1)} all-to-all(bf16[32,16,256]{2,1,0:T(8,128)(2,1)S(1)} %softmax_rows.1), channel_id=1, replica_groups=mesh['dp'=8,'segment'=4] {'dp','segment'}, dimensions={0} | all-to-all | bytes 524288 | tf_op jit(solution)/shard_map/all_to_all | solution.py:452
  64.6 1.0 pair_grads.1
  65.6 4.3 %all-to-all-start.3 = ((bf16[32,32,128]{2,1,0:T(8,128)(2,1)}), bf16[32,32,128]{2,1,0:T(8,128)(2,1)S(1)}, u32[]{:S(2)}, u32[]{:S(2)}) async-start(bf16[32,32,128]{2,1,0:T(8,128)(2,1)} %pair_grads.1), calls=%async_computation.3 | async-start | bytes 524288 | tf_op jit(solution)/shard_map/all_to_all | solution.py:462
  69.9 0.0 all-gather.3.cloned.1.call-done
  70.0 14.1 %forward.1 = (bf16[128,4096]{1,0:T(8,128)(2,1)}, f32[128,1792]{1,0:T(8,128)}, f32[128,1792]{1,0:T(8,128)}) custom-call(bf16[8,2,16,4096]{3,2,1,0:T(8,128)(2,1)} %bitcast.17, f32[1,4096]{1,0:T(1,128)} %gain_ref.3, bf16[4096,1792]{1,0:T(8,128)(2,1)} %bitcast.12, bf16[4096,1792]{1,0:T(8,128)(2,1)} %bitcast.14), custom_call_target="tpu_custom_call" | custom-call | flops 3758096384 | bytes 29360128 | tf_op jit(solution)/shard_map/forward/pallas_call | solution.py:468
  84.1 0.7 copy-done.4
  84.8 21.5 %backward.1 = (bf16[8,4096]{1,0:T(8,128)(2,1)}, bf16[8,4096]{1,0:T(8,128)(2,1)}, bf16[8,16,4608]{2,1,0:T(8,128)(2,1)}, bf16[128,1792]{1,0:T(8,128)(2,1)}, bf16[1...) custom-call(s32[1]{0:T(128)} %bitcast.refs_0_, s32[8]{0:T(128)} %refs_1_.1, ...), custom_call_target="tpu_custom_call" | custom-call | flops 5637144576 | bytes 44040192 | tf_op jit(solution)/shard_map/backward/pallas_call | solution.py:495
  106.4 6.0 %all-to-all-start.4 = ((bf16[8,16,4608]{2,1,0:T(8,128)(2,1)}), bf16[8,16,4608]{2,1,0:T(8,128)(2,1)S(1)}, u32[]{:S(2)}, u32[]{:S(2)}) async-start(bf16[8,16,4608]{2,1,0:T(8,128)(2,1)} %get-tuple-element.32), calls=%async_computation.4 | async-start | bytes 2359296 | tf_op jit(solution)/shard_map/all_to_all | solution.py:540
  112.3 0.9 constant_dynamic-slice_fusion.cot_ref
  113.3 16.7 %weight_grads.1 = (bf16[4096,1792]{1,0:T(8,128)(2,1)}, bf16[4096,1792]{1,0:T(8,128)(2,1)}, bf16[1792,4096]{1,0:T(8,128)(2,1)}) custom-call(bf16[128,4096]{1,0:T(8,128)(2,1)} %get-tuple-element.35.normed_ref, bf16[128,1792]{1,0:T(8,128)(2,1)} %get-tuple-element.36.d_gate_ref, bf16[128,1792]{1,0:T(8,128)(2,1)} %get-tuple-element.37.d_up_ref, ...), custom_call_target="tpu_custom_call" | custom-call | flops 5637144576 | bytes 44040192 | tf_op jit(solution)/shard_map/weight_grads/pallas_call | solution.py:543
  130.0 11.2 %all-to-all-done.4.parts_ref = bf16[8,16,4608]{2,1,0:T(8,128)(2,1)S(1)} async-done(((bf16[8,16,4608]{2,1,0:T(8,128)(2,1)}), bf16[8,16,4608]{2,1,0:T(8,128)(2,1)S(1)}, u32[]{:S(2)}, u32[]{:S(2)}) %all-to-all-start.4) | async-done | bytes 1179680 | tf_op jit(solution)/shard_map/all_to_all | solution.py:540
  141.2 1.0 finish.1
  (8 shorter events, 0.0 us)
Async XLA Ops:
  7.2 62.8 %all-gather.3.cloned.1.call-start = ((), (), s32[]{:S(2)}) async-start(), calls=%async_computation.5 | async-start | bytes 2359296 | tf_op jit(solution)/shard_map/all_gather | solution.py:419
  8.9 0.8 copy-start.2
  9.8 0.8 copy-start.3
  31.2 15.0 %all-to-all-start.1 = ((f32[32,8,256]{2,1,0:T(8,128)}), f32[32,8,256]{2,1,0:T(8,128)S(1)}, u32[]{:S(2)}, u32[]{:S(2)}) async-start(f32[32,8,256]{2,1,0:T(8,128)} %get-tuple-element.25), calls=%async_computation.1 | async-start | bytes 524288 | tf_op jit(solution)/shard_map/all_to_all | solution.py:443
  65.6 18.5 %all-to-all-start.3 = ((bf16[32,32,128]{2,1,0:T(8,128)(2,1)}), bf16[32,32,128]{2,1,0:T(8,128)(2,1)S(1)}, u32[]{:S(2)}, u32[]{:S(2)}) async-start(bf16[32,32,128]{2,1,0:T(8,128)(2,1)} %pair_grads.1), calls=%async_computation.3 | async-start | bytes 524288 | tf_op jit(solution)/shard_map/all_to_all | solution.py:462
  84.1 0.7 copy-start.4
  106.4 34.9 %copy-start = (bf16[1,16,4096]{2,1,0:T(8,128)(2,1)S(1)}, bf16[1,16,4096]{2,1,0:T(8,128)(2,1)}, u32[]{:S(2)}) copy-start(bf16[1,16,4096]{2,1,0:T(8,128)(2,1)} %param.14) | copy-start | bytes 393220
  106.4 34.9 %copy-start.1 = (f32[1,4096]{1,0:T(1,128)S(1)}, f32[1,4096]{1,0:T(1,128)}, u32[]{:S(2)}) copy-start(f32[1,4096]{1,0:T(1,128)} %gain_ref.3) | copy-start | bytes 49156
  106.4 34.8 %all-to-all-start.4 = ((bf16[8,16,4608]{2,1,0:T(8,128)(2,1)}), bf16[8,16,4608]{2,1,0:T(8,128)(2,1)S(1)}, u32[]{:S(2)}, u32[]{:S(2)}) async-start(bf16[8,16,4608]{2,1,0:T(8,128)(2,1)} %get-tuple-element.32), calls=%async_computation.4 | async-start | bytes 2359296 | tf_op jit(solution)/shard_map/all_to_all | solution.py:540
Sparse Core Ops, SparseCore 0:
  10.7 57.8 all-gather.2

commit v3 on v2

--- a/solution.py
+++ b/solution.py
@@ -71,9 +71,21 @@
     return lax.rsqrt(total + eps)
 
 
-def pack_rows(query_ref, passage_ref, out_ref):
+def pack_rows(
+    query_hbm, passage_hbm, x_hbm, cot_hbm, out_ref, both_ref, query_ref, passage_ref, sems
+):
     count, block, cols = out_ref.shape
     rows = query_ref.shape[0]
+    copies = [
+        pltpu.make_async_copy(query_hbm, query_ref, sems.at[0]),
+        pltpu.make_async_copy(passage_hbm, passage_ref, sems.at[1]),
+        pltpu.make_async_copy(x_hbm, both_ref.at[0], sems.at[2]),
+        pltpu.make_async_copy(cot_hbm, both_ref.at[1], sems.at[3]),
+    ]
+    for copy in copies:
+        copy.start()
+    copies[0].wait()
+    copies[1].wait()
     inverse = jnp.concatenate(
         [
             row_inverse(query_ref, rows, False, EPS_NORM),
@@ -96,6 +108,8 @@
             axis=0,
         )
         out_ref[peer] = both.astype(BF16)
+    copies[2].wait()
+    copies[3].wait()
 
 
 def partial_scores(rows_ref, out_ref, unit_ref, inverse_ref):
@@ -127,9 +141,10 @@
     row = first_ref[0] + iota((rows, pairs), 0)
     column = iota((rows, pairs), 1)
     base = row // HN_BLOCK * HN_BLOCK
+    offsets = to_columns(offsets_ref[...].astype(F32)[:, None, :], rows).astype(jnp.int32)
     tallies = jnp.zeros((rows, pairs), F32)
-    for k in range(offsets_ref.shape[1]):
-        tallies += (base + offsets_ref[:, k : k + 1] == column).astype(F32)
+    for k in range(offsets_ref.shape[0]):
+        tallies += (base + offsets[k] == column).astype(F32)
     weighted = (1.0 + HN_WEIGHT * tallies) * jnp.exp(scores)
     totals = jnp.sum(weighted, axis=1, keepdims=True)
     dscore = weighted / totals - (row == column).astype(F32)
@@ -182,22 +197,128 @@
     out_ref[...] = jnp.concatenate(pieces, axis=1).astype(BF16)
 
 
-def forward(tokens_ref, gain_ref, gate_ref, up_ref, normed_out, gate_out, up_out):
-    @pl.when(pl.program_id(0) == 0)
-    def _():
-        tokens, width = normed_out.shape
-        x = tokens_ref[...].reshape(tokens, width).astype(F32)
-        inverse = lax.rsqrt(jnp.sum(x * x, axis=1, keepdims=True) / width + EPS_RMS)
-        normed_out[...] = (x * inverse * gain_ref[...]).astype(BF16)
-
-    gate_out[...] = jnp.dot(normed_out[...], gate_ref[...], preferred_element_type=F32)
-    up_out[...] = jnp.dot(normed_out[...], up_ref[...], preferred_element_type=F32)
+class Ring:
+    def __init__(self, hbm, slots, sems, step):
+        self.hbm, self.slots, self.sems, self.step = hbm, slots, sems, step
+
+    def copy(self, c):
+        slot = lax.rem(c, WINDOW)
+        part = pl.ds(c * self.step, self.step)
+        return pltpu.make_async_copy(self.hbm.at[part], self.slots.at[slot], self.sems.at[slot])
+
+
+def forward(
+    both_hbm,
+    gain_ref,
+    gate_hbm,
+    up_hbm,
+    normed_out,
+    gate_out,
+    up_out,
+    x_s,
+    gate_w,
+    up_w,
+    x_sem,
+    gate_sem,
+    up_sem,
+):
+    tokens, width = normed_out.shape
+    step = gate_w.shape[1]
+    blocks = width // step
+    gate_ring = Ring(gate_hbm, gate_w, gate_sem, step)
+    up_ring = Ring(up_hbm, up_w, up_sem, step)
+    fetch = pltpu.make_async_copy(both_hbm.at[:, 0], x_s, x_sem.at[0])
+    fetch.start()
+    for c in range(min(WINDOW, blocks)):
+        gate_ring.copy(c).start()
+        up_ring.copy(c).start()
+    fetch.wait()
+    x = x_s[...].reshape(tokens, width).astype(F32)
+    inverse = lax.rsqrt(jnp.sum(x * x, axis=1, keepdims=True) / width + EPS_RMS)
+    normed_out[...] = (x * inverse * gain_ref[...]).astype(BF16)
+
+    def block(c, first):
+        slot = lax.rem(c, WINDOW)
+        cut = pl.ds(pl.multiple_of(c * step, step), step)
+        normed = normed_out[:, cut]
+        gate_ring.copy(c).wait()
+        gate = jnp.dot(normed, gate_w[slot], preferred_element_type=F32)
+        gate_out[...] = gate if first else gate_out[...] + gate
+        up_ring.copy(c).wait()
+        up = jnp.dot(normed, up_w[slot], preferred_element_type=F32)
+        up_out[...] = up if first else up_out[...] + up
+
+        @pl.when(c + WINDOW < blocks)
+        def _():
+            gate_ring.copy(c + WINDOW).start()
+            up_ring.copy(c + WINDOW).start()
+
+    def more(c, carry):
+        block(c, False)
+        return carry
+
+    block(jnp.int32(0), True)
+    lax.fori_loop(1, blocks, more, 0)
+
+
+def partner(mine, k, n):
+    if n & (n - 1) == 0:
+        return mine ^ k
+    return (k + n - mine) % n
+
+
+def delta_columns(mine, cuts, rings, started, both_ref, d_gate_t, d_up_t, outs, delta_s, gain_s, inverse_s):
+    owners = len(outs)
+    own, total = outs[0].shape
+    width = gain_s.shape[1]
+    tokens = owners * own
+    gate_ring, up_ring = rings
+    step = gate_ring.step
+    for c in range(started, min(WINDOW, cuts)):
+        gate_ring.copy(c).start()
+        up_ring.copy(c).start()
+    x = both_ref[:, 0].reshape(tokens, width).astype(F32)
+    inverse_s[...] = lax.rsqrt(jnp.sum(x * x, axis=1, keepdims=True) / width + EPS_RMS)
+
+    def one(c, carry):
+        slot = lax.rem(c, WINDOW)
+        gate_ring.copy(c).wait()
+        up_ring.copy(c).wait()
+        cut = pl.ds(pl.multiple_of(c * step, step), step)
+        delta = (
+            jnp.dot(gate_ring.slots[slot], d_gate_t[...], preferred_element_type=F32)
+            + jnp.dot(up_ring.slots[slot], d_up_t[...], preferred_element_type=F32)
+        ).T
+        low = delta.astype(BF16)
+        for owner in range(owners):
+            delta_s[partner(mine, owner, owners), :, cut] = low[owner * own : (owner + 1) * own]
+        unit = both_ref[:, 0, :, cut].reshape(tokens, step).astype(F32) * inverse_s[...]
+        gain_s[:, cut] = jnp.sum(delta * unit, axis=0, keepdims=True)
+
+        @pl.when(c + WINDOW < cuts)
+        def _():
+            gate_ring.copy(c + WINDOW).start()
+            up_ring.copy(c + WINDOW).start()
+
+        return carry
+
+    lax.fori_loop(0, cuts, one, 0)
+    fold = width // own
+    gain = jnp.concatenate(
+        [gain_s[:, r * fold : (r + 1) * fold] for r in range(own)], axis=0
+    )
+    high, low, _ = split3(gain)
+    tail = jnp.concatenate([high, low], axis=1).astype(BF16)
+    for k in range(owners):
+        outs[k][:, :width] = delta_s[k]
+        outs[k][:, width:] = tail
 
 
 def backward(
     cuts,
     deep_cuts,
-    place_ref,
+    last_ref,
+    mine_ref,
     lengths_ref,
     back_ref,
     both_ref,
@@ -208,51 +329,26 @@
     down_hbm,
     query_out,
     passage_out,
-    delta_out,
     hidden_out,
     d_up_out,
     d_gate_out,
     cot_out,
-    gate_w,
-    up_w,
-    down_w,
-    gain_s,
-    x_s,
-    inverse_s,
-    d_gate_t,
-    d_up_t,
-    gate_sem,
-    up_sem,
-    down_sem,
+    cot_own_out,
+    *more,
 ):
+    *delta_outs, gate_w, up_w, down_w, d_up_t, d_gate_t, delta_s, gain_s, inverse_s = more[:-3]
+    gate_sem, up_sem, down_sem = more[-3:]
     tokens, width = cot_out.shape
     units = gate_ref.shape[1]
-    owners, own, _ = delta_out.shape
+    own = delta_outs[0].shape[0]
     deep = units // deep_cuts
-    step = width // cuts
-
-    def down_copy(c):
-        slot = lax.rem(c, WINDOW)
-        return pltpu.make_async_copy(
-            down_hbm.at[pl.ds(c * deep, deep)], down_w.at[slot], down_sem.at[slot]
-        )
-
-    def wide_copies(c):
-        slot = lax.rem(c, WINDOW)
-        part = pl.ds(c * step, step)
-        return (
-            pltpu.make_async_copy(gate_hbm.at[part], gate_w.at[slot], gate_sem.at[slot]),
-            pltpu.make_async_copy(up_hbm.at[part], up_w.at[slot], up_sem.at[slot]),
-        )
-
-    def start_wide(c):
-        for copy in wide_copies(c):
-            copy.start()
-
+    step = gain_s.shape[1] // cuts
+    down_ring = Ring(down_hbm, down_w, down_sem, deep)
+    gate_ring = Ring(gate_hbm, gate_w, gate_sem, step)
+    up_ring = Ring(up_hbm, up_w, up_sem, step)
+    early = min(WINDOW, deep_cuts, cuts)
     for c in range(min(WINDOW, deep_cuts)):
-        down_copy(c).start()
-    for c in range(WINDOW - deep_cuts):
-        start_wide(c)
+        down_ring.copy(c).start()
 
     count, block, cols = back_ref.shape
     rows = query_out.shape[0]
@@ -269,7 +365,7 @@
         scale = jnp.where(inside, 1.0 / (jnp.zeros((tokens, 1), F32) + length.astype(F32)), scale)
         start = start + length
     member = member.astype(BF16)
-    last = place_ref[0] == 1
+    last = last_ref[0] == 1
     for peer in range(count):
         cut = slice(peer * cols, (peer + 1) * cols)
         piece = back_ref[peer].astype(F32)
@@ -280,67 +376,50 @@
         given = both_ref[:, 1, :, cut].reshape(tokens, cols)
         cot_out[:, cut] = jnp.where(last, pooled, given)
 
+    cot_own_out[...] = cot_out[pl.ds(pl.multiple_of(mine_ref[0] * own, own), own), :]
+
     def down_step(c, carry):
-        down_copy(c).wait()
+        slot = lax.rem(c, WINDOW)
+        down_ring.copy(c).wait()
         cut = pl.ds(pl.multiple_of(c * deep, deep), deep)
-        d_hidden = lax.dot_general(cot_out[...], down_w[lax.rem(c, WINDOW)], NT, preferred_element_type=F32)
+        d_hidden = lax.dot_general(cot_out[...], down_w[slot], NT, preferred_element_type=F32)
         gate, up = gate_ref[:, cut], up_ref[:, cut]
         sigmoid = jax.nn.sigmoid(gate)
         active = gate * sigmoid
         hidden_out[:, cut] = (active * up).astype(BF16)
-        d_up_out[:, cut] = (d_hidden * active).astype(BF16)
-        d_gate_out[:, cut] = (
-            d_hidden * up * sigmoid * (1.0 + gate * (1.0 - sigmoid))
-        ).astype(BF16)
+        d_up = (d_hidden * active).astype(BF16)
+        d_gate = (d_hidden * up * sigmoid * (1.0 + gate * (1.0 - sigmoid))).astype(BF16)
+        d_up_out[:, cut] = d_up
+        d_gate_out[:, cut] = d_gate
+        d_up_t[cut, :] = d_up.T
+        d_gate_t[cut, :] = d_gate.T
         ahead = c + WINDOW
 
         @pl.when(ahead < deep_cuts)
         def _():
-            down_copy(ahead).start()
-
-        @pl.when(jnp.logical_and(ahead >= deep_cuts, ahead - deep_cuts < cuts))
+            down_ring.copy(ahead).start()
+
+        @pl.when(jnp.logical_and(ahead >= deep_cuts, ahead - deep_cuts < early))
         def _():
-            start_wide(ahead - deep_cuts)
+            gate_ring.copy(ahead - deep_cuts).start()
+            up_ring.copy(ahead - deep_cuts).start()
 
         return carry
 
     lax.fori_loop(0, deep_cuts, down_step, 0)
-
-    x = both_ref[:, 0].reshape(tokens, width).astype(F32)
-    x_s[...] = x
-    inverse_s[...] = lax.rsqrt(jnp.sum(x * x, axis=1, keepdims=True) / width + EPS_RMS)
-    d_gate_t[...] = d_gate_out[...].T
-    d_up_t[...] = d_up_out[...].T
-
-    def wide_step(c, carry):
-        for copy in wide_copies(c):
-            copy.wait()
-        cut = pl.ds(pl.multiple_of(c * step, step), step)
-        delta = (
-            jnp.dot(gate_w[lax.rem(c, WINDOW)], d_gate_t[...], preferred_element_type=F32)
-            + jnp.dot(up_w[lax.rem(c, WINDOW)], d_up_t[...], preferred_element_type=F32)
-        ).T
-        delta_out[:, :, cut] = delta.astype(BF16).reshape(owners, own, step)
-        gain_s[:, cut] = jnp.sum(
-            delta * (x_s[:, cut] * inverse_s[...]), axis=0, keepdims=True
-        )
-
-        @pl.when(c + WINDOW < cuts)
-        def _():
-            start_wide(c + WINDOW)
-
-        return carry
-
-    lax.fori_loop(0, cuts, wide_step, 0)
-
-    fold = width // own
-    gain = jnp.concatenate(
-        [gain_s[:, r * fold : (r + 1) * fold] for r in range(own)], axis=0
-    )
-    high, low, _ = split3(gain)
-    tail = jnp.concatenate([high, low], axis=1).astype(BF16)
-    for owner in range(owners):
-        delta_out[owner, :, width:] = tail
+    delta_columns(
+        mine_ref[0],
+        cuts,
+        (gate_ring, up_ring),
+        early,
+        both_ref,
+        d_gate_t,
+        d_up_t,
+        delta_outs,
+        delta_s,
+        gain_s,
+        inverse_s,
+    )
 
 
 def weight_grads(
@@ -361,19 +440,22 @@
     ).astype(BF16)
 
 
-def finish(parts_ref, x_ref, cot_ref, gain_ref, input_out, gain_out):
-    owners, own, total = parts_ref.shape
-    width = x_ref.shape[1]
+def finish(mine_ref, *refs):
+    *part_refs, x_ref, cot_ref, gain_ref, input_out, gain_out, tail_s = refs
+    owners = len(part_refs)
+    own, width = x_ref.shape
     fold = width // own
-    gain = jnp.zeros((own, fold), F32)
-    for p in range(owners):
-        gain += parts_ref[p, :, width : width + fold].astype(F32)
-        gain += parts_ref[p, :, width + fold : width + 2 * fold].astype(F32)
+    for k in range(owners):
+        tail = part_refs[k][:, width:].astype(F32)
+        tail_s[partner(mine_ref[0], k, owners)] = tail[:, :fold] + tail[:, fold:]
+    gain = tail_s[0]
+    for p in range(1, owners):
+        gain += tail_s[p]
     for r in range(own):
         gain_out[:, r * fold : (r + 1) * fold] = gain[r : r + 1]
-    delta = parts_ref[0, :, :width].astype(F32)
-    for p in range(1, owners):
-        delta += parts_ref[p, :, :width].astype(F32)
+    delta = part_refs[0][:, :width].astype(F32)
+    for k in range(1, owners):
+        delta += part_refs[k][:, :width].astype(F32)
     inverse = row_inverse(x_ref, own, True, EPS_RMS)
     unit = x_ref[...].astype(F32) * inverse
     scaled = delta * gain_ref[...]
@@ -414,19 +496,24 @@
     dp = lax.axis_index("dp")
     first_row = (lax.axis_index(everyone) * rows).astype(jnp.int32).reshape(1)
     is_last = (section == sections - 1).astype(jnp.int32).reshape(1)
+    mine = dp.astype(jnp.int32).reshape(1)
 
     x_own, cot_own, gain = segment_inputs[0], segment_cotangents[0], norm_gain
-    both = lax.all_gather(jnp.stack([x_own, cot_own]), "dp", axis=0, tiled=False)
-
     block1 = 4 * rows
-    message = pl.pallas_call(
+    message, both = pl.pallas_call(
         pack_rows,
-        out_shape=shape((count, block1, cols), BF16),
-        in_specs=[vmem(), vmem()],
-        out_specs=vmem(),
-        compiler_params=params(16),
+        out_shape=(shape((count, block1, cols), BF16), shape((2, own, width), BF16)),
+        in_specs=[anywhere()] * 4,
+        out_specs=(vmem(), vmem()),
+        scratch_shapes=[
+            pltpu.VMEM((rows, width), BF16),
+            pltpu.VMEM((rows, width), BF16),
+            pltpu.SemaphoreType.DMA((4,)),
+        ],
+        compiler_params=params(BIG),
         name="pack_rows",
-    )(query_cache, passage_cache)
+    )(query_cache, passage_cache, x_own, cot_own)
+    both = lax.all_gather(both, "dp", axis=0, tiled=False)
     message = lax.all_to_all(message, everyone, 0, 0, tiled=True)
     parts, unit, inverse = pl.pallas_call(
         partial_scores,
@@ -448,7 +535,7 @@
         out_specs=vmem(),
         compiler_params=params(32),
         name="softmax_rows",
-    )(first_row, parts, hard_offsets)
+    )(first_row, parts, hard_offsets.T)
     message = lax.all_to_all(message, everyone, 0, 0, tiled=True)
     back = -(-(2 * rows + passages) // 16) * 16
     message = pl.pallas_call(
@@ -462,24 +549,25 @@
     message = lax.all_to_all(message, everyone, 0, 0, tiled=True)
 
     whole = lambda dims: pl.BlockSpec(dims, lambda i: (0,) * len(dims))
-    step = 256 if units % 256 == 0 else units
-    weight = pl.BlockSpec((width, step), lambda i: (0, i))
-    part = pl.BlockSpec((tokens, step), lambda i: (0, i))
+    ring = pltpu.SemaphoreType.DMA((WINDOW,))
+    step = min(512, width)
     normed, gate, up = pl.pallas_call(
         forward,
-        grid=(units // step,),
         out_shape=(
             shape((tokens, width), BF16),
             shape((tokens, units), F32),
             shape((tokens, units), F32),
         ),
-        in_specs=[
-            pl.BlockSpec((owners, None, own, width), lambda i: (0, 0, 0, 0)),
-            whole((1, width)),
-            weight,
-            weight,
+        in_specs=[anywhere(), vmem(), anywhere(), anywhere()],
+        out_specs=(vmem(), vmem(), vmem()),
+        scratch_shapes=[
+            pltpu.VMEM((owners, own, width), BF16),
+            pltpu.VMEM((WINDOW, step, units), BF16),
+            pltpu.VMEM((WINDOW, step, units), BF16),
+            pltpu.SemaphoreType.DMA((1,)),
+            ring,
+            ring,
         ],
-        out_specs=(whole((tokens, width)), part, part),
         compiler_params=params(BIG),
         cost_estimate=pl.CostEstimate(
             flops=4 * tokens * width * units,
@@ -489,34 +577,36 @@
         name="forward",
     )(both, gain, gate_weight[0], up_weight[0])
 
-    cuts = 8
+    cuts = max(1, width // 512)
     deep_cuts = units // 256 if units % 256 == 0 else 1
-    fold = width // own
+    part_shape = shape((own, width + 2 * (width // own)), BF16)
+    block = (WINDOW, width // cuts, units)
     outs = pl.pallas_call(
         lambda *refs: backward(cuts, deep_cuts, *refs),
         out_shape=(
             shape((rows, width), BF16),
             shape((rows, width), BF16),
-            shape((owners, own, width + 2 * fold), BF16),
             shape((tokens, units), BF16),
             shape((tokens, units), BF16),
             shape((tokens, units), BF16),
             shape((tokens, width), BF16),
-        ),
-        in_specs=[smem(), smem()] + [vmem()] * 4 + [anywhere()] * 3,
-        out_specs=tuple(vmem() for _ in range(7)),
+            shape((own, width), BF16),
+        )
+        + (part_shape,) * owners,
+        in_specs=[smem(), smem(), smem()] + [vmem()] * 4 + [anywhere()] * 3,
+        out_specs=tuple(vmem() for _ in range(7 + owners)),
         scratch_shapes=[
-            pltpu.VMEM((WINDOW, width // cuts, units), BF16),
-            pltpu.VMEM((WINDOW, width // cuts, units), BF16),
+            pltpu.VMEM(block, BF16),
+            pltpu.VMEM(block, BF16),
             pltpu.VMEM((WINDOW, units // deep_cuts, width), BF16),
-            pltpu.VMEM((1, width), F32),
-            pltpu.VMEM((tokens, width), F32),
-            pltpu.VMEM((tokens, 1), F32),
             pltpu.VMEM((units, tokens), BF16),
             pltpu.VMEM((units, tokens), BF16),
-            pltpu.SemaphoreType.DMA((WINDOW,)),
-            pltpu.SemaphoreType.DMA((WINDOW,)),
-            pltpu.SemaphoreType.DMA((WINDOW,)),
+            pltpu.VMEM((owners, own, width), BF16),
+            pltpu.VMEM((1, width), F32),
+            pltpu.VMEM((tokens, 1), F32),
+            ring,
+            ring,
+            ring,
         ],
         compiler_params=params(BIG),
         cost_estimate=pl.CostEstimate(
@@ -527,6 +617,7 @@
         name="backward",
     )(
         is_last,
+        mine,
         passage_lengths,
         message,
         both,
@@ -536,8 +627,11 @@
         up_weight[0],
         down_weight[0],
     )
-    query_grads, passage_grads, delta, hidden, d_up, d_gate, cot = outs
-    delta = lax.all_to_all(delta, "dp", 0, 0, tiled=True)
+    query_grads, passage_grads, hidden, d_up, d_gate, cot, cot_rows = outs[:7]
+    deltas = [outs[7]]
+    for k in range(1, owners):
+        pairs_ = [(partner(i, k, owners), i) for i in range(owners)]
+        deltas.append(lax.ppermute(outs[7 + k], "dp", pairs_))
 
     step = min(512, width)
     gate_grads, up_grads, down_grads = pl.pallas_call(
@@ -570,15 +664,15 @@
         name="weight_grads",
     )(normed, d_gate, d_up, hidden, cot)
 
-    cot_rows = lax.dynamic_slice_in_dim(cot, dp * own, own, axis=0)
     input_grads, gain_grads = pl.pallas_call(
         finish,
         out_shape=(shape((own, width), BF16), shape((1, width), F32)),
-        in_specs=[vmem()] * 4,
+        in_specs=[smem()] + [vmem()] * (owners + 3),
         out_specs=(vmem(), vmem()),
+        scratch_shapes=[pltpu.VMEM((owners, own, width // own), F32)],
         compiler_params=params(32),
         name="finish",
-    )(delta, x_own, cot_rows, gain)
+    )(mine, *deltas, x_own, cot_rows, gain)
     return (
         query_grads,
         passage_grads,

time: 150 us -> 144 us (0.960)
  waiting for transfers between devices: 21.2 us -> 13.6 us
  starting transfers between devices: 14.6 us -> 20.7 us
  local copies, waits for them, and re-layouts: 4.03 us -> 1.38 us
  other arithmetic: 1.7 us -> 0 us
  blocking collectives: 37.5 us -> 35.9 us
    ppermute x0 -> x7, starting transfers between devices: none -> 11.9 us  [local(): deltas.append(lax.ppermute(outs[7 + k], 'dp', pairs_))]
    all_to_all x1 -> x0, waiting for transfers between devices: 11.2 us -> none  [local(): delta = lax.all_to_all(delta, 'dp', 0, 0, tiled=True)]
    all_to_all x1 -> x0, starting transfers between devices: 5.95 us -> none  [local(): delta = lax.all_to_all(delta, 'dp', 0, 0, tiled=True)]
    ppermute x0 -> x7, waiting for transfers between devices: none -> 3.01 us  [local(): deltas.append(lax.ppermute(outs[7 + k], 'dp', pairs_))]
    unnamed x11 -> x12, local copies, waits for them, and re-layouts: 3.12 us -> 1.38 us
    another operation x1 -> x0, other arithmetic: 1.7 us -> none  [local(): jnp.stack([x_own, cot_own])]
    all_to_all x2, blocking collectives: 37.5 us -> 35.9 us  [local(): message = lax.all_to_all(message, everyone, 0, 0, tiled=True)]
  transfers between devices with their start and end apart: 4 -> 10, of which waited for: 2 -> 2; matrix products, arithmetic and copies ran while one was open for 1% -> 0% of each run, Pallas kernels for 22% -> 23%
where the time goes in v3:
time: 144 us; the launch traced here: 143 us
  Pallas kernels  57.2 us (40%)
  blocking collectives  35.9 us (25%)
  starting transfers between devices  20.7 us (14%)
  between operations  14.2 us (10%)
  waiting for transfers between devices  13.6 us (9%)
    all_to_all x2, blocking collectives, local(): message = lax.all_to_all(message, everyone, 0, 0, tiled=True)  35.9 us
    pallas_call x1, Pallas kernels, local(): pl.pallas_call(lambda *refs: backward(cuts, deep_cuts, *refs), out_shape=...  22 us
    pallas_call x1, Pallas kernels, local(): pl.pallas_call(weight_grads, grid=(width // step,), out_shape=(shape((wid...  16.7 us
    pallas_call x1, Pallas kernels, local(): pl.pallas_call(forward, out_shape=(shape((tokens, width), BF16), shape((t...  13.3 us
    ppermute x7, starting transfers between devices, local(): deltas.append(lax.ppermute(outs[7 + k], 'dp', pairs_))  11.9 us
    all_to_all x1, waiting for transfers between devices, local(): parts = lax.all_to_all(parts, everyone, 0, 0, tiled=True)  10.6 us
    all_to_all x1, starting transfers between devices, local(): message = lax.all_to_all(message, everyone, 0, 0, tiled=True)  4.64 us
    all_to_all x1, starting transfers between devices, local(): parts = lax.all_to_all(parts, everyone, 0, 0, tiled=True)  4.19 us
  transfers between devices with their start and end apart: 10, of which 2 were waited for; matrix products, arithmetic and copies ran while one was open for 0% of the time, Pallas kernels for 23%

profile of v3, /device:TPU:0, one launch (start us, length us, event | category | flops | bytes accessed | tf_op | source)
XLA Modules:
  0.0 143.1 jit_solution(12626583022960313129)
XLA Ops:
  7.2 0.0 all-gather.3.cloned.1.call-start
  7.2 1.9 %pack_rows.1 = (bf16[32,32,128]{2,1,0:T(8,128)(2,1)}, bf16[2,16,4096]{2,1,0:T(8,128)(2,1)}) custom-call(bf16[8,4096]{1,0:T(8,128)(2,1)} %query_hbm.1, bf16[8,4096]{1,0:T(8,128)(2,1)} %passage_hbm.1, bf16[16,4096]{1,0:T(8,128)(2,1)} %bitcast.14, bf16[16,4096]{1,0:T(8,128)(2,1)} %bitcast.24), custom_call_target="tpu_custom_call" | custom-call | tf_op jit(solution)/shard_map/pack_rows/pallas_call | solution.py:503
  9.2 18.3 %all_to_all.20.rows_ref = bf16[32,32,128]{2,1,0:T(8,128)(2,1)S(1)} all-to-all(bf16[32,32,128]{2,1,0:T(8,128)(2,1)} %get-tuple-element.35), channel_id=1, replica_groups=mesh['dp'=8,'segment'=4] {'dp','segment'}, dimensions={0} | all-to-all | bytes 524288 | tf_op jit(solution)/shard_map/all_to_all | solution.py:517
  27.5 1.0 partial_scores.1
  28.5 4.2 %all-to-all-start.1 = ((f32[32,8,256]{2,1,0:T(8,128)}), f32[32,8,256]{2,1,0:T(8,128)S(1)}, u32[]{:S(2)}, u32[]{:S(2)}) async-start(f32[32,8,256]{2,1,0:T(8,128)} %get-tuple-element.36), calls=%async_computation.1 | async-start | bytes 524288 | tf_op jit(solution)/shard_map/all_to_all | solution.py:530
  32.7 10.6 %all-to-all-done.1.parts_ref = f32[32,8,256]{2,1,0:T(8,128)S(1)} async-done(((f32[32,8,256]{2,1,0:T(8,128)}), f32[32,8,256]{2,1,0:T(8,128)S(1)}, u32[]{:S(2)}, u32[]{:S(2)}) %all-to-all-start.1) | async-done | bytes 262176 | tf_op jit(solution)/shard_map/all_to_all | solution.py:530
  43.3 0.7 copy-done.4
  43.9 0.3 softmax_rows.1
  44.2 17.6 %all_to_all.21.refs_0_ = bf16[32,16,256]{2,1,0:T(8,128)(2,1)S(1)} all-to-all(bf16[32,16,256]{2,1,0:T(8,128)(2,1)S(1)} %softmax_rows.1), channel_id=1, replica_groups=mesh['dp'=8,'segment'=4] {'dp','segment'}, dimensions={0} | all-to-all | bytes 524288 | tf_op jit(solution)/shard_map/all_to_all | solution.py:539
  61.8 1.0 pair_grads.1
  62.9 4.6 %all-to-all-start.3 = ((bf16[32,32,128]{2,1,0:T(8,128)(2,1)}), bf16[32,32,128]{2,1,0:T(8,128)(2,1)S(1)}, u32[]{:S(2)}, u32[]{:S(2)}) async-start(bf16[32,32,128]{2,1,0:T(8,128)(2,1)} %pair_grads.1), calls=%async_computation.3 | async-start | bytes 524288 | tf_op jit(solution)/shard_map/all_to_all | solution.py:549
  67.5 13.3 %forward.1 = (bf16[128,4096]{1,0:T(8,128)(2,1)}, f32[128,1792]{1,0:T(8,128)}, f32[128,1792]{1,0:T(8,128)}) custom-call(bf16[8,2,16,4096]{3,2,1,0:T(8,128)(2,1)} %bitcast.22, f32[1,4096]{1,0:T(1,128)} %refs_10_.1, bf16[4096,1792]{1,0:T(8,128)(2,1)} %bitcast.17, bf16[4096,1792]{1,0:T(8,128)(2,1)} %bitcast.19), custom_call_target="tpu_custom_call" | custom-call | flops 3758096384 | bytes 29360128 | tf_op jit(solution)/shard_map/forward/pallas_call | solution.py:554
  80.9 0.7 copy-done.5
  81.6 22.0 %backward.1 = (bf16[8,4096]{1,0:T(8,128)(2,1)}, bf16[8,4096]{1,0:T(8,128)(2,1)}, bf16[128,1792]{1,0:T(8,128)(2,1)}, bf16[128,1792]{1,0:T(8,128)(2,1)}, bf16[128,...) custom-call(s32[1]{0:T(128)} %bitcast.refs_0_, ...), custom_call_target="tpu_custom_call" | custom-call | flops 5637144576 | bytes 44040192 | tf_op jit(solution)/shard_map/backward/pallas_call | solution.py:584
  103.6 1.8 %collective-permute-start = (bf16[16,4608]{1,0:T(8,128)(2,1)}, bf16[16,4608]{1,0:T(8,128)(2,1)S(1)}, u32[]{:S(2)}, u32[]{:S(2)}) collective-permute-start(bf16[16,4608]{1,0:T(8,128)(2,1)} %get-tuple-element.45), channel_id=1, source_target_pairs={{4,0},{0,4},{12,8},{8,12},{20,16},{16,20},{28,24},{24,28},{5,1},{1... | collective-permute-start | bytes 442376 | tf_op jit(solution)/shard_map/ppermute | solution.py:634
  105.4 1.5 %collective-permute-start.1 = (bf16[16,4608]{1,0:T(8,128)(2,1)}, bf16[16,4608]{1,0:T(8,128)(2,1)S(1)}, u32[]{:S(2)}, u32[]{:S(2)}) collective-permute-start(bf16[16,4608]{1,0:T(8,128)(2,1)} %get-tuple-element.46), channel_id=1, source_target_pairs={{8,0},{12,4},{0,8},{4,12},{24,16},{28,20},{16,24},{20,28},{9,1},{1... | collective-permute-start | bytes 442376 | tf_op jit(solution)/shard_map/ppermute | solution.py:634
  106.9 0.3 collective-permute-start.2
  107.1 2.7 %collective-permute-start.3 = (bf16[16,4608]{1,0:T(8,128)(2,1)}, bf16[16,4608]{1,0:T(8,128)(2,1)S(1)}, u32[]{:S(2)}, u32[]{:S(2)}) collective-permute-start(bf16[16,4608]{1,0:T(8,128)(2,1)} %get-tuple-element.48), channel_id=1, source_target_pairs={{16,0},{20,4},{24,8},{28,12},{0,16},{4,20},{8,24},{12,28},{17,1},{... | collective-permute-start | bytes 442376 | tf_op jit(solution)/shard_map/ppermute | solution.py:634
  109.8 1.5 %collective-permute-start.4 = (bf16[16,4608]{1,0:T(8,128)(2,1)}, bf16[16,4608]{1,0:T(8,128)(2,1)S(1)}, u32[]{:S(2)}, u32[]{:S(2)}) collective-permute-start(bf16[16,4608]{1,0:T(8,128)(2,1)} %get-tuple-element.49), channel_id=1, source_target_pairs={{20,0},{16,4},{28,8},{24,12},{4,16},{0,20},{12,24},{8,28},{21,1},{... | collective-permute-start | bytes 442376 | tf_op jit(solution)/shard_map/ppermute | solution.py:634
  111.3 3.3 %collective-permute-start.5 = (bf16[16,4608]{1,0:T(8,128)(2,1)}, bf16[16,4608]{1,0:T(8,128)(2,1)S(1)}, u32[]{:S(2)}, u32[]{:S(2)}) collective-permute-start(bf16[16,4608]{1,0:T(8,128)(2,1)} %get-tuple-element.50), channel_id=1, source_target_pairs={{24,0},{28,4},{16,8},{20,12},{8,16},{12,20},{0,24},{4,28},{25,1},{... | collective-permute-start | bytes 442376 | tf_op jit(solution)/shard_map/ppermute | solution.py:634
  114.6 3.0 %collective-permute-done.1.refs_2_ = bf16[16,4608]{1,0:T(8,128)(2,1)S(1)} collective-permute-done((bf16[16,4608]{1,0:T(8,128)(2,1)}, bf16[16,4608]{1,0:T(8,128)(2,1)S(1)}, u32[]{:S(2)}, u32[]{:S(2)}) %collective-permute-start.1) | collective-permute-done | bytes 147488 | tf_op jit(solution)/shard_map/ppermute | solution.py:634
  117.6 0.8 collective-permute-start.6
  118.4 16.7 %weight_grads.1 = (bf16[4096,1792]{1,0:T(8,128)(2,1)}, bf16[4096,1792]{1,0:T(8,128)(2,1)}, bf16[1792,4096]{1,0:T(8,128)(2,1)}) custom-call(bf16[128,4096]{1,0:T(8,128)(2,1)} %get-tuple-element.54.normed_ref, bf16[128,1792]{1,0:T(8,128)(2,1)} %get-tuple-element.55.d_gate_ref, bf16[128,1792]{1,0:T(8,128)(2,1)} %get-tuple-element.56.d_up_ref, ...), custom_call_target="tpu_custom_call" | custom-call | flops 5637144576 | bytes 44040192 | tf_op jit(solution)/shard_map/weight_grads/pallas_call | solution.py:637
  135.2 1.0 finish.1
  (19 shorter events, 0.1 us)
Async XLA Ops:
  7.2 60.4 %all-gather.3.cloned.1.call-start = ((), (), s32[]{:S(2)}) async-start(), calls=%async_computation.4 | async-start | bytes 2359296 | tf_op jit(solution)/shard_map/all_gather | solution.py:516
  28.5 14.8 %all-to-all-start.1 = ((f32[32,8,256]{2,1,0:T(8,128)}), f32[32,8,256]{2,1,0:T(8,128)S(1)}, u32[]{:S(2)}, u32[]{:S(2)}) async-start(f32[32,8,256]{2,1,0:T(8,128)} %get-tuple-element.36), calls=%async_computation.1 | async-start | bytes 524288 | tf_op jit(solution)/shard_map/all_to_all | solution.py:530
  43.3 0.7 copy-start.4
  62.9 18.0 %all-to-all-start.3 = ((bf16[32,32,128]{2,1,0:T(8,128)(2,1)}), bf16[32,32,128]{2,1,0:T(8,128)(2,1)S(1)}, u32[]{:S(2)}, u32[]{:S(2)}) async-start(bf16[32,32,128]{2,1,0:T(8,128)(2,1)} %pair_grads.1), calls=%async_computation.3 | async-start | bytes 524288 | tf_op jit(solution)/shard_map/all_to_all | solution.py:549
  80.8 0.7 copy-start.5
  103.5 31.6 %copy-start = (bf16[1,16,4096]{2,1,0:T(8,128)(2,1)S(1)}, bf16[1,16,4096]{2,1,0:T(8,128)(2,1)}, u32[]{:S(2)}) copy-start(bf16[1,16,4096]{2,1,0:T(8,128)(2,1)} %param.14) | copy-start | bytes 393220
  103.5 31.6 %copy-start.1 = (bf16[16,4608]{1,0:T(8,128)(2,1)S(1)}, bf16[16,4608]{1,0:T(8,128)(2,1)}, u32[]{:S(2)}) copy-start(bf16[16,4608]{1,0:T(8,128)(2,1)} %get-tuple-element.44.refs_0_) | copy-start | bytes 442372
  103.5 31.6 %copy-start.2 = (bf16[16,4096]{1,0:T(8,128)(2,1)S(1)}, bf16[16,4096]{1,0:T(8,128)(2,1)}, u32[]{:S(2)}) copy-start(bf16[16,4096]{1,0:T(8,128)(2,1)} %get-tuple-element.52.refs_9_) | copy-start | bytes 393220
  103.6 31.6 %copy-start.3 = (f32[1,4096]{1,0:T(1,128)S(1)}, f32[1,4096]{1,0:T(1,128)}, u32[]{:S(2)}) copy-start(f32[1,4096]{1,0:T(1,128)} %refs_10_.1) | copy-start | bytes 49156
  103.6 7.7 %collective-permute-start = (bf16[16,4608]{1,0:T(8,128)(2,1)}, bf16[16,4608]{1,0:T(8,128)(2,1)S(1)}, u32[]{:S(2)}, u32[]{:S(2)}) collective-permute-start(bf16[16,4608]{1,0:T(8,128)(2,1)} %get-tuple-element.45), channel_id=1, source_target_pairs={{4,0},{0,4},{12,8},{8,12},{20,16},{16,20},{28,24},{24,28},{5,1},{1... | collective-permute-start | bytes 442376 | tf_op jit(solution)/shard_map/ppermute | solution.py:634
  105.4 12.2 %collective-permute-start.1 = (bf16[16,4608]{1,0:T(8,128)(2,1)}, bf16[16,4608]{1,0:T(8,128)(2,1)S(1)}, u32[]{:S(2)}, u32[]{:S(2)}) collective-permute-start(bf16[16,4608]{1,0:T(8,128)(2,1)} %get-tuple-element.46), channel_id=1, source_target_pairs={{8,0},{12,4},{0,8},{4,12},{24,16},{28,20},{16,24},{20,28},{9,1},{1... | collective-permute-start | bytes 442376 | tf_op jit(solution)/shard_map/ppermute | solution.py:634
  106.9 28.3 %collective-permute-start.2 = (bf16[16,4608]{1,0:T(8,128)(2,1)}, bf16[16,4608]{1,0:T(8,128)(2,1)S(1)}, u32[]{:S(2)}, u32[]{:S(2)}) collective-permute-start(bf16[16,4608]{1,0:T(8,128)(2,1)} %get-tuple-element.47), channel_id=1, source_target_pairs={{12,0},{8,4},{4,8},{0,12},{28,16},{24,20},{20,24},{16,28},{13,1},{... | collective-permute-start | bytes 442376 | tf_op jit(solution)/shard_map/ppermute | solution.py:634
  107.1 28.0 %collective-permute-start.3 = (bf16[16,4608]{1,0:T(8,128)(2,1)}, bf16[16,4608]{1,0:T(8,128)(2,1)S(1)}, u32[]{:S(2)}, u32[]{:S(2)}) collective-permute-start(bf16[16,4608]{1,0:T(8,128)(2,1)} %get-tuple-element.48), channel_id=1, source_target_pairs={{16,0},{20,4},{24,8},{28,12},{0,16},{4,20},{8,24},{12,28},{17,1},{... | collective-permute-start | bytes 442376 | tf_op jit(solution)/shard_map/ppermute | solution.py:634
  109.8 25.3 %collective-permute-start.4 = (bf16[16,4608]{1,0:T(8,128)(2,1)}, bf16[16,4608]{1,0:T(8,128)(2,1)S(1)}, u32[]{:S(2)}, u32[]{:S(2)}) collective-permute-start(bf16[16,4608]{1,0:T(8,128)(2,1)} %get-tuple-element.49), channel_id=1, source_target_pairs={{20,0},{16,4},{28,8},{24,12},{4,16},{0,20},{12,24},{8,28},{21,1},{... | collective-permute-start | bytes 442376 | tf_op jit(solution)/shard_map/ppermute | solution.py:634
  111.3 23.9 %collective-permute-start.5 = (bf16[16,4608]{1,0:T(8,128)(2,1)}, bf16[16,4608]{1,0:T(8,128)(2,1)S(1)}, u32[]{:S(2)}, u32[]{:S(2)}) collective-permute-start(bf16[16,4608]{1,0:T(8,128)(2,1)} %get-tuple-element.50), channel_id=1, source_target_pairs={{24,0},{28,4},{16,8},{20,12},{8,16},{12,20},{0,24},{4,28},{25,1},{... | collective-permute-start | bytes 442376 | tf_op jit(solution)/shard_map/ppermute | solution.py:634
  117.6 17.6 %collective-permute-start.6 = (bf16[16,4608]{1,0:T(8,128)(2,1)}, bf16[16,4608]{1,0:T(8,128)(2,1)S(1)}, u32[]{:S(2)}, u32[]{:S(2)}) collective-permute-start(bf16[16,4608]{1,0:T(8,128)(2,1)} %get-tuple-element.51), channel_id=1, source_target_pairs={{28,0},{24,4},{20,8},{16,12},{12,16},{8,20},{4,24},{0,28},{29,1},{... | collective-permute-start | bytes 442376 | tf_op jit(solution)/shard_map/ppermute | solution.py:634
Sparse Core Ops, SparseCore 0:
  10.7 55.8 all-gather.2

commit v4 on v3

--- a/solution.py
+++ b/solution.py
@@ -71,16 +71,12 @@
     return lax.rsqrt(total + eps)
 
 
-def pack_rows(
-    query_hbm, passage_hbm, x_hbm, cot_hbm, out_ref, both_ref, query_ref, passage_ref, sems
-):
+def pack_rows(query_hbm, passage_hbm, out_ref, query_ref, passage_ref, sems):
     count, block, cols = out_ref.shape
     rows = query_ref.shape[0]
     copies = [
         pltpu.make_async_copy(query_hbm, query_ref, sems.at[0]),
         pltpu.make_async_copy(passage_hbm, passage_ref, sems.at[1]),
-        pltpu.make_async_copy(x_hbm, both_ref.at[0], sems.at[2]),
-        pltpu.make_async_copy(cot_hbm, both_ref.at[1], sems.at[3]),
     ]
     for copy in copies:
         copy.start()
@@ -108,8 +104,6 @@
             axis=0,
         )
         out_ref[peer] = both.astype(BF16)
-    copies[2].wait()
-    copies[3].wait()
 
 
 def partial_scores(rows_ref, out_ref, unit_ref, inverse_ref):
@@ -208,7 +202,8 @@
 
 
 def forward(
-    both_hbm,
+    near_hbm,
+    far_hbm,
     gain_ref,
     gate_hbm,
     up_hbm,
@@ -227,13 +222,19 @@
     blocks = width // step
     gate_ring = Ring(gate_hbm, gate_w, gate_sem, step)
     up_ring = Ring(up_hbm, up_w, up_sem, step)
-    fetch = pltpu.make_async_copy(both_hbm.at[:, 0], x_s, x_sem.at[0])
-    fetch.start()
+    half = tokens // 2
+    fetches = [
+        pltpu.make_async_copy(near_hbm, x_s.at[pl.ds(0, half)], x_sem.at[0]),
+        pltpu.make_async_copy(far_hbm, x_s.at[pl.ds(half, half)], x_sem.at[1]),
+    ]
+    for fetch in fetches:
+        fetch.start()
     for c in range(min(WINDOW, blocks)):
         gate_ring.copy(c).start()
         up_ring.copy(c).start()
-    fetch.wait()
-    x = x_s[...].reshape(tokens, width).astype(F32)
+    for fetch in fetches:
+        fetch.wait()
+    x = x_s[...].astype(F32)
     inverse = lax.rsqrt(jnp.sum(x * x, axis=1, keepdims=True) / width + EPS_RMS)
     normed_out[...] = (x * inverse * gain_ref[...]).astype(BF16)
 
@@ -261,13 +262,7 @@
     lax.fori_loop(1, blocks, more, 0)
 
 
-def partner(mine, k, n):
-    if n & (n - 1) == 0:
-        return mine ^ k
-    return (k + n - mine) % n
-
-
-def delta_columns(mine, cuts, rings, started, both_ref, d_gate_t, d_up_t, outs, delta_s, gain_s, inverse_s):
+def delta_columns(cuts, rings, started, x_s, d_gate_t, d_up_t, outs, gain_s, inverse_s):
     owners = len(outs)
     own, total = outs[0].shape
     width = gain_s.shape[1]
@@ -277,7 +272,7 @@
     for c in range(started, min(WINDOW, cuts)):
         gate_ring.copy(c).start()
         up_ring.copy(c).start()
-    x = both_ref[:, 0].reshape(tokens, width).astype(F32)
+    x = x_s[...].astype(F32)
     inverse_s[...] = lax.rsqrt(jnp.sum(x * x, axis=1, keepdims=True) / width + EPS_RMS)
 
     def one(c, carry):
@@ -291,8 +286,8 @@
         ).T
         low = delta.astype(BF16)
         for owner in range(owners):
-            delta_s[partner(mine, owner, owners), :, cut] = low[owner * own : (owner + 1) * own]
-        unit = both_ref[:, 0, :, cut].reshape(tokens, step).astype(F32) * inverse_s[...]
+            outs[owner][:, cut] = low[owner * own : (owner + 1) * own]
+        unit = x_s[:, cut].astype(F32) * inverse_s[...]
         gain_s[:, cut] = jnp.sum(delta * unit, axis=0, keepdims=True)
 
         @pl.when(c + WINDOW < cuts)
@@ -310,18 +305,21 @@
     high, low, _ = split3(gain)
     tail = jnp.concatenate([high, low], axis=1).astype(BF16)
     for k in range(owners):
-        outs[k][:, :width] = delta_s[k]
         outs[k][:, width:] = tail
 
 
 def backward(
+    order,
     cuts,
     deep_cuts,
     last_ref,
     mine_ref,
     lengths_ref,
     back_ref,
-    both_ref,
+    x_near,
+    x_far,
+    cot_near,
+    cot_far,
     gate_ref,
     up_ref,
     gate_hbm,
@@ -333,10 +331,9 @@
     d_up_out,
     d_gate_out,
     cot_out,
-    cot_own_out,
     *more,
 ):
-    *delta_outs, gate_w, up_w, down_w, d_up_t, d_gate_t, delta_s, gain_s, inverse_s = more[:-3]
+    *delta_outs, gate_w, up_w, down_w, d_up_t, d_gate_t, x_s, gain_s, inverse_s = more[:-3]
     gate_sem, up_sem, down_sem = more[-3:]
     tokens, width = cot_out.shape
     units = gate_ref.shape[1]
@@ -353,7 +350,12 @@
     count, block, cols = back_ref.shape
     rows = query_out.shape[0]
     passages = block - 2 * rows
-    token = iota((tokens, 1), 0)
+    token = jnp.concatenate(
+        [iota((own, 1), 0) + (mine_ref[0] ^ mask) * own for mask in order], axis=0
+    )
+    half = tokens // 2
+    x_s[:half, :] = x_near[...]
+    x_s[half:, :] = x_far[...]
     lane = iota((tokens, passages), 1)
     start = jnp.int32(0)
     member = jnp.zeros((tokens, passages), F32)
@@ -373,10 +375,8 @@
         passage_out[:, cut] = piece[rows : 2 * rows].astype(BF16)
         spread = jnp.dot(member, piece[2 * rows :].astype(BF16), preferred_element_type=F32)
         pooled = (spread * scale).astype(BF16)
-        given = both_ref[:, 1, :, cut].reshape(tokens, cols)
+        given = jnp.concatenate([cot_near[:, cut], cot_far[:, cut]], axis=0)
         cot_out[:, cut] = jnp.where(last, pooled, given)
-
-    cot_own_out[...] = cot_out[pl.ds(pl.multiple_of(mine_ref[0] * own, own), own), :]
 
     def down_step(c, carry):
         slot = lax.rem(c, WINDOW)
@@ -408,15 +408,13 @@
 
     lax.fori_loop(0, deep_cuts, down_step, 0)
     delta_columns(
-        mine_ref[0],
         cuts,
         (gate_ring, up_ring),
         early,
-        both_ref,
+        x_s,
         d_gate_t,
         d_up_t,
         delta_outs,
-        delta_s,
         gain_s,
         inverse_s,
     )
@@ -440,14 +438,14 @@
     ).astype(BF16)
 
 
-def finish(mine_ref, *refs):
+def finish(order, mine_ref, *refs):
     *part_refs, x_ref, cot_ref, gain_ref, input_out, gain_out, tail_s = refs
     owners = len(part_refs)
     own, width = x_ref.shape
     fold = width // own
     for k in range(owners):
         tail = part_refs[k][:, width:].astype(F32)
-        tail_s[partner(mine_ref[0], k, owners)] = tail[:, :fold] + tail[:, fold:]
+        tail_s[mine_ref[0] ^ order[k]] = tail[:, :fold] + tail[:, fold:]
     gain = tail_s[0]
     for p in range(1, owners):
         gain += tail_s[p]
@@ -498,23 +496,42 @@
     is_last = (section == sections - 1).astype(jnp.int32).reshape(1)
     mine = dp.astype(jnp.int32).reshape(1)
 
+    assert owners & (owners - 1) == 0 and owners > 1
     x_own, cot_own, gain = segment_inputs[0], segment_cotangents[0], norm_gain
     block1 = 4 * rows
-    message, both = pl.pallas_call(
+    message = pl.pallas_call(
         pack_rows,
-        out_shape=(shape((count, block1, cols), BF16), shape((2, own, width), BF16)),
-        in_specs=[anywhere()] * 4,
-        out_specs=(vmem(), vmem()),
+        out_shape=shape((count, block1, cols), BF16),
+        in_specs=[anywhere()] * 2,
+        out_specs=vmem(),
         scratch_shapes=[
             pltpu.VMEM((rows, width), BF16),
             pltpu.VMEM((rows, width), BF16),
-            pltpu.SemaphoreType.DMA((4,)),
+            pltpu.SemaphoreType.DMA((2,)),
         ],
         compiler_params=params(BIG),
         name="pack_rows",
-    )(query_cache, passage_cache, x_own, cot_own)
-    both = lax.all_gather(both, "dp", axis=0, tiled=False)
+    )(query_cache, passage_cache)
+    order = [0]
+    x_half, cot_half = x_own, cot_own
+    moved = []
+
+    def double(values):
+        nonlocal x_half, cot_half
+        if len(order) == owners:
+            return values
+        if moved:
+            x_half = jnp.concatenate([x_half, moved[0]], axis=0)
+            cot_half = jnp.concatenate([cot_half, moved[1]], axis=0)
+        mask = owners // 2 // len(order)
+        swap = [(i, i ^ mask) for i in range(owners)]
+        moved[:] = [lax.ppermute(x_half, "dp", swap), lax.ppermute(cot_half, "dp", swap)]
+        order.extend([o ^ mask for o in order])
+        return values
+
+    message = double(message)
     message = lax.all_to_all(message, everyone, 0, 0, tiled=True)
+    message = double(message)
     parts, unit, inverse = pl.pallas_call(
         partial_scores,
         out_shape=(
@@ -528,6 +545,7 @@
         name="partial_scores",
     )(message)
     parts = lax.all_to_all(parts, everyone, 0, 0, tiled=True)
+    parts = double(parts)
     message = pl.pallas_call(
         softmax_rows,
         out_shape=shape((count, 2 * rows, pairs), BF16),
@@ -548,6 +566,9 @@
     )(message, unit, inverse)
     message = lax.all_to_all(message, everyone, 0, 0, tiled=True)
 
+    while len(order) < owners:
+        message = double(message)
+    halves = (x_half, moved[0], cot_half, moved[1])
     whole = lambda dims: pl.BlockSpec(dims, lambda i: (0,) * len(dims))
     ring = pltpu.SemaphoreType.DMA((WINDOW,))
     step = min(512, width)
@@ -558,13 +579,13 @@
             shape((tokens, units), F32),
             shape((tokens, units), F32),
         ),
-        in_specs=[anywhere(), vmem(), anywhere(), anywhere()],
+        in_specs=[anywhere(), anywhere(), vmem(), anywhere(), anywhere()],
         out_specs=(vmem(), vmem(), vmem()),
         scratch_shapes=[
-            pltpu.VMEM((owners, own, width), BF16),
+            pltpu.VMEM((tokens, width), BF16),
             pltpu.VMEM((WINDOW, step, units), BF16),
             pltpu.VMEM((WINDOW, step, units), BF16),
-            pltpu.SemaphoreType.DMA((1,)),
+            pltpu.SemaphoreType.DMA((2,)),
             ring,
             ring,
         ],
@@ -575,14 +596,14 @@
             transcendentals=0,
         ),
         name="forward",
-    )(both, gain, gate_weight[0], up_weight[0])
+    )(*halves[:2], gain, gate_weight[0], up_weight[0])
 
     cuts = max(1, width // 512)
     deep_cuts = units // 256 if units % 256 == 0 else 1
     part_shape = shape((own, width + 2 * (width // own)), BF16)
     block = (WINDOW, width // cuts, units)
     outs = pl.pallas_call(
-        lambda *refs: backward(cuts, deep_cuts, *refs),
+        lambda *refs: backward(order, cuts, deep_cuts, *refs),
         out_shape=(
             shape((rows, width), BF16),
             shape((rows, width), BF16),
@@ -590,18 +611,17 @@
             shape((tokens, units), BF16),
             shape((tokens, units), BF16),
             shape((tokens, width), BF16),
-            shape((own, width), BF16),
         )
         + (part_shape,) * owners,
-        in_specs=[smem(), smem(), smem()] + [vmem()] * 4 + [anywhere()] * 3,
-        out_specs=tuple(vmem() for _ in range(7 + owners)),
+        in_specs=[smem(), smem(), smem()] + [vmem()] * 7 + [anywhere()] * 3,
+        out_specs=tuple(vmem() for _ in range(6 + owners)),
         scratch_shapes=[
             pltpu.VMEM(block, BF16),
             pltpu.VMEM(block, BF16),
             pltpu.VMEM((WINDOW, units // deep_cuts, width), BF16),
             pltpu.VMEM((units, tokens), BF16),
             pltpu.VMEM((units, tokens), BF16),
-            pltpu.VMEM((owners, own, width), BF16),
+            pltpu.VMEM((tokens, width), BF16),
             pltpu.VMEM((1, width), F32),
             pltpu.VMEM((tokens, 1), F32),
             ring,
@@ -620,18 +640,17 @@
         mine,
         passage_lengths,
         message,
-        both,
+        *halves,
         gate,
         up,
         gate_weight[0],
         up_weight[0],
         down_weight[0],
     )
-    query_grads, passage_grads, hidden, d_up, d_gate, cot, cot_rows = outs[:7]
-    deltas = [outs[7]]
-    for k in range(1, owners):
-        pairs_ = [(partner(i, k, owners), i) for i in range(owners)]
-        deltas.append(lax.ppermute(outs[7 + k], "dp", pairs_))
+    query_grads, passage_grads, hidden, d_up, d_gate, cot = outs[:6]
+    deltas = [outs[6]]
+    for mask, part in zip(order[1:], outs[7:]):
+        deltas.append(lax.ppermute(part, "dp", [(i, i ^ mask) for i in range(owners)]))
 
     step = min(512, width)
     gate_grads, up_grads, down_grads = pl.pallas_call(
@@ -665,14 +684,14 @@
     )(normed, d_gate, d_up, hidden, cot)
 
     input_grads, gain_grads = pl.pallas_call(
-        finish,
+        lambda *refs: finish(order, *refs),
         out_shape=(shape((own, width), BF16), shape((1, width), F32)),
         in_specs=[smem()] + [vmem()] * (owners + 3),
         out_specs=(vmem(), vmem()),
         scratch_shapes=[pltpu.VMEM((owners, own, width // own), F32)],
         compiler_params=params(32),
         name="finish",
-    )(mine, *deltas, x_own, cot_rows, gain)
+    )(mine, *deltas, x_own, cot[:own], gain)
     return (
         query_grads,
         passage_grads,

time: 144 us -> 136 us (0.944); the launches traced: 143 us -> 133 us
  blocking collectives: 35.9 us -> 0 us
  waiting for transfers between devices: 13.6 us -> 33.9 us
  between operations: 14.2 us -> 0.86 us
  starting transfers between devices: 20.7 us -> 33.9 us
  other arithmetic: 0 us -> 3.73 us
  local copies, waits for them, and re-layouts: 1.38 us -> 3.1 us
    all_to_all x2 -> x0, blocking collectives: 35.9 us -> none  [local(): message = lax.all_to_all(message, everyone, 0, 0, tiled=True)]
    all_to_all x1 -> x3, waiting for transfers between devices: 0.01 us -> 17.6 us  [local(): message = lax.all_to_all(message, everyone, 0, 0, tiled=True)]
    all_to_all x1 -> x3, starting transfers between devices: 4.64 us -> 12.6 us  [local(): message = lax.all_to_all(message, everyone, 0, 0, tiled=True)]
    ppermute x7 -> x13, starting transfers between devices: 11.9 us -> 18.7 us  [the longest x7 10.3 us: local(): lax.ppermute(part, 'dp', [(i, i ^ mask) for i in range(owners)])]
    ppermute x7 -> x13, waiting for transfers between devices: 3.01 us -> 9.87 us  [the longest x7 4.79 us: local(): lax.ppermute(part, 'dp', [(i, i ^ mask) for i in range(owners)])]
    all_to_all x1, waiting for transfers between devices: 10.6 us -> 6.45 us  [local(): parts = lax.all_to_all(parts, everyone, 0, 0, tiled=True)]
    concatenate x0 -> x4, other arithmetic: none -> 3.73 us  [the longest x2 1.87 us: double(): x_half = jnp.concatenate([x_half, moved[0]], axis=0)]
    all_to_all x1, starting transfers between devices: 4.19 us -> 2.59 us  [local(): parts = lax.all_to_all(parts, everyone, 0, 0, tiled=True)]
  transfers between devices with their start and end apart: 10 -> 17, of which waited for: 2 -> 7; matrix products, arithmetic and copies ran while one was open for 0% -> 3% of each run, Pallas kernels for 23% -> 25%
where the time goes in v4:
time: 136 us; the launch traced here: 133 us
  Pallas kernels  57.7 us (42%)
  starting transfers between devices  33.9 us (25%)
  waiting for transfers between devices  33.9 us (25%)
  other arithmetic  3.73 us (3%)
  local copies, waits for them, and re-layouts  3.1 us (2%)
    pallas_call x1, Pallas kernels, local(): pl.pallas_call(lambda *refs: backward(order, cuts, deep_cuts, *refs), out...  21.9 us
    all_to_all x3, waiting for transfers between devices, local(): message = lax.all_to_all(message, everyone, 0, 0, tiled=True)  17.6 us
    pallas_call x1, Pallas kernels, local(): pl.pallas_call(weight_grads, grid=(width // step,), out_shape=(shape((wid...  16.7 us
    pallas_call x1, Pallas kernels, local(): pl.pallas_call(forward, out_shape=(shape((tokens, width), BF16), shape((t...  13.3 us
    all_to_all x3, starting transfers between devices, local(): message = lax.all_to_all(message, everyone, 0, 0, tiled=True)  12.6 us
    ppermute x7, starting transfers between devices, local(): lax.ppermute(part, 'dp', [(i, i ^ mask) for i in range(owners)])  10.3 us
    all_to_all x1, waiting for transfers between devices, local(): parts = lax.all_to_all(parts, everyone, 0, 0, tiled=True)  6.45 us
    ppermute x3, starting transfers between devices, double(): lax.ppermute(x_half, 'dp', swap)  6.19 us
  transfers between devices with their start and end apart: 17, of which 7 were waited for; matrix products, arithmetic and copies ran while one was open for 3% of the time, Pallas kernels for 25%

profile of v4, /device:TPU:0, one launch (start us, length us, event | category | flops | bytes accessed | tf_op | source)
XLA Modules:
  0.0 133.2 jit_solution(15522931869387363495)
XLA Ops:
  0.6 1.8 %pack_rows.1 = bf16[32,32,128]{2,1,0:T(8,128)(2,1)} custom-call(bf16[8,4096]{1,0:T(8,128)(2,1)} %query_hbm.1, bf16[8,4096]{1,0:T(8,128)(2,1)} %passage_hbm.1), custom_call_target="tpu_custom_call" | custom-call | tf_op jit(solution)/shard_map/pack_rows/pallas_call | solution.py:502
  2.5 7.3 %all-to-all-start = ((bf16[32,32,128]{2,1,0:T(8,128)(2,1)}), bf16[32,32,128]{2,1,0:T(8,128)(2,1)S(1)}, u32[]{:S(2)}, u32[]{:S(2)}) async-start(bf16[32,32,128]{2,1,0:T(8,128)(2,1)} %pack_rows.1), calls=%async_computation | async-start | bytes 524288 | tf_op jit(solution)/shard_map/all_to_all | solution.py:533
  9.8 2.7 %collective-permute-start = (bf16[16,4096]{1,0:T(8,128)(2,1)}, bf16[16,4096]{1,0:T(8,128)(2,1)S(1)}, u32[]{:S(2)}, u32[]{:S(2)}) collective-permute-start(bf16[16,4096]{1,0:T(8,128)(2,1)} %bitcast.13), channel_id=1, source_target_pairs={{0,16},{4,20},{8,24},{12,28},{16,0},{20,4},{24,8},{28,12},{1,17},{... | collective-permute-start | bytes 393224 | tf_op jit(solution)/shard_map/ppermute | solution.py:528
  12.8 13.4 %all-to-all-done.rows_ref = bf16[32,32,128]{2,1,0:T(8,128)(2,1)S(1)} async-done(((bf16[32,32,128]{2,1,0:T(8,128)(2,1)}), bf16[32,32,128]{2,1,0:T(8,128)(2,1)S(1)}, u32[]{:S(2)}, u32[]{:S(2)}) %all-to-all-start) | async-done | bytes 262176 | tf_op jit(solution)/shard_map/all_to_all | solution.py:533
  27.2 2.6 %all-to-all-start.1 = ((f32[32,8,256]{2,1,0:T(8,128)}), f32[32,8,256]{2,1,0:T(8,128)S(1)}, u32[]{:S(2)}, u32[]{:S(2)}) async-start(f32[32,8,256]{2,1,0:T(8,128)} %get-tuple-element.32), calls=%async_computation.1 | async-start | bytes 524288 | tf_op jit(solution)/shard_map/all_to_all | solution.py:547
  30.7 1.8 %collective-permute-start.1 = (bf16[32,4096]{1,0:T(8,128)(2,1)S(1)}, bf16[32,4096]{1,0:T(8,128)(2,1)S(1)}, u32[]{:S(2)}, u32[]{:S(2)}) collective-permute-start(bf16[32,4096]{1,0:T(8,128)(2,1)S(1)} %pad_maximum_fusion.2), channel_id=1, source_target_pairs={{0,8},{4,12},{8,0},{12,4},{16,24},{20,28},{24,16},{28,20},{1,9},{5... | collective-permute-start | bytes 786440 | tf_op jit(solution)/shard_map/ppermute | solution.py:528
  33.8 6.4 %all-to-all-done.1.parts_ref = f32[32,8,256]{2,1,0:T(8,128)S(1)} async-done(((f32[32,8,256]{2,1,0:T(8,128)}), f32[32,8,256]{2,1,0:T(8,128)S(1)}, u32[]{:S(2)}, u32[]{:S(2)}) %all-to-all-start.1) | async-done | bytes 262176 | tf_op jit(solution)/shard_map/all_to_all | solution.py:547
  41.9 2.6 %all-to-all-start.2 = ((bf16[32,16,256]{2,1,0:T(8,128)(2,1)}), bf16[32,16,256]{2,1,0:T(8,128)(2,1)S(1)}, u32[]{:S(2)}, u32[]{:S(2)}) async-start(bf16[32,16,256]{2,1,0:T(8,128)(2,1)} %softmax_rows.1), calls=%async_computation.2 | async-start | bytes 524288 | tf_op jit(solution)/shard_map/all_to_all | solution.py:557
  45.4 1.7 %collective-permute-start.2 = (bf16[64,4096]{1,0:T(8,128)(2,1)S(1)}, bf16[64,4096]{1,0:T(8,128)(2,1)S(1)}, u32[]{:S(2)}, u32[]{:S(2)}) collective-permute-start(bf16[64,4096]{1,0:T(8,128)(2,1)S(1)} %pad_maximum_fusion.near_hbm.refs_4_), channel_id=1, source_target_pairs={{0,4},{4,0},{8,12},{12,8},{16,20},{20,16},{24,28},{28,24},{1,5},{5... | collective-permute-start | bytes 1572872 | tf_op jit(solution)/shard_map/ppermute | solution.py:528
  47.1 1.3 %collective-permute-done.4 = bf16[32,4096]{1,0:T(8,128)(2,1)S(1)} collective-permute-done((bf16[32,4096]{1,0:T(8,128)(2,1)S(1)}, bf16[32,4096]{1,0:T(8,128)(2,1)S(1)}, u32[]{:S(2)}, u32[]{:S(2)}) %collective-permute-start.4) | collective-permute-done | bytes 262176 | tf_op jit(solution)/shard_map/ppermute | solution.py:528
  49.4 1.5 %collective-permute-start.5 = (bf16[64,4096]{1,0:T(8,128)(2,1)S(1)}, bf16[64,4096]{1,0:T(8,128)(2,1)}, u32[]{:S(2)}, u32[]{:S(2)}) collective-permute-start(bf16[64,4096]{1,0:T(8,128)(2,1)S(1)} %pad_maximum_fusion.1.refs_6_), channel_id=1, source_target_pairs={{0,4},{4,0},{8,12},{12,8},{16,20},{20,16},{24,28},{28,24},{1,5},{5... | collective-permute-start | bytes 1572872 | tf_op jit(solution)/shard_map/ppermute | solution.py:528
  51.0 3.7 %all-to-all-done.2.refs_0_ = bf16[32,16,256]{2,1,0:T(8,128)(2,1)S(1)} async-done(((bf16[32,16,256]{2,1,0:T(8,128)(2,1)}), bf16[32,16,256]{2,1,0:T(8,128)(2,1)S(1)}, u32[]{:S(2)}, u32[]{:S(2)}) %all-to-all-start.2) | async-done | bytes 262176 | tf_op jit(solution)/shard_map/all_to_all | solution.py:557
  54.7 1.0 pair_grads.1
  55.7 2.7 %all-to-all-start.3 = ((bf16[32,32,128]{2,1,0:T(8,128)(2,1)}), bf16[32,32,128]{2,1,0:T(8,128)(2,1)S(1)}, u32[]{:S(2)}, u32[]{:S(2)}) async-start(bf16[32,32,128]{2,1,0:T(8,128)(2,1)} %pair_grads.1), calls=%async_computation.3 | async-start | bytes 524288 | tf_op jit(solution)/shard_map/all_to_all | solution.py:567
  58.5 3.7 %collective-permute-done.2.far_hbm.refs_5_ = bf16[64,4096]{1,0:T(8,128)(2,1)S(1)} collective-permute-done((bf16[64,4096]{1,0:T(8,128)(2,1)S(1)}, bf16[64,4096]{1,0:T(8,128)(2,1)S(1)}, u32[]{:S(2)}, u32[]{:S(2)}) %collective-permute-start.2) | collective-permute-done | bytes 524320 | tf_op jit(solution)/shard_map/ppermute | solution.py:528
  63.0 13.3 %forward.1 = (bf16[128,4096]{1,0:T(8,128)(2,1)}, f32[128,1792]{1,0:T(8,128)}, f32[128,1792]{1,0:T(8,128)}) custom-call(bf16[64,4096]{1,0:T(8,128)(2,1)} %copy-done.4, bf16[64,4096]{1,0:T(8,128)(2,1)} %copy-done.5, f32[1,4096]{1,0:T(1,128)} %refs_11_.1, bf16[4096,1792]{1,0:T(8,128)(2,1)} %bitcast.18, bf16[4096,1792]{1,0:T(8,128)(2,1)} %bitcast.20), custom_call_target="tpu_custom_call" | custom-call | flops 3758096384 | bytes 29360128 | tf_op jit(solution)/shard_map/forward/pallas_call | solution.py:575
  77.4 21.9 %backward.1 = (bf16[8,4096]{1,0:T(8,128)(2,1)}, bf16[8,4096]{1,0:T(8,128)(2,1)}, bf16[128,1792]{1,0:T(8,128)(2,1)}, bf16[128,1792]{1,0:T(8,128)(2,1)}, bf16[128,...) custom-call(s32[1]{0:T(128)} %bitcast.refs_0_, ...), custom_call_target="tpu_custom_call" | custom-call | flops 5637144576 | bytes 44040192 | tf_op jit(solution)/shard_map/backward/pallas_call | solution.py:605
  99.4 2.3 %collective-permute-start.6 = (bf16[16,4608]{1,0:T(8,128)(2,1)}, bf16[16,4608]{1,0:T(8,128)(2,1)S(1)}, u32[]{:S(2)}, u32[]{:S(2)}) collective-permute-start(bf16[16,4608]{1,0:T(8,128)(2,1)} %get-tuple-element.40), channel_id=1, source_target_pairs={{0,16},{4,20},{8,24},{12,28},{16,0},{20,4},{24,8},{28,12},{1,17},{... | collective-permute-start | bytes 442376 | tf_op jit(solution)/shard_map/ppermute | solution.py:653
  101.7 1.7 %collective-permute-start.7 = (bf16[16,4608]{1,0:T(8,128)(2,1)}, bf16[16,4608]{1,0:T(8,128)(2,1)S(1)}, u32[]{:S(2)}, u32[]{:S(2)}) collective-permute-start(bf16[16,4608]{1,0:T(8,128)(2,1)} %get-tuple-element.41), channel_id=1, source_target_pairs={{0,8},{4,12},{8,0},{12,4},{16,24},{20,28},{24,16},{28,20},{1,9},{5... | collective-permute-start | bytes 442376 | tf_op jit(solution)/shard_map/ppermute | solution.py:653
  103.8 1.3 collective-permute-start.9
  105.1 1.5 %collective-permute-start.10 = (bf16[16,4608]{1,0:T(8,128)(2,1)}, bf16[16,4608]{1,0:T(8,128)(2,1)S(1)}, u32[]{:S(2)}, u32[]{:S(2)}) collective-permute-start(bf16[16,4608]{1,0:T(8,128)(2,1)} %get-tuple-element.44), channel_id=1, source_target_pairs={{0,20},{4,16},{8,28},{12,24},{16,4},{20,0},{24,12},{28,8},{1,21},{... | collective-permute-start | bytes 442376 | tf_op jit(solution)/shard_map/ppermute | solution.py:653
  106.6 4.8 %collective-permute-done.6.refs_2_ = bf16[16,4608]{1,0:T(8,128)(2,1)S(1)} collective-permute-done((bf16[16,4608]{1,0:T(8,128)(2,1)}, bf16[16,4608]{1,0:T(8,128)(2,1)S(1)}, u32[]{:S(2)}, u32[]{:S(2)}) %collective-permute-start.6) | collective-permute-done | bytes 147488 | tf_op jit(solution)/shard_map/ppermute | solution.py:653
  111.4 3.1 %collective-permute-start.12 = (bf16[16,4608]{1,0:T(8,128)(2,1)}, bf16[16,4608]{1,0:T(8,128)(2,1)S(1)}, u32[]{:S(2)}, u32[]{:S(2)}) collective-permute-start(bf16[16,4608]{1,0:T(8,128)(2,1)} %get-tuple-element.46), channel_id=1, source_target_pairs={{0,28},{4,24},{8,20},{12,16},{16,12},{20,8},{24,4},{28,0},{1,29},{... | collective-permute-start | bytes 442376 | tf_op jit(solution)/shard_map/ppermute | solution.py:653
  114.5 16.7 %weight_grads.1 = (bf16[4096,1792]{1,0:T(8,128)(2,1)}, bf16[4096,1792]{1,0:T(8,128)(2,1)}, bf16[1792,4096]{1,0:T(8,128)(2,1)}) custom-call(bf16[128,4096]{1,0:T(8,128)(2,1)} %get-tuple-element.49.normed_ref, bf16[128,1792]{1,0:T(8,128)(2,1)} %get-tuple-element.50.d_gate_ref, bf16[128,1792]{1,0:T(8,128)(2,1)} %get-tuple-element.51.d_up_ref, ...), custom_call_target="tpu_custom_call" | custom-call | flops 5637144576 | bytes 44040192 | tf_op jit(solution)/shard_map/weight_grads/pallas_call | solution.py:656
  (39 shorter events, 11.3 us)
Async XLA Ops:
  2.5 23.7 %all-to-all-start = ((bf16[32,32,128]{2,1,0:T(8,128)(2,1)}), bf16[32,32,128]{2,1,0:T(8,128)(2,1)S(1)}, u32[]{:S(2)}, u32[]{:S(2)}) async-start(bf16[32,32,128]{2,1,0:T(8,128)(2,1)} %pack_rows.1), calls=%async_computation | async-start | bytes 524288 | tf_op jit(solution)/shard_map/all_to_all | solution.py:533
  9.8 20.0 %collective-permute-start = (bf16[16,4096]{1,0:T(8,128)(2,1)}, bf16[16,4096]{1,0:T(8,128)(2,1)S(1)}, u32[]{:S(2)}, u32[]{:S(2)}) collective-permute-start(bf16[16,4096]{1,0:T(8,128)(2,1)} %bitcast.13), channel_id=1, source_target_pairs={{0,16},{4,20},{8,24},{12,28},{16,0},{20,4},{24,8},{28,12},{1,17},{... | collective-permute-start | bytes 393224 | tf_op jit(solution)/shard_map/ppermute | solution.py:528
  12.5 20.0 %collective-permute-start.3 = (bf16[16,4096]{1,0:T(8,128)(2,1)}, bf16[16,4096]{1,0:T(8,128)(2,1)S(1)}, u32[]{:S(2)}, u32[]{:S(2)}) collective-permute-start(bf16[16,4096]{1,0:T(8,128)(2,1)} %bitcast.23), channel_id=1, source_target_pairs={{0,16},{4,20},{8,24},{12,28},{16,0},{20,4},{24,8},{28,12},{1,17},{... | collective-permute-start | bytes 393224 | tf_op jit(solution)/shard_map/ppermute | solution.py:528
  27.2 13.1 %all-to-all-start.1 = ((f32[32,8,256]{2,1,0:T(8,128)}), f32[32,8,256]{2,1,0:T(8,128)S(1)}, u32[]{:S(2)}, u32[]{:S(2)}) async-start(f32[32,8,256]{2,1,0:T(8,128)} %get-tuple-element.32), calls=%async_computation.1 | async-start | bytes 524288 | tf_op jit(solution)/shard_map/all_to_all | solution.py:547
  30.7 13.8 %collective-permute-start.1 = (bf16[32,4096]{1,0:T(8,128)(2,1)S(1)}, bf16[32,4096]{1,0:T(8,128)(2,1)S(1)}, u32[]{:S(2)}, u32[]{:S(2)}) collective-permute-start(bf16[32,4096]{1,0:T(8,128)(2,1)S(1)} %pad_maximum_fusion.2), channel_id=1, source_target_pairs={{0,8},{4,12},{8,0},{12,4},{16,24},{20,28},{24,16},{28,20},{1,9},{5... | collective-permute-start | bytes 786440 | tf_op jit(solution)/shard_map/ppermute | solution.py:528
  33.4 15.1 %collective-permute-start.4 = (bf16[32,4096]{1,0:T(8,128)(2,1)S(1)}, bf16[32,4096]{1,0:T(8,128)(2,1)S(1)}, u32[]{:S(2)}, u32[]{:S(2)}) collective-permute-start(bf16[32,4096]{1,0:T(8,128)(2,1)S(1)} %pad_maximum_fusion.3), channel_id=1, source_target_pairs={{0,8},{4,12},{8,0},{12,4},{16,24},{20,28},{24,16},{28,20},{1,9},{5... | collective-permute-start | bytes 786440 | tf_op jit(solution)/shard_map/ppermute | solution.py:528
  41.9 12.8 %all-to-all-start.2 = ((bf16[32,16,256]{2,1,0:T(8,128)(2,1)}), bf16[32,16,256]{2,1,0:T(8,128)(2,1)S(1)}, u32[]{:S(2)}, u32[]{:S(2)}) async-start(bf16[32,16,256]{2,1,0:T(8,128)(2,1)} %softmax_rows.1), calls=%async_computation.2 | async-start | bytes 524288 | tf_op jit(solution)/shard_map/all_to_all | solution.py:557
  45.4 16.8 %copy-start.4 = (bf16[64,4096]{1,0:T(8,128)(2,1)}, bf16[64,4096]{1,0:T(8,128)(2,1)S(1)}, u32[]{:S(2)}) copy-start(bf16[64,4096]{1,0:T(8,128)(2,1)S(1)} %pad_maximum_fusion.near_hbm.refs_4_) | copy-start | bytes 1572868
  45.4 16.8 %collective-permute-start.2 = (bf16[64,4096]{1,0:T(8,128)(2,1)S(1)}, bf16[64,4096]{1,0:T(8,128)(2,1)S(1)}, u32[]{:S(2)}, u32[]{:S(2)}) collective-permute-start(bf16[64,4096]{1,0:T(8,128)(2,1)S(1)} %pad_maximum_fusion.near_hbm.refs_4_), channel_id=1, source_target_pairs={{0,4},{4,0},{8,12},{12,8},{16,20},{20,16},{24,28},{28,24},{1,5},{5... | collective-permute-start | bytes 1572872 | tf_op jit(solution)/shard_map/ppermute | solution.py:528
  49.4 26.9 %copy-start.6 = (bf16[64,4096]{1,0:T(8,128)(2,1)}, bf16[64,4096]{1,0:T(8,128)(2,1)S(1)}, u32[]{:S(2)}) copy-start(bf16[64,4096]{1,0:T(8,128)(2,1)S(1)} %pad_maximum_fusion.1.refs_6_) | copy-start | bytes 1572868
  49.4 26.9 %collective-permute-start.5 = (bf16[64,4096]{1,0:T(8,128)(2,1)S(1)}, bf16[64,4096]{1,0:T(8,128)(2,1)}, u32[]{:S(2)}, u32[]{:S(2)}) collective-permute-start(bf16[64,4096]{1,0:T(8,128)(2,1)S(1)} %pad_maximum_fusion.1.refs_6_), channel_id=1, source_target_pairs={{0,4},{4,0},{8,12},{12,8},{16,20},{20,16},{24,28},{28,24},{1,5},{5... | collective-permute-start | bytes 1572872 | tf_op jit(solution)/shard_map/ppermute | solution.py:528
  55.7 21.0 %all-to-all-start.3 = ((bf16[32,32,128]{2,1,0:T(8,128)(2,1)}), bf16[32,32,128]{2,1,0:T(8,128)(2,1)S(1)}, u32[]{:S(2)}, u32[]{:S(2)}) async-start(bf16[32,32,128]{2,1,0:T(8,128)(2,1)} %pair_grads.1), calls=%async_computation.3 | async-start | bytes 524288 | tf_op jit(solution)/shard_map/all_to_all | solution.py:567
  62.2 0.8 copy-start.5
  76.7 0.7 copy-start.7
  99.3 32.8 %copy-start = (bf16[1,16,4096]{2,1,0:T(8,128)(2,1)S(1)}, bf16[1,16,4096]{2,1,0:T(8,128)(2,1)}, u32[]{:S(2)}) copy-start(bf16[1,16,4096]{2,1,0:T(8,128)(2,1)} %param.14) | copy-start | bytes 393220
  99.3 32.8 %copy-start.1 = (bf16[16,4608]{1,0:T(8,128)(2,1)S(1)}, bf16[16,4608]{1,0:T(8,128)(2,1)}, u32[]{:S(2)}) copy-start(bf16[16,4608]{1,0:T(8,128)(2,1)} %get-tuple-element.39.refs_1_) | copy-start | bytes 442372
  99.3 32.8 %copy-start.2 = (f32[1,4096]{1,0:T(1,128)S(1)}, f32[1,4096]{1,0:T(1,128)}, u32[]{:S(2)}) copy-start(f32[1,4096]{1,0:T(1,128)} %refs_11_.1) | copy-start | bytes 49156
  99.4 12.0 %collective-permute-start.6 = (bf16[16,4608]{1,0:T(8,128)(2,1)}, bf16[16,4608]{1,0:T(8,128)(2,1)S(1)}, u32[]{:S(2)}, u32[]{:S(2)}) collective-permute-start(bf16[16,4608]{1,0:T(8,128)(2,1)} %get-tuple-element.40), channel_id=1, source_target_pairs={{0,16},{4,20},{8,24},{12,28},{16,0},{20,4},{24,8},{28,12},{1,17},{... | collective-permute-start | bytes 442376 | tf_op jit(solution)/shard_map/ppermute | solution.py:653
  101.7 9.7 %collective-permute-start.7 = (bf16[16,4608]{1,0:T(8,128)(2,1)}, bf16[16,4608]{1,0:T(8,128)(2,1)S(1)}, u32[]{:S(2)}, u32[]{:S(2)}) collective-permute-start(bf16[16,4608]{1,0:T(8,128)(2,1)} %get-tuple-element.41), channel_id=1, source_target_pairs={{0,8},{4,12},{8,0},{12,4},{16,24},{20,28},{24,16},{28,20},{1,9},{5... | collective-permute-start | bytes 442376 | tf_op jit(solution)/shard_map/ppermute | solution.py:653
  103.4 28.7 %collective-permute-start.8 = (bf16[16,4608]{1,0:T(8,128)(2,1)}, bf16[16,4608]{1,0:T(8,128)(2,1)S(1)}, u32[]{:S(2)}, u32[]{:S(2)}) collective-permute-start(bf16[16,4608]{1,0:T(8,128)(2,1)} %get-tuple-element.42), channel_id=1, source_target_pairs={{0,24},{4,28},{8,16},{12,20},{16,8},{20,12},{24,0},{28,4},{1,25},{... | collective-permute-start | bytes 442376 | tf_op jit(solution)/shard_map/ppermute | solution.py:653
  103.8 28.3 %collective-permute-start.9 = (bf16[16,4608]{1,0:T(8,128)(2,1)}, bf16[16,4608]{1,0:T(8,128)(2,1)S(1)}, u32[]{:S(2)}, u32[]{:S(2)}) collective-permute-start(bf16[16,4608]{1,0:T(8,128)(2,1)} %get-tuple-element.43), channel_id=1, source_target_pairs={{0,4},{4,0},{8,12},{12,8},{16,20},{20,16},{24,28},{28,24},{1,5},{5... | collective-permute-start | bytes 442376 | tf_op jit(solution)/shard_map/ppermute | solution.py:653
  105.1 27.0 %collective-permute-start.10 = (bf16[16,4608]{1,0:T(8,128)(2,1)}, bf16[16,4608]{1,0:T(8,128)(2,1)S(1)}, u32[]{:S(2)}, u32[]{:S(2)}) collective-permute-start(bf16[16,4608]{1,0:T(8,128)(2,1)} %get-tuple-element.44), channel_id=1, source_target_pairs={{0,20},{4,16},{8,28},{12,24},{16,4},{20,0},{24,12},{28,8},{1,21},{... | collective-permute-start | bytes 442376 | tf_op jit(solution)/shard_map/ppermute | solution.py:653
  111.4 20.7 %collective-permute-start.11 = (bf16[16,4608]{1,0:T(8,128)(2,1)}, bf16[16,4608]{1,0:T(8,128)(2,1)S(1)}, u32[]{:S(2)}, u32[]{:S(2)}) collective-permute-start(bf16[16,4608]{1,0:T(8,128)(2,1)} %get-tuple-element.45), channel_id=1, source_target_pairs={{0,12},{4,8},{8,4},{12,0},{16,28},{20,24},{24,20},{28,16},{1,13},{... | collective-permute-start | bytes 442376 | tf_op jit(solution)/shard_map/ppermute | solution.py:653
  111.4 20.7 %collective-permute-start.12 = (bf16[16,4608]{1,0:T(8,128)(2,1)}, bf16[16,4608]{1,0:T(8,128)(2,1)S(1)}, u32[]{:S(2)}, u32[]{:S(2)}) collective-permute-start(bf16[16,4608]{1,0:T(8,128)(2,1)} %get-tuple-element.46), channel_id=1, source_target_pairs={{0,28},{4,24},{8,20},{12,16},{16,12},{20,8},{24,4},{28,0},{1,29},{... | collective-permute-start | bytes 442376 | tf_op jit(solution)/shard_map/ppermute | solution.py:653
  (1 other events, 0.7 us)

commit v5 on v4

--- a/solution.py
+++ b/solution.py
@@ -331,6 +331,7 @@
     d_up_out,
     d_gate_out,
     cot_out,
+    cot_own_out,
     *more,
 ):
     *delta_outs, gate_w, up_w, down_w, d_up_t, d_gate_t, x_s, gain_s, inverse_s = more[:-3]
@@ -377,6 +378,8 @@
         pooled = (spread * scale).astype(BF16)
         given = jnp.concatenate([cot_near[:, cut], cot_far[:, cut]], axis=0)
         cot_out[:, cut] = jnp.where(last, pooled, given)
+
+    cot_own_out[...] = cot_out[:own, :]
 
     def down_step(c, carry):
         slot = lax.rem(c, WINDOW)
@@ -525,7 +528,10 @@
             cot_half = jnp.concatenate([cot_half, moved[1]], axis=0)
         mask = owners // 2 // len(order)
         swap = [(i, i ^ mask) for i in range(owners)]
-        moved[:] = [lax.ppermute(x_half, "dp", swap), lax.ppermute(cot_half, "dp", swap)]
+        x_far = lax.ppermute(x_half, "dp", swap)
+        if mask == 1:
+            x_far, cot_half = lax.optimization_barrier((x_far, cot_half))
+        moved[:] = [x_far, lax.ppermute(cot_half, "dp", swap)]
         order.extend([o ^ mask for o in order])
         return values
 
@@ -611,10 +617,11 @@
             shape((tokens, units), BF16),
             shape((tokens, units), BF16),
             shape((tokens, width), BF16),
+            shape((own, width), BF16),
         )
         + (part_shape,) * owners,
         in_specs=[smem(), smem(), smem()] + [vmem()] * 7 + [anywhere()] * 3,
-        out_specs=tuple(vmem() for _ in range(6 + owners)),
+        out_specs=tuple(vmem() for _ in range(7 + owners)),
         scratch_shapes=[
             pltpu.VMEM(block, BF16),
             pltpu.VMEM(block, BF16),
@@ -647,10 +654,11 @@
         up_weight[0],
         down_weight[0],
     )
-    query_grads, passage_grads, hidden, d_up, d_gate, cot = outs[:6]
-    deltas = [outs[6]]
-    for mask, part in zip(order[1:], outs[7:]):
-        deltas.append(lax.ppermute(part, "dp", [(i, i ^ mask) for i in range(owners)]))
+    query_grads, passage_grads, hidden, d_up, d_gate, cot, cot_rows = outs[:7]
+    deltas = list(outs[7:])
+    for mask in range(1, owners):
+        j = order.index(mask)
+        deltas[j] = lax.ppermute(deltas[j], "dp", [(i, i ^ mask) for i in range(owners)])
 
     step = min(512, width)
     gate_grads, up_grads, down_grads = pl.pallas_call(
@@ -691,7 +699,7 @@
         scratch_shapes=[pltpu.VMEM((owners, own, width // own), F32)],
         compiler_params=params(32),
         name="finish",
-    )(mine, *deltas, x_own, cot[:own], gain)
+    )(mine, *deltas, x_own, cot_rows, gain)
     return (
         query_grads,
         passage_grads,

time: 136 us -> 126 us (0.926); the launches traced: 133 us -> 126 us
  waiting for transfers between devices: 33.9 us -> 24.7 us
  starting transfers between devices: 33.9 us -> 37.3 us
  local copies, waits for them, and re-layouts: 3.1 us -> 1.4 us
    ppermute x13, starting transfers between devices: 18.7 us -> 25.4 us  [the longest x7 11.8 us: local(): lax.ppermute(deltas[j], 'dp', [(i, i ^ mask) for i in range(owners)])]
    all_to_all x3, waiting for transfers between devices: 17.6 us -> 12.3 us  [local(): message = lax.all_to_all(message, everyone, 0, 0, tiled=True)]
    all_to_all x3, starting transfers between devices: 12.6 us -> 9 us  [local(): message = lax.all_to_all(message, everyone, 0, 0, tiled=True)]
    ppermute x13, waiting for transfers between devices: 9.87 us -> 7.23 us  [the longest x7 3.76 us: local(): lax.ppermute(deltas[j], 'dp', [(i, i ^ mask) for i in range(owners)])]
  transfers between devices with their start and end apart: 17 -> 17, of which waited for: 7 -> 5; matrix products, arithmetic and copies ran while one was open for 3% -> 3% of each run, Pallas kernels for 25% -> 28%
where the time goes in v5:
time: 126 us
  Pallas kernels  57.7 us (46%)
  starting transfers between devices  37.3 us (30%)
  waiting for transfers between devices  24.7 us (20%)
  other arithmetic  3.73 us (3%)
  local copies, waits for them, and re-layouts  1.4 us (1%)
    pallas_call x1, Pallas kernels, local(): pl.pallas_call(lambda *refs: backward(order, cuts, deep_cuts, *refs), out...  21.9 us
    pallas_call x1, Pallas kernels, local(): pl.pallas_call(weight_grads, grid=(width // step,), out_shape=(shape((wid...  16.7 us
    pallas_call x1, Pallas kernels, local(): pl.pallas_call(forward, out_shape=(shape((tokens, width), BF16), shape((t...  13.3 us
    all_to_all x3, waiting for transfers between devices, local(): message = lax.all_to_all(message, everyone, 0, 0, tiled=True)  12.3 us
    ppermute x7, starting transfers between devices, local(): lax.ppermute(deltas[j], 'dp', [(i, i ^ mask) for i in range(owners)])  11.8 us
    all_to_all x3, starting transfers between devices, local(): message = lax.all_to_all(message, everyone, 0, 0, tiled=True)  9 us
    ppermute x3, starting transfers between devices, double(): x_far = lax.ppermute(x_half, 'dp', swap)  7.21 us
    ppermute x3, starting transfers between devices, double(): moved[:] = [x_far, lax.ppermute(cot_half, 'dp', swap)]  6.39 us
  transfers between devices with their start and end apart: 17, of which 5 were waited for; matrix products, arithmetic and copies ran while one was open for 3% of the time, Pallas kernels for 28%

profile of v5, /device:TPU:0, one launch (start us, length us, event | category | flops | bytes accessed | tf_op | source)
XLA Modules:
  0.0 125.7 jit_solution(16358547474682347352)
XLA Ops:
  0.6 4.1 %collective-permute-start = (bf16[16,4096]{1,0:T(8,128)(2,1)}, bf16[16,4096]{1,0:T(8,128)(2,1)S(1)}, u32[]{:S(2)}, u32[]{:S(2)}) collective-permute-start(bf16[16,4096]{1,0:T(8,128)(2,1)} %bitcast.13), channel_id=1, source_target_pairs={{0,16},{4,20},{8,24},{12,28},{16,0},{20,4},{24,8},{28,12},{1,17},{... | collective-permute-start | bytes 393224 | tf_op jit(solution)/shard_map/ppermute | solution.py:531
  4.7 1.8 %pack_rows.1 = bf16[32,32,128]{2,1,0:T(8,128)(2,1)} custom-call(bf16[8,4096]{1,0:T(8,128)(2,1)} %query_hbm.1, bf16[8,4096]{1,0:T(8,128)(2,1)} %passage_hbm.1), custom_call_target="tpu_custom_call" | custom-call | tf_op jit(solution)/shard_map/pack_rows/pallas_call | solution.py:505
  6.6 3.8 %all-to-all-start = ((bf16[32,32,128]{2,1,0:T(8,128)(2,1)}), bf16[32,32,128]{2,1,0:T(8,128)(2,1)S(1)}, u32[]{:S(2)}, u32[]{:S(2)}) async-start(bf16[32,32,128]{2,1,0:T(8,128)(2,1)} %pack_rows.1), calls=%async_computation | async-start | bytes 524288 | tf_op jit(solution)/shard_map/all_to_all | solution.py:539
  10.4 2.7 %collective-permute-start.3 = (bf16[16,4096]{1,0:T(8,128)(2,1)}, bf16[16,4096]{1,0:T(8,128)(2,1)S(1)}, u32[]{:S(2)}, u32[]{:S(2)}) collective-permute-start(bf16[16,4096]{1,0:T(8,128)(2,1)} %bitcast.23), channel_id=1, source_target_pairs={{0,16},{4,20},{8,24},{12,28},{16,0},{20,4},{24,8},{28,12},{1,17},{... | collective-permute-start | bytes 393224 | tf_op jit(solution)/shard_map/ppermute | solution.py:534
  14.1 1.6 %collective-permute-start.1 = (bf16[32,4096]{1,0:T(8,128)(2,1)S(1)}, bf16[32,4096]{1,0:T(8,128)(2,1)S(1)}, u32[]{:S(2)}, u32[]{:S(2)}) collective-permute-start(bf16[32,4096]{1,0:T(8,128)(2,1)S(1)} %pad_maximum_fusion.2), channel_id=1, source_target_pairs={{0,8},{4,12},{8,0},{12,4},{16,24},{20,28},{24,16},{28,20},{1,9},{5... | collective-permute-start | bytes 786440 | tf_op jit(solution)/shard_map/ppermute | solution.py:531
  15.6 7.9 %all-to-all-done.rows_ref = bf16[32,32,128]{2,1,0:T(8,128)(2,1)S(1)} async-done(((bf16[32,32,128]{2,1,0:T(8,128)(2,1)}), bf16[32,32,128]{2,1,0:T(8,128)(2,1)S(1)}, u32[]{:S(2)}, u32[]{:S(2)}) %all-to-all-start) | async-done | bytes 262176 | tf_op jit(solution)/shard_map/all_to_all | solution.py:539
  24.5 2.8 %all-to-all-start.1 = ((f32[32,8,256]{2,1,0:T(8,128)}), f32[32,8,256]{2,1,0:T(8,128)S(1)}, u32[]{:S(2)}, u32[]{:S(2)}) async-start(f32[32,8,256]{2,1,0:T(8,128)} %get-tuple-element.35), calls=%async_computation.1 | async-start | bytes 524288 | tf_op jit(solution)/shard_map/all_to_all | solution.py:553
  28.3 1.8 %collective-permute-start.4 = (bf16[32,4096]{1,0:T(8,128)(2,1)S(1)}, bf16[32,4096]{1,0:T(8,128)(2,1)S(1)}, u32[]{:S(2)}, u32[]{:S(2)}) collective-permute-start(bf16[32,4096]{1,0:T(8,128)(2,1)S(1)} %pad_maximum_fusion.3), channel_id=1, source_target_pairs={{0,8},{4,12},{8,0},{12,4},{16,24},{20,28},{24,16},{28,20},{1,9},{5... | collective-permute-start | bytes 786440 | tf_op jit(solution)/shard_map/ppermute | solution.py:534
  31.1 1.5 %collective-permute-start.2 = (bf16[64,4096]{1,0:T(8,128)(2,1)S(1)}, bf16[64,4096]{1,0:T(8,128)(2,1)S(1)}, u32[]{:S(2)}, u32[]{:S(2)}) collective-permute-start(bf16[64,4096]{1,0:T(8,128)(2,1)S(1)} %pad_maximum_fusion.near_hbm.refs_4_), channel_id=1, source_target_pairs={{0,4},{4,0},{8,12},{12,8},{16,20},{20,16},{24,28},{28,24},{1,5},{5... | collective-permute-start | bytes 1572872 | tf_op jit(solution)/shard_map/ppermute | solution.py:531
  32.7 5.2 %all-to-all-done.1.parts_ref = f32[32,8,256]{2,1,0:T(8,128)S(1)} async-done(((f32[32,8,256]{2,1,0:T(8,128)}), f32[32,8,256]{2,1,0:T(8,128)S(1)}, u32[]{:S(2)}, u32[]{:S(2)}) %all-to-all-start.1) | async-done | bytes 262176 | tf_op jit(solution)/shard_map/all_to_all | solution.py:553
  39.5 2.6 %all-to-all-start.2 = ((bf16[32,16,256]{2,1,0:T(8,128)(2,1)}), bf16[32,16,256]{2,1,0:T(8,128)(2,1)S(1)}, u32[]{:S(2)}, u32[]{:S(2)}) async-start(bf16[32,16,256]{2,1,0:T(8,128)(2,1)} %softmax_rows.1), calls=%async_computation.2 | async-start | bytes 524288 | tf_op jit(solution)/shard_map/all_to_all | solution.py:563
  43.1 3.5 %collective-permute-done.2.far_hbm.refs_5_ = bf16[64,4096]{1,0:T(8,128)(2,1)S(1)} collective-permute-done((bf16[64,4096]{1,0:T(8,128)(2,1)S(1)}, bf16[64,4096]{1,0:T(8,128)(2,1)S(1)}, u32[]{:S(2)}, u32[]{:S(2)}) %collective-permute-start.2) | collective-permute-done | bytes 524320 | tf_op jit(solution)/shard_map/ppermute | solution.py:531
  46.5 1.8 %collective-permute-start.5 = (bf16[64,4096]{1,0:T(8,128)(2,1)S(1)}, bf16[64,4096]{1,0:T(8,128)(2,1)}, u32[]{:S(2)}, u32[]{:S(2)}) collective-permute-start(bf16[64,4096]{1,0:T(8,128)(2,1)S(1)} %pad_maximum_fusion.1.refs_6_), channel_id=1, source_target_pairs={{0,4},{4,0},{8,12},{12,8},{16,20},{20,16},{24,28},{28,24},{1,5},{5... | collective-permute-start | bytes 1572872 | tf_op jit(solution)/shard_map/ppermute | solution.py:534
  48.3 4.4 %all-to-all-done.2.refs_0_ = bf16[32,16,256]{2,1,0:T(8,128)(2,1)S(1)} async-done(((bf16[32,16,256]{2,1,0:T(8,128)(2,1)}), bf16[32,16,256]{2,1,0:T(8,128)(2,1)S(1)}, u32[]{:S(2)}, u32[]{:S(2)}) %all-to-all-start.2) | async-done | bytes 262176 | tf_op jit(solution)/shard_map/all_to_all | solution.py:563
  53.7 2.6 %all-to-all-start.3 = ((bf16[32,32,128]{2,1,0:T(8,128)(2,1)}), bf16[32,32,128]{2,1,0:T(8,128)(2,1)S(1)}, u32[]{:S(2)}, u32[]{:S(2)}) async-start(bf16[32,32,128]{2,1,0:T(8,128)(2,1)} %pair_grads.1), calls=%async_computation.3 | async-start | bytes 524288 | tf_op jit(solution)/shard_map/all_to_all | solution.py:573
  56.3 13.3 %forward.1 = (bf16[128,4096]{1,0:T(8,128)(2,1)}, f32[128,1792]{1,0:T(8,128)}, f32[128,1792]{1,0:T(8,128)}) custom-call(bf16[64,4096]{1,0:T(8,128)(2,1)} %copy-done.5, bf16[64,4096]{1,0:T(8,128)(2,1)} %copy-done.6, f32[1,4096]{1,0:T(1,128)} %refs_11_.1, bf16[4096,1792]{1,0:T(8,128)(2,1)} %bitcast.18, bf16[4096,1792]{1,0:T(8,128)(2,1)} %bitcast.20), custom_call_target="tpu_custom_call" | custom-call | flops 3758096384 | bytes 29360128 | tf_op jit(solution)/shard_map/forward/pallas_call | solution.py:581
  70.4 21.9 %backward.1 = (bf16[8,4096]{1,0:T(8,128)(2,1)}, bf16[8,4096]{1,0:T(8,128)(2,1)}, bf16[128,1792]{1,0:T(8,128)(2,1)}, bf16[128,1792]{1,0:T(8,128)(2,1)}, bf16[128,...) custom-call(s32[1]{0:T(128)} %bitcast.refs_0_, ...), custom_call_target="tpu_custom_call" | custom-call | flops 5637144576 | bytes 44040192 | tf_op jit(solution)/shard_map/backward/pallas_call | solution.py:611
  92.4 2.7 %collective-permute-start.6 = (bf16[16,4608]{1,0:T(8,128)(2,1)}, bf16[16,4608]{1,0:T(8,128)(2,1)S(1)}, u32[]{:S(2)}, u32[]{:S(2)}) collective-permute-start(bf16[16,4608]{1,0:T(8,128)(2,1)} %get-tuple-element.45), channel_id=1, source_target_pairs={{0,16},{4,20},{8,24},{12,28},{16,0},{20,4},{24,8},{28,12},{1,17},{... | collective-permute-start | bytes 442376 | tf_op jit(solution)/shard_map/ppermute | solution.py:661
  95.1 1.5 %collective-permute-start.7 = (bf16[16,4608]{1,0:T(8,128)(2,1)}, bf16[16,4608]{1,0:T(8,128)(2,1)S(1)}, u32[]{:S(2)}, u32[]{:S(2)}) collective-permute-start(bf16[16,4608]{1,0:T(8,128)(2,1)} %get-tuple-element.46), channel_id=1, source_target_pairs={{0,8},{4,12},{8,0},{12,4},{16,24},{20,28},{24,16},{28,20},{1,9},{5... | collective-permute-start | bytes 442376 | tf_op jit(solution)/shard_map/ppermute | solution.py:661
  96.8 1.6 %collective-permute-start.9 = (bf16[16,4608]{1,0:T(8,128)(2,1)}, bf16[16,4608]{1,0:T(8,128)(2,1)S(1)}, u32[]{:S(2)}, u32[]{:S(2)}) collective-permute-start(bf16[16,4608]{1,0:T(8,128)(2,1)} %get-tuple-element.48), channel_id=1, source_target_pairs={{0,4},{4,0},{8,12},{12,8},{16,20},{20,16},{24,28},{28,24},{1,5},{5... | collective-permute-start | bytes 442376 | tf_op jit(solution)/shard_map/ppermute | solution.py:661
  98.4 1.6 %collective-permute-start.10 = (bf16[16,4608]{1,0:T(8,128)(2,1)}, bf16[16,4608]{1,0:T(8,128)(2,1)S(1)}, u32[]{:S(2)}, u32[]{:S(2)}) collective-permute-start(bf16[16,4608]{1,0:T(8,128)(2,1)} %get-tuple-element.49), channel_id=1, source_target_pairs={{0,20},{4,16},{8,28},{12,24},{16,4},{20,0},{24,12},{28,8},{1,21},{... | collective-permute-start | bytes 442376 | tf_op jit(solution)/shard_map/ppermute | solution.py:661
  100.0 3.7 %collective-permute-done.6.refs_2_ = bf16[16,4608]{1,0:T(8,128)(2,1)S(1)} collective-permute-done((bf16[16,4608]{1,0:T(8,128)(2,1)}, bf16[16,4608]{1,0:T(8,128)(2,1)S(1)}, u32[]{:S(2)}, u32[]{:S(2)}) %collective-permute-start.6) | collective-permute-done | bytes 147488 | tf_op jit(solution)/shard_map/ppermute | solution.py:661
  105.0 3.0 %collective-permute-start.12 = (bf16[16,4608]{1,0:T(8,128)(2,1)}, bf16[16,4608]{1,0:T(8,128)(2,1)S(1)}, u32[]{:S(2)}, u32[]{:S(2)}) collective-permute-start(bf16[16,4608]{1,0:T(8,128)(2,1)} %get-tuple-element.51), channel_id=1, source_target_pairs={{0,28},{4,24},{8,20},{12,16},{16,12},{20,8},{24,4},{28,0},{1,29},{... | collective-permute-start | bytes 442376 | tf_op jit(solution)/shard_map/ppermute | solution.py:661
  108.0 16.7 %weight_grads.1 = (bf16[4096,1792]{1,0:T(8,128)(2,1)}, bf16[4096,1792]{1,0:T(8,128)(2,1)}, bf16[1792,4096]{1,0:T(8,128)(2,1)}) custom-call(bf16[128,4096]{1,0:T(8,128)(2,1)} %get-tuple-element.54.normed_ref, bf16[128,1792]{1,0:T(8,128)(2,1)} %get-tuple-element.55.d_gate_ref, bf16[128,1792]{1,0:T(8,128)(2,1)} %get-tuple-element.56.d_up_ref, ...), custom_call_target="tpu_custom_call" | custom-call | flops 5637144576 | bytes 44040192 | tf_op jit(solution)/shard_map/weight_grads/pallas_call | solution.py:664
  (40 shorter events, 10.5 us)
Async XLA Ops:
  0.6 12.5 %collective-permute-start = (bf16[16,4096]{1,0:T(8,128)(2,1)}, bf16[16,4096]{1,0:T(8,128)(2,1)S(1)}, u32[]{:S(2)}, u32[]{:S(2)}) collective-permute-start(bf16[16,4096]{1,0:T(8,128)(2,1)} %bitcast.13), channel_id=1, source_target_pairs={{0,16},{4,20},{8,24},{12,28},{16,0},{20,4},{24,8},{28,12},{1,17},{... | collective-permute-start | bytes 393224 | tf_op jit(solution)/shard_map/ppermute | solution.py:531
  6.6 17.0 %all-to-all-start = ((bf16[32,32,128]{2,1,0:T(8,128)(2,1)}), bf16[32,32,128]{2,1,0:T(8,128)(2,1)S(1)}, u32[]{:S(2)}, u32[]{:S(2)}) async-start(bf16[32,32,128]{2,1,0:T(8,128)(2,1)} %pack_rows.1), calls=%async_computation | async-start | bytes 524288 | tf_op jit(solution)/shard_map/all_to_all | solution.py:539
  10.4 17.0 %collective-permute-start.3 = (bf16[16,4096]{1,0:T(8,128)(2,1)}, bf16[16,4096]{1,0:T(8,128)(2,1)S(1)}, u32[]{:S(2)}, u32[]{:S(2)}) collective-permute-start(bf16[16,4096]{1,0:T(8,128)(2,1)} %bitcast.23), channel_id=1, source_target_pairs={{0,16},{4,20},{8,24},{12,28},{16,0},{20,4},{24,8},{28,12},{1,17},{... | collective-permute-start | bytes 393224 | tf_op jit(solution)/shard_map/ppermute | solution.py:534
  14.1 16.1 %collective-permute-start.1 = (bf16[32,4096]{1,0:T(8,128)(2,1)S(1)}, bf16[32,4096]{1,0:T(8,128)(2,1)S(1)}, u32[]{:S(2)}, u32[]{:S(2)}) collective-permute-start(bf16[32,4096]{1,0:T(8,128)(2,1)S(1)} %pad_maximum_fusion.2), channel_id=1, source_target_pairs={{0,8},{4,12},{8,0},{12,4},{16,24},{20,28},{24,16},{28,20},{1,9},{5... | collective-permute-start | bytes 786440 | tf_op jit(solution)/shard_map/ppermute | solution.py:531
  24.5 13.3 %all-to-all-start.1 = ((f32[32,8,256]{2,1,0:T(8,128)}), f32[32,8,256]{2,1,0:T(8,128)S(1)}, u32[]{:S(2)}, u32[]{:S(2)}) async-start(f32[32,8,256]{2,1,0:T(8,128)} %get-tuple-element.35), calls=%async_computation.1 | async-start | bytes 524288 | tf_op jit(solution)/shard_map/all_to_all | solution.py:553
  28.3 13.8 %collective-permute-start.4 = (bf16[32,4096]{1,0:T(8,128)(2,1)S(1)}, bf16[32,4096]{1,0:T(8,128)(2,1)S(1)}, u32[]{:S(2)}, u32[]{:S(2)}) collective-permute-start(bf16[32,4096]{1,0:T(8,128)(2,1)S(1)} %pad_maximum_fusion.3), channel_id=1, source_target_pairs={{0,8},{4,12},{8,0},{12,4},{16,24},{20,28},{24,16},{28,20},{1,9},{5... | collective-permute-start | bytes 786440 | tf_op jit(solution)/shard_map/ppermute | solution.py:534
  31.1 25.2 %copy-start.5 = (bf16[64,4096]{1,0:T(8,128)(2,1)}, bf16[64,4096]{1,0:T(8,128)(2,1)S(1)}, u32[]{:S(2)}) copy-start(bf16[64,4096]{1,0:T(8,128)(2,1)S(1)} %pad_maximum_fusion.near_hbm.refs_4_) | copy-start | bytes 1572868
  31.1 15.4 %collective-permute-start.2 = (bf16[64,4096]{1,0:T(8,128)(2,1)S(1)}, bf16[64,4096]{1,0:T(8,128)(2,1)S(1)}, u32[]{:S(2)}, u32[]{:S(2)}) collective-permute-start(bf16[64,4096]{1,0:T(8,128)(2,1)S(1)} %pad_maximum_fusion.near_hbm.refs_4_), channel_id=1, source_target_pairs={{0,4},{4,0},{8,12},{12,8},{16,20},{20,16},{24,28},{28,24},{1,5},{5... | collective-permute-start | bytes 1572872 | tf_op jit(solution)/shard_map/ppermute | solution.py:531
  39.5 13.2 %all-to-all-start.2 = ((bf16[32,16,256]{2,1,0:T(8,128)(2,1)}), bf16[32,16,256]{2,1,0:T(8,128)(2,1)S(1)}, u32[]{:S(2)}, u32[]{:S(2)}) async-start(bf16[32,16,256]{2,1,0:T(8,128)(2,1)} %softmax_rows.1), calls=%async_computation.2 | async-start | bytes 524288 | tf_op jit(solution)/shard_map/all_to_all | solution.py:563
  43.1 26.6 %copy-start.7 = (bf16[64,4096]{1,0:T(8,128)(2,1)}, bf16[64,4096]{1,0:T(8,128)(2,1)S(1)}, u32[]{:S(2)}) copy-start(bf16[64,4096]{1,0:T(8,128)(2,1)S(1)} %pad_maximum_fusion.1.refs_6_) | copy-start | bytes 1572868
  46.5 9.8 %copy-start.6 = (bf16[64,4096]{1,0:T(8,128)(2,1)}, bf16[64,4096]{1,0:T(8,128)(2,1)S(1)}, u32[]{:S(2)}) copy-start(bf16[64,4096]{1,0:T(8,128)(2,1)S(1)} %collective-permute-done.2.far_hbm.refs_5_) | copy-start | bytes 1572868
  46.5 23.1 %collective-permute-start.5 = (bf16[64,4096]{1,0:T(8,128)(2,1)S(1)}, bf16[64,4096]{1,0:T(8,128)(2,1)}, u32[]{:S(2)}, u32[]{:S(2)}) collective-permute-start(bf16[64,4096]{1,0:T(8,128)(2,1)S(1)} %pad_maximum_fusion.1.refs_6_), channel_id=1, source_target_pairs={{0,4},{4,0},{8,12},{12,8},{16,20},{20,16},{24,28},{28,24},{1,5},{5... | collective-permute-start | bytes 1572872 | tf_op jit(solution)/shard_map/ppermute | solution.py:534
  53.7 15.9 %all-to-all-start.3 = ((bf16[32,32,128]{2,1,0:T(8,128)(2,1)}), bf16[32,32,128]{2,1,0:T(8,128)(2,1)S(1)}, u32[]{:S(2)}, u32[]{:S(2)}) async-start(bf16[32,32,128]{2,1,0:T(8,128)(2,1)} %pair_grads.1), calls=%async_computation.3 | async-start | bytes 524288 | tf_op jit(solution)/shard_map/all_to_all | solution.py:573
  92.3 32.4 %copy-start = (bf16[1,16,4096]{2,1,0:T(8,128)(2,1)S(1)}, bf16[1,16,4096]{2,1,0:T(8,128)(2,1)}, u32[]{:S(2)}) copy-start(bf16[1,16,4096]{2,1,0:T(8,128)(2,1)} %param.14) | copy-start | bytes 393220
  92.3 32.4 %copy-start.1 = (bf16[16,4608]{1,0:T(8,128)(2,1)S(1)}, bf16[16,4608]{1,0:T(8,128)(2,1)}, u32[]{:S(2)}) copy-start(bf16[16,4608]{1,0:T(8,128)(2,1)} %get-tuple-element.44.refs_1_) | copy-start | bytes 442372
  92.3 32.4 %copy-start.2 = (bf16[16,4096]{1,0:T(8,128)(2,1)S(1)}, bf16[16,4096]{1,0:T(8,128)(2,1)}, u32[]{:S(2)}) copy-start(bf16[16,4096]{1,0:T(8,128)(2,1)} %get-tuple-element.52.refs_10_) | copy-start | bytes 393220
  92.3 32.4 %copy-start.3 = (f32[1,4096]{1,0:T(1,128)S(1)}, f32[1,4096]{1,0:T(1,128)}, u32[]{:S(2)}) copy-start(f32[1,4096]{1,0:T(1,128)} %refs_11_.1) | copy-start | bytes 49156
  92.4 11.4 %collective-permute-start.6 = (bf16[16,4608]{1,0:T(8,128)(2,1)}, bf16[16,4608]{1,0:T(8,128)(2,1)S(1)}, u32[]{:S(2)}, u32[]{:S(2)}) collective-permute-start(bf16[16,4608]{1,0:T(8,128)(2,1)} %get-tuple-element.45), channel_id=1, source_target_pairs={{0,16},{4,20},{8,24},{12,28},{16,0},{20,4},{24,8},{28,12},{1,17},{... | collective-permute-start | bytes 442376 | tf_op jit(solution)/shard_map/ppermute | solution.py:661
  95.1 9.9 %collective-permute-start.7 = (bf16[16,4608]{1,0:T(8,128)(2,1)}, bf16[16,4608]{1,0:T(8,128)(2,1)S(1)}, u32[]{:S(2)}, u32[]{:S(2)}) collective-permute-start(bf16[16,4608]{1,0:T(8,128)(2,1)} %get-tuple-element.46), channel_id=1, source_target_pairs={{0,8},{4,12},{8,0},{12,4},{16,24},{20,28},{24,16},{28,20},{1,9},{5... | collective-permute-start | bytes 442376 | tf_op jit(solution)/shard_map/ppermute | solution.py:661
  96.6 28.1 %collective-permute-start.8 = (bf16[16,4608]{1,0:T(8,128)(2,1)}, bf16[16,4608]{1,0:T(8,128)(2,1)S(1)}, u32[]{:S(2)}, u32[]{:S(2)}) collective-permute-start(bf16[16,4608]{1,0:T(8,128)(2,1)} %get-tuple-element.47), channel_id=1, source_target_pairs={{0,24},{4,28},{8,16},{12,20},{16,8},{20,12},{24,0},{28,4},{1,25},{... | collective-permute-start | bytes 442376 | tf_op jit(solution)/shard_map/ppermute | solution.py:661
  96.8 27.9 %collective-permute-start.9 = (bf16[16,4608]{1,0:T(8,128)(2,1)}, bf16[16,4608]{1,0:T(8,128)(2,1)S(1)}, u32[]{:S(2)}, u32[]{:S(2)}) collective-permute-start(bf16[16,4608]{1,0:T(8,128)(2,1)} %get-tuple-element.48), channel_id=1, source_target_pairs={{0,4},{4,0},{8,12},{12,8},{16,20},{20,16},{24,28},{28,24},{1,5},{5... | collective-permute-start | bytes 442376 | tf_op jit(solution)/shard_map/ppermute | solution.py:661
  98.4 26.2 %collective-permute-start.10 = (bf16[16,4608]{1,0:T(8,128)(2,1)}, bf16[16,4608]{1,0:T(8,128)(2,1)S(1)}, u32[]{:S(2)}, u32[]{:S(2)}) collective-permute-start(bf16[16,4608]{1,0:T(8,128)(2,1)} %get-tuple-element.49), channel_id=1, source_target_pairs={{0,20},{4,16},{8,28},{12,24},{16,4},{20,0},{24,12},{28,8},{1,21},{... | collective-permute-start | bytes 442376 | tf_op jit(solution)/shard_map/ppermute | solution.py:661
  103.8 20.9 %collective-permute-start.11 = (bf16[16,4608]{1,0:T(8,128)(2,1)}, bf16[16,4608]{1,0:T(8,128)(2,1)S(1)}, u32[]{:S(2)}, u32[]{:S(2)}) collective-permute-start(bf16[16,4608]{1,0:T(8,128)(2,1)} %get-tuple-element.50), channel_id=1, source_target_pairs={{0,12},{4,8},{8,4},{12,0},{16,28},{20,24},{24,20},{28,16},{1,13},{... | collective-permute-start | bytes 442376 | tf_op jit(solution)/shard_map/ppermute | solution.py:661
  105.0 19.7 %collective-permute-start.12 = (bf16[16,4608]{1,0:T(8,128)(2,1)}, bf16[16,4608]{1,0:T(8,128)(2,1)S(1)}, u32[]{:S(2)}, u32[]{:S(2)}) collective-permute-start(bf16[16,4608]{1,0:T(8,128)(2,1)} %get-tuple-element.51), channel_id=1, source_target_pairs={{0,28},{4,24},{8,20},{12,16},{16,12},{20,8},{24,4},{28,0},{1,29},{... | collective-permute-start | bytes 442376 | tf_op jit(solution)/shard_map/ppermute | solution.py:661
  (2 other events, 1.4 us)

commit v6 on v5

--- a/solution.py
+++ b/solution.py
@@ -334,7 +334,8 @@
     cot_own_out,
     *more,
 ):
-    *delta_outs, gate_w, up_w, down_w, d_up_t, d_gate_t, x_s, gain_s, inverse_s = more[:-3]
+    *by_mask, gate_w, up_w, down_w, d_up_t, d_gate_t, x_s, gain_s, inverse_s = more[:-3]
+    delta_outs = [by_mask[mask] for mask in order]
     gate_sem, up_sem, down_sem = more[-3:]
     tokens, width = cot_out.shape
     units = gate_ref.shape[1]
@@ -402,10 +403,12 @@
         def _():
             down_ring.copy(ahead).start()
 
-        @pl.when(jnp.logical_and(ahead >= deep_cuts, ahead - deep_cuts < early))
+        late = c - (deep_cuts - early)
+
+        @pl.when(late >= 0)
         def _():
-            gate_ring.copy(ahead - deep_cuts).start()
-            up_ring.copy(ahead - deep_cuts).start()
+            gate_ring.copy(late).start()
+            up_ring.copy(late).start()
 
         return carry
 
@@ -441,14 +444,14 @@
     ).astype(BF16)
 
 
-def finish(order, mine_ref, *refs):
+def finish(mine_ref, *refs):
     *part_refs, x_ref, cot_ref, gain_ref, input_out, gain_out, tail_s = refs
     owners = len(part_refs)
     own, width = x_ref.shape
     fold = width // own
     for k in range(owners):
         tail = part_refs[k][:, width:].astype(F32)
-        tail_s[mine_ref[0] ^ order[k]] = tail[:, :fold] + tail[:, fold:]
+        tail_s[mine_ref[0] ^ k] = tail[:, :fold] + tail[:, fold:]
     gain = tail_s[0]
     for p in range(1, owners):
         gain += tail_s[p]
@@ -493,6 +496,7 @@
     own = segment_inputs.shape[1]
     tokens = own * owners
     units = gate_weight.shape[2]
+    room = min(BIG, 45 + tokens // 16)
     section = lax.axis_index("segment")
     dp = lax.axis_index("dp")
     first_row = (lax.axis_index(everyone) * rows).astype(jnp.int32).reshape(1)
@@ -595,7 +599,7 @@
             ring,
             ring,
         ],
-        compiler_params=params(BIG),
+        compiler_params=params(room),
         cost_estimate=pl.CostEstimate(
             flops=4 * tokens * width * units,
             bytes_accessed=4 * width * units,
@@ -635,7 +639,7 @@
             ring,
             ring,
         ],
-        compiler_params=params(BIG),
+        compiler_params=params(room),
         cost_estimate=pl.CostEstimate(
             flops=6 * tokens * width * units,
             bytes_accessed=6 * width * units,
@@ -655,10 +659,11 @@
         down_weight[0],
     )
     query_grads, passage_grads, hidden, d_up, d_gate, cot, cot_rows = outs[:7]
-    deltas = list(outs[7:])
+    by_mask = list(outs[7:])
     for mask in range(1, owners):
-        j = order.index(mask)
-        deltas[j] = lax.ppermute(deltas[j], "dp", [(i, i ^ mask) for i in range(owners)])
+        by_mask[mask] = lax.ppermute(
+            by_mask[mask], "dp", [(i, i ^ mask) for i in range(owners)]
+        )
 
     step = min(512, width)
     gate_grads, up_grads, down_grads = pl.pallas_call(
@@ -692,14 +697,14 @@
     )(normed, d_gate, d_up, hidden, cot)
 
     input_grads, gain_grads = pl.pallas_call(
-        lambda *refs: finish(order, *refs),
+        finish,
         out_shape=(shape((own, width), BF16), shape((1, width), F32)),
         in_specs=[smem()] + [vmem()] * (owners + 3),
         out_specs=(vmem(), vmem()),
         scratch_shapes=[pltpu.VMEM((owners, own, width // own), F32)],
         compiler_params=params(32),
         name="finish",
-    )(mine, *deltas, x_own, cot_rows, gain)
+    )(mine, *by_mask, x_own, cot_rows, gain)
     return (
         query_grads,
         passage_grads,

time: 126 us -> 125 us (level)
  transfers between devices with their start and end apart: 17 -> 17, of which waited for: 5 -> 5; matrix products, arithmetic and copies ran while one was open for 3% -> 3% of each run, Pallas kernels for 28% -> 27%
where the time goes in v6:
time: 125 us; the launch traced here: 124 us
  Pallas kernels  56.6 us (45%)
  starting transfers between devices  37.4 us (30%)
  waiting for transfers between devices  23.6 us (19%)
  other arithmetic  3.73 us (3%)
  local copies, waits for them, and re-layouts  2.26 us (2%)
    pallas_call x1, Pallas kernels, local(): pl.pallas_call(lambda *refs: backward(order, cuts, deep_cuts, *refs), out...  21.7 us
    pallas_call x1, Pallas kernels, local(): pl.pallas_call(weight_grads, grid=(width // step,), out_shape=(shape((wid...  16.7 us
    pallas_call x1, Pallas kernels, local(): pl.pallas_call(forward, out_shape=(shape((tokens, width), BF16), shape((t...  12.4 us
    all_to_all x3, waiting for transfers between devices, local(): message = lax.all_to_all(message, everyone, 0, 0, tiled=True)  12.3 us
    ppermute x7, starting transfers between devices, local(): lax.ppermute(by_mask[mask], 'dp', [(i, i ^ mask) for i in range(owners)])  12 us
    all_to_all x3, starting transfers between devices, local(): message = lax.all_to_all(message, everyone, 0, 0, tiled=True)  9 us
    ppermute x3, starting transfers between devices, double(): x_far = lax.ppermute(x_half, 'dp', swap)  7.21 us
    ppermute x3, starting transfers between devices, double(): moved[:] = [x_far, lax.ppermute(cot_half, 'dp', swap)]  6.39 us
  transfers between devices with their start and end apart: 17, of which 5 were waited for; matrix products, arithmetic and copies ran while one was open for 3% of the time, Pallas kernels for 27%

profile of v6, /device:TPU:0, one launch (start us, length us, event | category | flops | bytes accessed | tf_op | source)
XLA Modules:
  0.0 124.5 jit_solution(16175810242393321217)
XLA Ops:
  0.6 4.1 %collective-permute-start = (bf16[16,4096]{1,0:T(8,128)(2,1)}, bf16[16,4096]{1,0:T(8,128)(2,1)S(1)}, u32[]{:S(2)}, u32[]{:S(2)}) collective-permute-start(bf16[16,4096]{1,0:T(8,128)(2,1)} %bitcast.13), channel_id=1, source_target_pairs={{0,16},{4,20},{8,24},{12,28},{16,0},{20,4},{24,8},{28,12},{1,17},{... | collective-permute-start | bytes 393224 | tf_op jit(solution)/shard_map/ppermute | solution.py:535
  4.7 1.8 %pack_rows.1 = bf16[32,32,128]{2,1,0:T(8,128)(2,1)} custom-call(bf16[8,4096]{1,0:T(8,128)(2,1)} %query_hbm.1, bf16[8,4096]{1,0:T(8,128)(2,1)} %passage_hbm.1), custom_call_target="tpu_custom_call" | custom-call | tf_op jit(solution)/shard_map/pack_rows/pallas_call | solution.py:509
  6.6 3.8 %all-to-all-start = ((bf16[32,32,128]{2,1,0:T(8,128)(2,1)}), bf16[32,32,128]{2,1,0:T(8,128)(2,1)S(1)}, u32[]{:S(2)}, u32[]{:S(2)}) async-start(bf16[32,32,128]{2,1,0:T(8,128)(2,1)} %pack_rows.1), calls=%async_computation | async-start | bytes 524288 | tf_op jit(solution)/shard_map/all_to_all | solution.py:543
  10.4 2.7 %collective-permute-start.3 = (bf16[16,4096]{1,0:T(8,128)(2,1)}, bf16[16,4096]{1,0:T(8,128)(2,1)S(1)}, u32[]{:S(2)}, u32[]{:S(2)}) collective-permute-start(bf16[16,4096]{1,0:T(8,128)(2,1)} %bitcast.23), channel_id=1, source_target_pairs={{0,16},{4,20},{8,24},{12,28},{16,0},{20,4},{24,8},{28,12},{1,17},{... | collective-permute-start | bytes 393224 | tf_op jit(solution)/shard_map/ppermute | solution.py:538
  14.1 1.6 %collective-permute-start.1 = (bf16[32,4096]{1,0:T(8,128)(2,1)S(1)}, bf16[32,4096]{1,0:T(8,128)(2,1)S(1)}, u32[]{:S(2)}, u32[]{:S(2)}) collective-permute-start(bf16[32,4096]{1,0:T(8,128)(2,1)S(1)} %pad_maximum_fusion.2), channel_id=1, source_target_pairs={{0,8},{4,12},{8,0},{12,4},{16,24},{20,28},{24,16},{28,20},{1,9},{5... | collective-permute-start | bytes 786440 | tf_op jit(solution)/shard_map/ppermute | solution.py:535
  15.6 7.9 %all-to-all-done.rows_ref = bf16[32,32,128]{2,1,0:T(8,128)(2,1)S(1)} async-done(((bf16[32,32,128]{2,1,0:T(8,128)(2,1)}), bf16[32,32,128]{2,1,0:T(8,128)(2,1)S(1)}, u32[]{:S(2)}, u32[]{:S(2)}) %all-to-all-start) | async-done | bytes 262176 | tf_op jit(solution)/shard_map/all_to_all | solution.py:543
  24.5 2.8 %all-to-all-start.1 = ((f32[32,8,256]{2,1,0:T(8,128)}), f32[32,8,256]{2,1,0:T(8,128)S(1)}, u32[]{:S(2)}, u32[]{:S(2)}) async-start(f32[32,8,256]{2,1,0:T(8,128)} %get-tuple-element.35), calls=%async_computation.1 | async-start | bytes 524288 | tf_op jit(solution)/shard_map/all_to_all | solution.py:557
  28.3 1.8 %collective-permute-start.4 = (bf16[32,4096]{1,0:T(8,128)(2,1)S(1)}, bf16[32,4096]{1,0:T(8,128)(2,1)S(1)}, u32[]{:S(2)}, u32[]{:S(2)}) collective-permute-start(bf16[32,4096]{1,0:T(8,128)(2,1)S(1)} %pad_maximum_fusion.3), channel_id=1, source_target_pairs={{0,8},{4,12},{8,0},{12,4},{16,24},{20,28},{24,16},{28,20},{1,9},{5... | collective-permute-start | bytes 786440 | tf_op jit(solution)/shard_map/ppermute | solution.py:538
  31.1 1.5 %collective-permute-start.2 = (bf16[64,4096]{1,0:T(8,128)(2,1)S(1)}, bf16[64,4096]{1,0:T(8,128)(2,1)S(1)}, u32[]{:S(2)}, u32[]{:S(2)}) collective-permute-start(bf16[64,4096]{1,0:T(8,128)(2,1)S(1)} %pad_maximum_fusion.near_hbm.refs_4_), channel_id=1, source_target_pairs={{0,4},{4,0},{8,12},{12,8},{16,20},{20,16},{24,28},{28,24},{1,5},{5... | collective-permute-start | bytes 1572872 | tf_op jit(solution)/shard_map/ppermute | solution.py:535
  32.7 5.2 %all-to-all-done.1.parts_ref = f32[32,8,256]{2,1,0:T(8,128)S(1)} async-done(((f32[32,8,256]{2,1,0:T(8,128)}), f32[32,8,256]{2,1,0:T(8,128)S(1)}, u32[]{:S(2)}, u32[]{:S(2)}) %all-to-all-start.1) | async-done | bytes 262176 | tf_op jit(solution)/shard_map/all_to_all | solution.py:557
  39.5 2.6 %all-to-all-start.2 = ((bf16[32,16,256]{2,1,0:T(8,128)(2,1)}), bf16[32,16,256]{2,1,0:T(8,128)(2,1)S(1)}, u32[]{:S(2)}, u32[]{:S(2)}) async-start(bf16[32,16,256]{2,1,0:T(8,128)(2,1)} %softmax_rows.1), calls=%async_computation.2 | async-start | bytes 524288 | tf_op jit(solution)/shard_map/all_to_all | solution.py:567
  43.1 3.5 %collective-permute-done.2.far_hbm.refs_5_ = bf16[64,4096]{1,0:T(8,128)(2,1)S(1)} collective-permute-done((bf16[64,4096]{1,0:T(8,128)(2,1)S(1)}, bf16[64,4096]{1,0:T(8,128)(2,1)S(1)}, u32[]{:S(2)}, u32[]{:S(2)}) %collective-permute-start.2) | collective-permute-done | bytes 524320 | tf_op jit(solution)/shard_map/ppermute | solution.py:535
  46.5 1.8 %collective-permute-start.5 = (bf16[64,4096]{1,0:T(8,128)(2,1)S(1)}, bf16[64,4096]{1,0:T(8,128)(2,1)S(1)}, u32[]{:S(2)}, u32[]{:S(2)}) collective-permute-start(bf16[64,4096]{1,0:T(8,128)(2,1)S(1)} %pad_maximum_fusion.1.refs_6_), channel_id=1, source_target_pairs={{0,4},{4,0},{8,12},{12,8},{16,20},{20,16},{24,28},{28,24},{1,5},{5... | collective-permute-start | bytes 1572872 | tf_op jit(solution)/shard_map/ppermute | solution.py:538
  48.3 4.4 %all-to-all-done.2.refs_0_ = bf16[32,16,256]{2,1,0:T(8,128)(2,1)S(1)} async-done(((bf16[32,16,256]{2,1,0:T(8,128)(2,1)}), bf16[32,16,256]{2,1,0:T(8,128)(2,1)S(1)}, u32[]{:S(2)}, u32[]{:S(2)}) %all-to-all-start.2) | async-done | bytes 262176 | tf_op jit(solution)/shard_map/all_to_all | solution.py:567
  53.7 2.6 %all-to-all-start.3 = ((bf16[32,32,128]{2,1,0:T(8,128)(2,1)}), bf16[32,32,128]{2,1,0:T(8,128)(2,1)S(1)}, u32[]{:S(2)}, u32[]{:S(2)}) async-start(bf16[32,32,128]{2,1,0:T(8,128)(2,1)} %pair_grads.1), calls=%async_computation.3 | async-start | bytes 524288 | tf_op jit(solution)/shard_map/all_to_all | solution.py:577
  57.1 12.4 %forward.1 = (bf16[128,4096]{1,0:T(8,128)(2,1)}, f32[128,1792]{1,0:T(8,128)}, f32[128,1792]{1,0:T(8,128)}) custom-call(bf16[64,4096]{1,0:T(8,128)(2,1)S(1)} %pad_maximum_fusion.near_hbm.refs_4_, bf16[64,4096]{1,0:T(8,128)(2,1)} %copy-done.6, f32[1,4096]{1,0:T(1,128)S(1)} %copy-done.2, bf16[4096,1792]{1,0:T(8,128)(2,1)} %bitcast.18, bf16[4096,1792]{1,0:T(8,128)(2,1)} %bitcast.20), custom_call_target="tpu_custom_call" | custom-call | flops 3758096384 | bytes 29360128 | tf_op jit(solution)/shard_map/forward/pallas_call | solution.py:585
  70.4 21.7 %backward.1 = (bf16[8,4096]{1,0:T(8,128)(2,1)}, bf16[8,4096]{1,0:T(8,128)(2,1)}, bf16[128,1792]{1,0:T(8,128)(2,1)}, bf16[128,1792]{1,0:T(8,128)(2,1)}, bf16[128,...) custom-call(s32[1]{0:T(128)} %bitcast.refs_0_, ...), custom_call_target="tpu_custom_call" | custom-call | flops 5637144576 | bytes 44040192 | tf_op jit(solution)/shard_map/backward/pallas_call | solution.py:615
  92.1 1.7 %collective-permute-start.6 = (bf16[16,4608]{1,0:T(8,128)(2,1)S(1)}, bf16[16,4608]{1,0:T(8,128)(2,1)S(1)}, u32[]{:S(2)}, u32[]{:S(2)}) collective-permute-start(bf16[16,4608]{1,0:T(8,128)(2,1)S(1)} %get-tuple-element.45), channel_id=1, source_target_pairs={{0,4},{4,0},{8,12},{12,8},{16,20},{20,16},{24,28},{28,24},{1,5},{5... | collective-permute-start | bytes 442376 | tf_op jit(solution)/shard_map/ppermute | solution.py:664
  93.8 1.5 %collective-permute-start.7 = (bf16[16,4608]{1,0:T(8,128)(2,1)S(1)}, bf16[16,4608]{1,0:T(8,128)(2,1)S(1)}, u32[]{:S(2)}, u32[]{:S(2)}) collective-permute-start(bf16[16,4608]{1,0:T(8,128)(2,1)S(1)} %get-tuple-element.46), channel_id=1, source_target_pairs={{0,8},{4,12},{8,0},{12,4},{16,24},{20,28},{24,16},{28,20},{1,9},{5... | collective-permute-start | bytes 442376 | tf_op jit(solution)/shard_map/ppermute | solution.py:664
  95.7 2.6 %collective-permute-start.9 = (bf16[16,4608]{1,0:T(8,128)(2,1)S(1)}, bf16[16,4608]{1,0:T(8,128)(2,1)S(1)}, u32[]{:S(2)}, u32[]{:S(2)}) collective-permute-start(bf16[16,4608]{1,0:T(8,128)(2,1)S(1)} %get-tuple-element.48), channel_id=1, source_target_pairs={{0,16},{4,20},{8,24},{12,28},{16,0},{20,4},{24,8},{28,12},{1,17},{... | collective-permute-start | bytes 442376 | tf_op jit(solution)/shard_map/ppermute | solution.py:664
  98.3 1.3 %collective-permute-start.10 = (bf16[16,4608]{1,0:T(8,128)(2,1)}, bf16[16,4608]{1,0:T(8,128)(2,1)S(1)}, u32[]{:S(2)}, u32[]{:S(2)}) collective-permute-start(bf16[16,4608]{1,0:T(8,128)(2,1)} %get-tuple-element.49), channel_id=1, source_target_pairs={{0,20},{4,16},{8,28},{12,24},{16,4},{20,0},{24,12},{28,8},{1,21},{... | collective-permute-start | bytes 442376 | tf_op jit(solution)/shard_map/ppermute | solution.py:664
  99.7 3.5 %collective-permute-start.11 = (bf16[16,4608]{1,0:T(8,128)(2,1)}, bf16[16,4608]{1,0:T(8,128)(2,1)S(1)}, u32[]{:S(2)}, u32[]{:S(2)}) collective-permute-start(bf16[16,4608]{1,0:T(8,128)(2,1)} %get-tuple-element.50), channel_id=1, source_target_pairs={{0,24},{4,28},{8,16},{12,20},{16,8},{20,12},{24,0},{28,4},{1,25},{... | collective-permute-start | bytes 442376 | tf_op jit(solution)/shard_map/ppermute | solution.py:664
  103.1 2.6 %collective-permute-done.7.refs_2_ = bf16[16,4608]{1,0:T(8,128)(2,1)S(1)} collective-permute-done((bf16[16,4608]{1,0:T(8,128)(2,1)S(1)}, bf16[16,4608]{1,0:T(8,128)(2,1)S(1)}, u32[]{:S(2)}, u32[]{:S(2)}) %collective-permute-start.7) | collective-permute-done | bytes 147488 | tf_op jit(solution)/shard_map/ppermute | solution.py:664
  106.7 16.7 %weight_grads.1 = (bf16[4096,1792]{1,0:T(8,128)(2,1)}, bf16[4096,1792]{1,0:T(8,128)(2,1)}, bf16[1792,4096]{1,0:T(8,128)(2,1)}) custom-call(bf16[128,4096]{1,0:T(8,128)(2,1)} %get-tuple-element.54.normed_ref, bf16[128,1792]{1,0:T(8,128)(2,1)} %get-tuple-element.55.d_gate_ref, bf16[128,1792]{1,0:T(8,128)(2,1)} %get-tuple-element.56.d_up_ref, ...), custom_call_target="tpu_custom_call" | custom-call | flops 5637144576 | bytes 44040192 | tf_op jit(solution)/shard_map/weight_grads/pallas_call | solution.py:669
  (42 shorter events, 11.3 us)
Async XLA Ops:
  0.6 12.5 %collective-permute-start = (bf16[16,4096]{1,0:T(8,128)(2,1)}, bf16[16,4096]{1,0:T(8,128)(2,1)S(1)}, u32[]{:S(2)}, u32[]{:S(2)}) collective-permute-start(bf16[16,4096]{1,0:T(8,128)(2,1)} %bitcast.13), channel_id=1, source_target_pairs={{0,16},{4,20},{8,24},{12,28},{16,0},{20,4},{24,8},{28,12},{1,17},{... | collective-permute-start | bytes 393224 | tf_op jit(solution)/shard_map/ppermute | solution.py:535
  6.6 17.0 %all-to-all-start = ((bf16[32,32,128]{2,1,0:T(8,128)(2,1)}), bf16[32,32,128]{2,1,0:T(8,128)(2,1)S(1)}, u32[]{:S(2)}, u32[]{:S(2)}) async-start(bf16[32,32,128]{2,1,0:T(8,128)(2,1)} %pack_rows.1), calls=%async_computation | async-start | bytes 524288 | tf_op jit(solution)/shard_map/all_to_all | solution.py:543
  10.4 17.0 %collective-permute-start.3 = (bf16[16,4096]{1,0:T(8,128)(2,1)}, bf16[16,4096]{1,0:T(8,128)(2,1)S(1)}, u32[]{:S(2)}, u32[]{:S(2)}) collective-permute-start(bf16[16,4096]{1,0:T(8,128)(2,1)} %bitcast.23), channel_id=1, source_target_pairs={{0,16},{4,20},{8,24},{12,28},{16,0},{20,4},{24,8},{28,12},{1,17},{... | collective-permute-start | bytes 393224 | tf_op jit(solution)/shard_map/ppermute | solution.py:538
  14.1 16.1 %collective-permute-start.1 = (bf16[32,4096]{1,0:T(8,128)(2,1)S(1)}, bf16[32,4096]{1,0:T(8,128)(2,1)S(1)}, u32[]{:S(2)}, u32[]{:S(2)}) collective-permute-start(bf16[32,4096]{1,0:T(8,128)(2,1)S(1)} %pad_maximum_fusion.2), channel_id=1, source_target_pairs={{0,8},{4,12},{8,0},{12,4},{16,24},{20,28},{24,16},{28,20},{1,9},{5... | collective-permute-start | bytes 786440 | tf_op jit(solution)/shard_map/ppermute | solution.py:535
  24.5 13.3 %all-to-all-start.1 = ((f32[32,8,256]{2,1,0:T(8,128)}), f32[32,8,256]{2,1,0:T(8,128)S(1)}, u32[]{:S(2)}, u32[]{:S(2)}) async-start(f32[32,8,256]{2,1,0:T(8,128)} %get-tuple-element.35), calls=%async_computation.1 | async-start | bytes 524288 | tf_op jit(solution)/shard_map/all_to_all | solution.py:557
  28.3 13.8 %collective-permute-start.4 = (bf16[32,4096]{1,0:T(8,128)(2,1)S(1)}, bf16[32,4096]{1,0:T(8,128)(2,1)S(1)}, u32[]{:S(2)}, u32[]{:S(2)}) collective-permute-start(bf16[32,4096]{1,0:T(8,128)(2,1)S(1)} %pad_maximum_fusion.3), channel_id=1, source_target_pairs={{0,8},{4,12},{8,0},{12,4},{16,24},{20,28},{24,16},{28,20},{1,9},{5... | collective-permute-start | bytes 786440 | tf_op jit(solution)/shard_map/ppermute | solution.py:538
  31.1 38.4 %copy-start = (bf16[64,4096]{1,0:T(8,128)(2,1)}, bf16[64,4096]{1,0:T(8,128)(2,1)S(1)}, u32[]{:S(2)}) copy-start(bf16[64,4096]{1,0:T(8,128)(2,1)S(1)} %pad_maximum_fusion.near_hbm.refs_4_) | copy-start | bytes 1572868
  31.1 15.4 %collective-permute-start.2 = (bf16[64,4096]{1,0:T(8,128)(2,1)S(1)}, bf16[64,4096]{1,0:T(8,128)(2,1)S(1)}, u32[]{:S(2)}, u32[]{:S(2)}) collective-permute-start(bf16[64,4096]{1,0:T(8,128)(2,1)S(1)} %pad_maximum_fusion.near_hbm.refs_4_), channel_id=1, source_target_pairs={{0,4},{4,0},{8,12},{12,8},{16,20},{20,16},{24,28},{28,24},{1,5},{5... | collective-permute-start | bytes 1572872 | tf_op jit(solution)/shard_map/ppermute | solution.py:535
  39.5 13.2 %all-to-all-start.2 = ((bf16[32,16,256]{2,1,0:T(8,128)(2,1)}), bf16[32,16,256]{2,1,0:T(8,128)(2,1)S(1)}, u32[]{:S(2)}, u32[]{:S(2)}) async-start(bf16[32,16,256]{2,1,0:T(8,128)(2,1)} %softmax_rows.1), calls=%async_computation.2 | async-start | bytes 524288 | tf_op jit(solution)/shard_map/all_to_all | solution.py:567
  43.1 26.5 %copy-start.7 = (bf16[64,4096]{1,0:T(8,128)(2,1)}, bf16[64,4096]{1,0:T(8,128)(2,1)S(1)}, u32[]{:S(2)}) copy-start(bf16[64,4096]{1,0:T(8,128)(2,1)S(1)} %pad_maximum_fusion.1.refs_6_) | copy-start | bytes 1572868
  46.5 9.8 %copy-start.6 = (bf16[64,4096]{1,0:T(8,128)(2,1)}, bf16[64,4096]{1,0:T(8,128)(2,1)S(1)}, u32[]{:S(2)}) copy-start(bf16[64,4096]{1,0:T(8,128)(2,1)S(1)} %collective-permute-done.2.far_hbm.refs_5_) | copy-start | bytes 1572868
  46.5 23.0 %collective-permute-start.5 = (bf16[64,4096]{1,0:T(8,128)(2,1)S(1)}, bf16[64,4096]{1,0:T(8,128)(2,1)S(1)}, u32[]{:S(2)}, u32[]{:S(2)}) collective-permute-start(bf16[64,4096]{1,0:T(8,128)(2,1)S(1)} %pad_maximum_fusion.1.refs_6_), channel_id=1, source_target_pairs={{0,4},{4,0},{8,12},{12,8},{16,20},{20,16},{24,28},{28,24},{1,5},{5... | collective-permute-start | bytes 1572872 | tf_op jit(solution)/shard_map/ppermute | solution.py:538
  53.7 15.8 %all-to-all-start.3 = ((bf16[32,32,128]{2,1,0:T(8,128)(2,1)}), bf16[32,32,128]{2,1,0:T(8,128)(2,1)S(1)}, u32[]{:S(2)}, u32[]{:S(2)}) async-start(bf16[32,32,128]{2,1,0:T(8,128)(2,1)} %pair_grads.1), calls=%async_computation.3 | async-start | bytes 524288 | tf_op jit(solution)/shard_map/all_to_all | solution.py:577
  57.1 13.4 %copy-start.4 = (s32[8]{0:T(128)S(1)}, s32[8]{0:T(128)}, u32[]{:S(2)}) copy-start(s32[8]{0:T(128)} %refs_2_.1) | copy-start | bytes 100
  69.6 0.9 copy-start.8
  92.1 31.3 %copy-start.1 = (bf16[1,16,4096]{2,1,0:T(8,128)(2,1)S(1)}, bf16[1,16,4096]{2,1,0:T(8,128)(2,1)}, u32[]{:S(2)}) copy-start(bf16[1,16,4096]{2,1,0:T(8,128)(2,1)} %param.14) | copy-start | bytes 393220
  92.1 31.3 %copy-start.3 = (f32[1,4096]{1,0:T(1,128)S(1)}, f32[1,4096]{1,0:T(1,128)}, u32[]{:S(2)}) copy-start(f32[1,4096]{1,0:T(1,128)} %refs_10_.1) | copy-start | bytes 49156
  92.1 7.6 %collective-permute-start.6 = (bf16[16,4608]{1,0:T(8,128)(2,1)S(1)}, bf16[16,4608]{1,0:T(8,128)(2,1)S(1)}, u32[]{:S(2)}, u32[]{:S(2)}) collective-permute-start(bf16[16,4608]{1,0:T(8,128)(2,1)S(1)} %get-tuple-element.45), channel_id=1, source_target_pairs={{0,4},{4,0},{8,12},{12,8},{16,20},{20,16},{24,28},{28,24},{1,5},{5... | collective-permute-start | bytes 442376 | tf_op jit(solution)/shard_map/ppermute | solution.py:664
  93.8 11.9 %collective-permute-start.7 = (bf16[16,4608]{1,0:T(8,128)(2,1)S(1)}, bf16[16,4608]{1,0:T(8,128)(2,1)S(1)}, u32[]{:S(2)}, u32[]{:S(2)}) collective-permute-start(bf16[16,4608]{1,0:T(8,128)(2,1)S(1)} %get-tuple-element.46), channel_id=1, source_target_pairs={{0,8},{4,12},{8,0},{12,4},{16,24},{20,28},{24,16},{28,20},{1,9},{5... | collective-permute-start | bytes 442376 | tf_op jit(solution)/shard_map/ppermute | solution.py:664
  95.4 28.0 %collective-permute-start.8 = (bf16[16,4608]{1,0:T(8,128)(2,1)S(1)}, bf16[16,4608]{1,0:T(8,128)(2,1)S(1)}, u32[]{:S(2)}, u32[]{:S(2)}) collective-permute-start(bf16[16,4608]{1,0:T(8,128)(2,1)S(1)} %get-tuple-element.47), channel_id=1, source_target_pairs={{0,12},{4,8},{8,4},{12,0},{16,28},{20,24},{24,20},{28,16},{1,13},{... | collective-permute-start | bytes 442376 | tf_op jit(solution)/shard_map/ppermute | solution.py:664
  95.7 27.7 %collective-permute-start.9 = (bf16[16,4608]{1,0:T(8,128)(2,1)S(1)}, bf16[16,4608]{1,0:T(8,128)(2,1)S(1)}, u32[]{:S(2)}, u32[]{:S(2)}) collective-permute-start(bf16[16,4608]{1,0:T(8,128)(2,1)S(1)} %get-tuple-element.48), channel_id=1, source_target_pairs={{0,16},{4,20},{8,24},{12,28},{16,0},{20,4},{24,8},{28,12},{1,17},{... | collective-permute-start | bytes 442376 | tf_op jit(solution)/shard_map/ppermute | solution.py:664
  98.3 25.1 %collective-permute-start.10 = (bf16[16,4608]{1,0:T(8,128)(2,1)}, bf16[16,4608]{1,0:T(8,128)(2,1)S(1)}, u32[]{:S(2)}, u32[]{:S(2)}) collective-permute-start(bf16[16,4608]{1,0:T(8,128)(2,1)} %get-tuple-element.49), channel_id=1, source_target_pairs={{0,20},{4,16},{8,28},{12,24},{16,4},{20,0},{24,12},{28,8},{1,21},{... | collective-permute-start | bytes 442376 | tf_op jit(solution)/shard_map/ppermute | solution.py:664
  99.7 23.7 %collective-permute-start.11 = (bf16[16,4608]{1,0:T(8,128)(2,1)}, bf16[16,4608]{1,0:T(8,128)(2,1)S(1)}, u32[]{:S(2)}, u32[]{:S(2)}) collective-permute-start(bf16[16,4608]{1,0:T(8,128)(2,1)} %get-tuple-element.50), channel_id=1, source_target_pairs={{0,24},{4,28},{8,16},{12,20},{16,8},{20,12},{24,0},{28,4},{1,25},{... | collective-permute-start | bytes 442376 | tf_op jit(solution)/shard_map/ppermute | solution.py:664
  105.7 17.7 %collective-permute-start.12 = (bf16[16,4608]{1,0:T(8,128)(2,1)}, bf16[16,4608]{1,0:T(8,128)(2,1)S(1)}, u32[]{:S(2)}, u32[]{:S(2)}) collective-permute-start(bf16[16,4608]{1,0:T(8,128)(2,1)} %get-tuple-element.51), channel_id=1, source_target_pairs={{0,28},{4,24},{8,20},{12,16},{16,12},{20,8},{24,4},{28,0},{1,29},{... | collective-permute-start | bytes 442376 | tf_op jit(solution)/shard_map/ppermute | solution.py:664
  (3 other events, 2.2 us)

commit v7 on v6

--- a/solution.py
+++ b/solution.py
@@ -302,10 +302,8 @@
     gain = jnp.concatenate(
         [gain_s[:, r * fold : (r + 1) * fold] for r in range(own)], axis=0
     )
-    high, low, _ = split3(gain)
-    tail = jnp.concatenate([high, low], axis=1).astype(BF16)
     for k in range(owners):
-        outs[k][:, width:] = tail
+        outs[k][:, width:] = gain.astype(BF16)
 
 
 def backward(
@@ -450,8 +448,7 @@
     own, width = x_ref.shape
     fold = width // own
     for k in range(owners):
-        tail = part_refs[k][:, width:].astype(F32)
-        tail_s[mine_ref[0] ^ k] = tail[:, :fold] + tail[:, fold:]
+        tail_s[mine_ref[0] ^ k] = part_refs[k][:, width:].astype(F32)
     gain = tail_s[0]
     for p in range(1, owners):
         gain += tail_s[p]
@@ -610,7 +607,7 @@
 
     cuts = max(1, width // 512)
     deep_cuts = units // 256 if units % 256 == 0 else 1
-    part_shape = shape((own, width + 2 * (width // own)), BF16)
+    part_shape = shape((own, width + width // own), BF16)
     block = (WINDOW, width // cuts, units)
     outs = pl.pallas_call(
         lambda *refs: backward(order, cuts, deep_cuts, *refs),

time: 125 us -> 124 us (level)
  no operation moved by 1% of the time
where the time goes in v7:
time: 124 us
  Pallas kernels  56.6 us (46%)
  starting transfers between devices  37.2 us (30%)
  waiting for transfers between devices  23 us (19%)
  other arithmetic  3.73 us (3%)
  local copies, waits for them, and re-layouts  2.26 us (2%)
    pallas_call x1, Pallas kernels, local(): pl.pallas_call(lambda *refs: backward(order, cuts, deep_cuts, *refs), out...  21.7 us
    pallas_call x1, Pallas kernels, local(): pl.pallas_call(weight_grads, grid=(width // step,), out_shape=(shape((wid...  16.7 us
    pallas_call x1, Pallas kernels, local(): pl.pallas_call(forward, out_shape=(shape((tokens, width), BF16), shape((t...  12.4 us
    all_to_all x3, waiting for transfers between devices, local(): message = lax.all_to_all(message, everyone, 0, 0, tiled=True)  12.3 us
    ppermute x7, starting transfers between devices, local(): lax.ppermute(by_mask[mask], 'dp', [(i, i ^ mask) for i in range(owners)])  11.8 us
    all_to_all x3, starting transfers between devices, local(): message = lax.all_to_all(message, everyone, 0, 0, tiled=True)  9 us
    ppermute x3, starting transfers between devices, double(): x_far = lax.ppermute(x_half, 'dp', swap)  7.21 us
    ppermute x3, starting transfers between devices, double(): moved[:] = [x_far, lax.ppermute(cot_half, 'dp', swap)]  6.39 us
  transfers between devices with their start and end apart: 17, of which 5 were waited for; matrix products, arithmetic and copies ran while one was open for 3% of the time, Pallas kernels for 27%

profile of v7, /device:TPU:0, one launch (start us, length us, event | category | flops | bytes accessed | tf_op | source)
XLA Modules:
  0.0 123.8 jit_solution(10563732853871296063)
XLA Ops:
  0.6 4.1 %collective-permute-start = (bf16[16,4096]{1,0:T(8,128)(2,1)}, bf16[16,4096]{1,0:T(8,128)(2,1)S(1)}, u32[]{:S(2)}, u32[]{:S(2)}) collective-permute-start(bf16[16,4096]{1,0:T(8,128)(2,1)} %bitcast.13), channel_id=1, source_target_pairs={{0,16},{4,20},{8,24},{12,28},{16,0},{20,4},{24,8},{28,12},{1,17},{... | collective-permute-start | bytes 393224 | tf_op jit(solution)/shard_map/ppermute | solution.py:532
  4.7 1.8 %pack_rows.1 = bf16[32,32,128]{2,1,0:T(8,128)(2,1)} custom-call(bf16[8,4096]{1,0:T(8,128)(2,1)} %query_hbm.1, bf16[8,4096]{1,0:T(8,128)(2,1)} %passage_hbm.1), custom_call_target="tpu_custom_call" | custom-call | tf_op jit(solution)/shard_map/pack_rows/pallas_call | solution.py:506
  6.6 3.8 %all-to-all-start = ((bf16[32,32,128]{2,1,0:T(8,128)(2,1)}), bf16[32,32,128]{2,1,0:T(8,128)(2,1)S(1)}, u32[]{:S(2)}, u32[]{:S(2)}) async-start(bf16[32,32,128]{2,1,0:T(8,128)(2,1)} %pack_rows.1), calls=%async_computation | async-start | bytes 524288 | tf_op jit(solution)/shard_map/all_to_all | solution.py:540
  10.4 2.7 %collective-permute-start.3 = (bf16[16,4096]{1,0:T(8,128)(2,1)}, bf16[16,4096]{1,0:T(8,128)(2,1)S(1)}, u32[]{:S(2)}, u32[]{:S(2)}) collective-permute-start(bf16[16,4096]{1,0:T(8,128)(2,1)} %bitcast.23), channel_id=1, source_target_pairs={{0,16},{4,20},{8,24},{12,28},{16,0},{20,4},{24,8},{28,12},{1,17},{... | collective-permute-start | bytes 393224 | tf_op jit(solution)/shard_map/ppermute | solution.py:535
  14.1 1.6 %collective-permute-start.1 = (bf16[32,4096]{1,0:T(8,128)(2,1)S(1)}, bf16[32,4096]{1,0:T(8,128)(2,1)S(1)}, u32[]{:S(2)}, u32[]{:S(2)}) collective-permute-start(bf16[32,4096]{1,0:T(8,128)(2,1)S(1)} %pad_maximum_fusion.2), channel_id=1, source_target_pairs={{0,8},{4,12},{8,0},{12,4},{16,24},{20,28},{24,16},{28,20},{1,9},{5... | collective-permute-start | bytes 786440 | tf_op jit(solution)/shard_map/ppermute | solution.py:532
  15.6 7.9 %all-to-all-done.rows_ref = bf16[32,32,128]{2,1,0:T(8,128)(2,1)S(1)} async-done(((bf16[32,32,128]{2,1,0:T(8,128)(2,1)}), bf16[32,32,128]{2,1,0:T(8,128)(2,1)S(1)}, u32[]{:S(2)}, u32[]{:S(2)}) %all-to-all-start) | async-done | bytes 262176 | tf_op jit(solution)/shard_map/all_to_all | solution.py:540
  24.5 2.8 %all-to-all-start.1 = ((f32[32,8,256]{2,1,0:T(8,128)}), f32[32,8,256]{2,1,0:T(8,128)S(1)}, u32[]{:S(2)}, u32[]{:S(2)}) async-start(f32[32,8,256]{2,1,0:T(8,128)} %get-tuple-element.35), calls=%async_computation.1 | async-start | bytes 524288 | tf_op jit(solution)/shard_map/all_to_all | solution.py:554
  28.3 1.8 %collective-permute-start.4 = (bf16[32,4096]{1,0:T(8,128)(2,1)S(1)}, bf16[32,4096]{1,0:T(8,128)(2,1)S(1)}, u32[]{:S(2)}, u32[]{:S(2)}) collective-permute-start(bf16[32,4096]{1,0:T(8,128)(2,1)S(1)} %pad_maximum_fusion.3), channel_id=1, source_target_pairs={{0,8},{4,12},{8,0},{12,4},{16,24},{20,28},{24,16},{28,20},{1,9},{5... | collective-permute-start | bytes 786440 | tf_op jit(solution)/shard_map/ppermute | solution.py:535
  31.1 1.5 %collective-permute-start.2 = (bf16[64,4096]{1,0:T(8,128)(2,1)S(1)}, bf16[64,4096]{1,0:T(8,128)(2,1)S(1)}, u32[]{:S(2)}, u32[]{:S(2)}) collective-permute-start(bf16[64,4096]{1,0:T(8,128)(2,1)S(1)} %pad_maximum_fusion.near_hbm.refs_4_), channel_id=1, source_target_pairs={{0,4},{4,0},{8,12},{12,8},{16,20},{20,16},{24,28},{28,24},{1,5},{5... | collective-permute-start | bytes 1572872 | tf_op jit(solution)/shard_map/ppermute | solution.py:532
  32.7 5.2 %all-to-all-done.1.parts_ref = f32[32,8,256]{2,1,0:T(8,128)S(1)} async-done(((f32[32,8,256]{2,1,0:T(8,128)}), f32[32,8,256]{2,1,0:T(8,128)S(1)}, u32[]{:S(2)}, u32[]{:S(2)}) %all-to-all-start.1) | async-done | bytes 262176 | tf_op jit(solution)/shard_map/all_to_all | solution.py:554
  39.5 2.6 %all-to-all-start.2 = ((bf16[32,16,256]{2,1,0:T(8,128)(2,1)}), bf16[32,16,256]{2,1,0:T(8,128)(2,1)S(1)}, u32[]{:S(2)}, u32[]{:S(2)}) async-start(bf16[32,16,256]{2,1,0:T(8,128)(2,1)} %softmax_rows.1), calls=%async_computation.2 | async-start | bytes 524288 | tf_op jit(solution)/shard_map/all_to_all | solution.py:564
  43.1 3.5 %collective-permute-done.2.far_hbm.refs_5_ = bf16[64,4096]{1,0:T(8,128)(2,1)S(1)} collective-permute-done((bf16[64,4096]{1,0:T(8,128)(2,1)S(1)}, bf16[64,4096]{1,0:T(8,128)(2,1)S(1)}, u32[]{:S(2)}, u32[]{:S(2)}) %collective-permute-start.2) | collective-permute-done | bytes 524320 | tf_op jit(solution)/shard_map/ppermute | solution.py:532
  46.5 1.8 %collective-permute-start.5 = (bf16[64,4096]{1,0:T(8,128)(2,1)S(1)}, bf16[64,4096]{1,0:T(8,128)(2,1)S(1)}, u32[]{:S(2)}, u32[]{:S(2)}) collective-permute-start(bf16[64,4096]{1,0:T(8,128)(2,1)S(1)} %pad_maximum_fusion.1.refs_6_), channel_id=1, source_target_pairs={{0,4},{4,0},{8,12},{12,8},{16,20},{20,16},{24,28},{28,24},{1,5},{5... | collective-permute-start | bytes 1572872 | tf_op jit(solution)/shard_map/ppermute | solution.py:535
  48.3 4.4 %all-to-all-done.2.refs_0_ = bf16[32,16,256]{2,1,0:T(8,128)(2,1)S(1)} async-done(((bf16[32,16,256]{2,1,0:T(8,128)(2,1)}), bf16[32,16,256]{2,1,0:T(8,128)(2,1)S(1)}, u32[]{:S(2)}, u32[]{:S(2)}) %all-to-all-start.2) | async-done | bytes 262176 | tf_op jit(solution)/shard_map/all_to_all | solution.py:564
  53.7 2.6 %all-to-all-start.3 = ((bf16[32,32,128]{2,1,0:T(8,128)(2,1)}), bf16[32,32,128]{2,1,0:T(8,128)(2,1)S(1)}, u32[]{:S(2)}, u32[]{:S(2)}) async-start(bf16[32,32,128]{2,1,0:T(8,128)(2,1)} %pair_grads.1), calls=%async_computation.3 | async-start | bytes 524288 | tf_op jit(solution)/shard_map/all_to_all | solution.py:574
  57.1 12.4 %forward.1 = (bf16[128,4096]{1,0:T(8,128)(2,1)}, f32[128,1792]{1,0:T(8,128)}, f32[128,1792]{1,0:T(8,128)}) custom-call(bf16[64,4096]{1,0:T(8,128)(2,1)S(1)} %pad_maximum_fusion.near_hbm.refs_4_, bf16[64,4096]{1,0:T(8,128)(2,1)} %copy-done.6, f32[1,4096]{1,0:T(1,128)S(1)} %copy-done.2, bf16[4096,1792]{1,0:T(8,128)(2,1)} %bitcast.18, bf16[4096,1792]{1,0:T(8,128)(2,1)} %bitcast.20), custom_call_target="tpu_custom_call" | custom-call | flops 3758096384 | bytes 29360128 | tf_op jit(solution)/shard_map/forward/pallas_call | solution.py:582
  70.4 21.7 %backward.1 = (bf16[8,4096]{1,0:T(8,128)(2,1)}, bf16[8,4096]{1,0:T(8,128)(2,1)}, bf16[128,1792]{1,0:T(8,128)(2,1)}, bf16[128,1792]{1,0:T(8,128)(2,1)}, bf16[128,...) custom-call(s32[1]{0:T(128)} %bitcast.refs_0_, ...), custom_call_target="tpu_custom_call" | custom-call | flops 5637144576 | bytes 44040192 | tf_op jit(solution)/shard_map/backward/pallas_call | solution.py:612
  92.1 1.7 %collective-permute-start.6 = (bf16[16,4352]{1,0:T(8,128)(2,1)S(1)}, bf16[16,4352]{1,0:T(8,128)(2,1)S(1)}, u32[]{:S(2)}, u32[]{:S(2)}) collective-permute-start(bf16[16,4352]{1,0:T(8,128)(2,1)S(1)} %get-tuple-element.45), channel_id=1, source_target_pairs={{0,4},{4,0},{8,12},{12,8},{16,20},{20,16},{24,28},{28,24},{1,5},{5... | collective-permute-start | bytes 417800 | tf_op jit(solution)/shard_map/ppermute | solution.py:661
  93.8 1.5 %collective-permute-start.7 = (bf16[16,4352]{1,0:T(8,128)(2,1)S(1)}, bf16[16,4352]{1,0:T(8,128)(2,1)S(1)}, u32[]{:S(2)}, u32[]{:S(2)}) collective-permute-start(bf16[16,4352]{1,0:T(8,128)(2,1)S(1)} %get-tuple-element.46), channel_id=1, source_target_pairs={{0,8},{4,12},{8,0},{12,4},{16,24},{20,28},{24,16},{28,20},{1,9},{5... | collective-permute-start | bytes 417800 | tf_op jit(solution)/shard_map/ppermute | solution.py:661
  95.7 2.6 %collective-permute-start.9 = (bf16[16,4352]{1,0:T(8,128)(2,1)S(1)}, bf16[16,4352]{1,0:T(8,128)(2,1)S(1)}, u32[]{:S(2)}, u32[]{:S(2)}) collective-permute-start(bf16[16,4352]{1,0:T(8,128)(2,1)S(1)} %get-tuple-element.48), channel_id=1, source_target_pairs={{0,16},{4,20},{8,24},{12,28},{16,0},{20,4},{24,8},{28,12},{1,17},{... | collective-permute-start | bytes 417800 | tf_op jit(solution)/shard_map/ppermute | solution.py:661
  98.3 1.3 %collective-permute-start.10 = (bf16[16,4352]{1,0:T(8,128)(2,1)S(1)}, bf16[16,4352]{1,0:T(8,128)(2,1)S(1)}, u32[]{:S(2)}, u32[]{:S(2)}) collective-permute-start(bf16[16,4352]{1,0:T(8,128)(2,1)S(1)} %get-tuple-element.49), channel_id=1, source_target_pairs={{0,20},{4,16},{8,28},{12,24},{16,4},{20,0},{24,12},{28,8},{1,21},{... | collective-permute-start | bytes 417800 | tf_op jit(solution)/shard_map/ppermute | solution.py:661
  99.7 3.5 %collective-permute-start.11 = (bf16[16,4352]{1,0:T(8,128)(2,1)}, bf16[16,4352]{1,0:T(8,128)(2,1)S(1)}, u32[]{:S(2)}, u32[]{:S(2)}) collective-permute-start(bf16[16,4352]{1,0:T(8,128)(2,1)} %get-tuple-element.50), channel_id=1, source_target_pairs={{0,24},{4,28},{8,16},{12,20},{16,8},{20,12},{24,0},{28,4},{1,25},{... | collective-permute-start | bytes 417800 | tf_op jit(solution)/shard_map/ppermute | solution.py:661
  103.1 2.0 %collective-permute-done.7.refs_2_ = bf16[16,4352]{1,0:T(8,128)(2,1)S(1)} collective-permute-done((bf16[16,4352]{1,0:T(8,128)(2,1)S(1)}, bf16[16,4352]{1,0:T(8,128)(2,1)S(1)}, u32[]{:S(2)}, u32[]{:S(2)}) %collective-permute-start.7) | collective-permute-done | bytes 139296 | tf_op jit(solution)/shard_map/ppermute | solution.py:661
  106.0 16.7 %weight_grads.1 = (bf16[4096,1792]{1,0:T(8,128)(2,1)}, bf16[4096,1792]{1,0:T(8,128)(2,1)}, bf16[1792,4096]{1,0:T(8,128)(2,1)}) custom-call(bf16[128,4096]{1,0:T(8,128)(2,1)} %get-tuple-element.54.normed_ref, bf16[128,1792]{1,0:T(8,128)(2,1)} %get-tuple-element.55.d_gate_ref, bf16[128,1792]{1,0:T(8,128)(2,1)} %get-tuple-element.56.d_up_ref, ...), custom_call_target="tpu_custom_call" | custom-call | flops 5637144576 | bytes 44040192 | tf_op jit(solution)/shard_map/weight_grads/pallas_call | solution.py:666
  (42 shorter events, 11.1 us)
Async XLA Ops:
  0.6 12.5 %collective-permute-start = (bf16[16,4096]{1,0:T(8,128)(2,1)}, bf16[16,4096]{1,0:T(8,128)(2,1)S(1)}, u32[]{:S(2)}, u32[]{:S(2)}) collective-permute-start(bf16[16,4096]{1,0:T(8,128)(2,1)} %bitcast.13), channel_id=1, source_target_pairs={{0,16},{4,20},{8,24},{12,28},{16,0},{20,4},{24,8},{28,12},{1,17},{... | collective-permute-start | bytes 393224 | tf_op jit(solution)/shard_map/ppermute | solution.py:532
  6.6 17.0 %all-to-all-start = ((bf16[32,32,128]{2,1,0:T(8,128)(2,1)}), bf16[32,32,128]{2,1,0:T(8,128)(2,1)S(1)}, u32[]{:S(2)}, u32[]{:S(2)}) async-start(bf16[32,32,128]{2,1,0:T(8,128)(2,1)} %pack_rows.1), calls=%async_computation | async-start | bytes 524288 | tf_op jit(solution)/shard_map/all_to_all | solution.py:540
  10.4 17.0 %collective-permute-start.3 = (bf16[16,4096]{1,0:T(8,128)(2,1)}, bf16[16,4096]{1,0:T(8,128)(2,1)S(1)}, u32[]{:S(2)}, u32[]{:S(2)}) collective-permute-start(bf16[16,4096]{1,0:T(8,128)(2,1)} %bitcast.23), channel_id=1, source_target_pairs={{0,16},{4,20},{8,24},{12,28},{16,0},{20,4},{24,8},{28,12},{1,17},{... | collective-permute-start | bytes 393224 | tf_op jit(solution)/shard_map/ppermute | solution.py:535
  14.1 16.1 %collective-permute-start.1 = (bf16[32,4096]{1,0:T(8,128)(2,1)S(1)}, bf16[32,4096]{1,0:T(8,128)(2,1)S(1)}, u32[]{:S(2)}, u32[]{:S(2)}) collective-permute-start(bf16[32,4096]{1,0:T(8,128)(2,1)S(1)} %pad_maximum_fusion.2), channel_id=1, source_target_pairs={{0,8},{4,12},{8,0},{12,4},{16,24},{20,28},{24,16},{28,20},{1,9},{5... | collective-permute-start | bytes 786440 | tf_op jit(solution)/shard_map/ppermute | solution.py:532
  24.5 13.3 %all-to-all-start.1 = ((f32[32,8,256]{2,1,0:T(8,128)}), f32[32,8,256]{2,1,0:T(8,128)S(1)}, u32[]{:S(2)}, u32[]{:S(2)}) async-start(f32[32,8,256]{2,1,0:T(8,128)} %get-tuple-element.35), calls=%async_computation.1 | async-start | bytes 524288 | tf_op jit(solution)/shard_map/all_to_all | solution.py:554
  28.3 13.8 %collective-permute-start.4 = (bf16[32,4096]{1,0:T(8,128)(2,1)S(1)}, bf16[32,4096]{1,0:T(8,128)(2,1)S(1)}, u32[]{:S(2)}, u32[]{:S(2)}) collective-permute-start(bf16[32,4096]{1,0:T(8,128)(2,1)S(1)} %pad_maximum_fusion.3), channel_id=1, source_target_pairs={{0,8},{4,12},{8,0},{12,4},{16,24},{20,28},{24,16},{28,20},{1,9},{5... | collective-permute-start | bytes 786440 | tf_op jit(solution)/shard_map/ppermute | solution.py:535
  31.1 38.4 %copy-start = (bf16[64,4096]{1,0:T(8,128)(2,1)}, bf16[64,4096]{1,0:T(8,128)(2,1)S(1)}, u32[]{:S(2)}) copy-start(bf16[64,4096]{1,0:T(8,128)(2,1)S(1)} %pad_maximum_fusion.near_hbm.refs_4_) | copy-start | bytes 1572868
  31.1 15.4 %collective-permute-start.2 = (bf16[64,4096]{1,0:T(8,128)(2,1)S(1)}, bf16[64,4096]{1,0:T(8,128)(2,1)S(1)}, u32[]{:S(2)}, u32[]{:S(2)}) collective-permute-start(bf16[64,4096]{1,0:T(8,128)(2,1)S(1)} %pad_maximum_fusion.near_hbm.refs_4_), channel_id=1, source_target_pairs={{0,4},{4,0},{8,12},{12,8},{16,20},{20,16},{24,28},{28,24},{1,5},{5... | collective-permute-start | bytes 1572872 | tf_op jit(solution)/shard_map/ppermute | solution.py:532
  39.5 13.2 %all-to-all-start.2 = ((bf16[32,16,256]{2,1,0:T(8,128)(2,1)}), bf16[32,16,256]{2,1,0:T(8,128)(2,1)S(1)}, u32[]{:S(2)}, u32[]{:S(2)}) async-start(bf16[32,16,256]{2,1,0:T(8,128)(2,1)} %softmax_rows.1), calls=%async_computation.2 | async-start | bytes 524288 | tf_op jit(solution)/shard_map/all_to_all | solution.py:564
  43.1 26.5 %copy-start.7 = (bf16[64,4096]{1,0:T(8,128)(2,1)}, bf16[64,4096]{1,0:T(8,128)(2,1)S(1)}, u32[]{:S(2)}) copy-start(bf16[64,4096]{1,0:T(8,128)(2,1)S(1)} %pad_maximum_fusion.1.refs_6_) | copy-start | bytes 1572868
  46.5 9.8 %copy-start.6 = (bf16[64,4096]{1,0:T(8,128)(2,1)}, bf16[64,4096]{1,0:T(8,128)(2,1)S(1)}, u32[]{:S(2)}) copy-start(bf16[64,4096]{1,0:T(8,128)(2,1)S(1)} %collective-permute-done.2.far_hbm.refs_5_) | copy-start | bytes 1572868
  46.5 23.0 %collective-permute-start.5 = (bf16[64,4096]{1,0:T(8,128)(2,1)S(1)}, bf16[64,4096]{1,0:T(8,128)(2,1)S(1)}, u32[]{:S(2)}, u32[]{:S(2)}) collective-permute-start(bf16[64,4096]{1,0:T(8,128)(2,1)S(1)} %pad_maximum_fusion.1.refs_6_), channel_id=1, source_target_pairs={{0,4},{4,0},{8,12},{12,8},{16,20},{20,16},{24,28},{28,24},{1,5},{5... | collective-permute-start | bytes 1572872 | tf_op jit(solution)/shard_map/ppermute | solution.py:535
  53.7 15.8 %all-to-all-start.3 = ((bf16[32,32,128]{2,1,0:T(8,128)(2,1)}), bf16[32,32,128]{2,1,0:T(8,128)(2,1)S(1)}, u32[]{:S(2)}, u32[]{:S(2)}) async-start(bf16[32,32,128]{2,1,0:T(8,128)(2,1)} %pair_grads.1), calls=%async_computation.3 | async-start | bytes 524288 | tf_op jit(solution)/shard_map/all_to_all | solution.py:574
  57.1 13.4 %copy-start.4 = (s32[8]{0:T(128)S(1)}, s32[8]{0:T(128)}, u32[]{:S(2)}) copy-start(s32[8]{0:T(128)} %refs_2_.1) | copy-start | bytes 100
  69.6 0.9 copy-start.8
  92.1 30.6 %copy-start.1 = (bf16[1,16,4096]{2,1,0:T(8,128)(2,1)S(1)}, bf16[1,16,4096]{2,1,0:T(8,128)(2,1)}, u32[]{:S(2)}) copy-start(bf16[1,16,4096]{2,1,0:T(8,128)(2,1)} %param.14) | copy-start | bytes 393220
  92.1 30.6 %copy-start.3 = (f32[1,4096]{1,0:T(1,128)S(1)}, f32[1,4096]{1,0:T(1,128)}, u32[]{:S(2)}) copy-start(f32[1,4096]{1,0:T(1,128)} %refs_10_.1) | copy-start | bytes 49156
  92.1 7.6 %collective-permute-start.6 = (bf16[16,4352]{1,0:T(8,128)(2,1)S(1)}, bf16[16,4352]{1,0:T(8,128)(2,1)S(1)}, u32[]{:S(2)}, u32[]{:S(2)}) collective-permute-start(bf16[16,4352]{1,0:T(8,128)(2,1)S(1)} %get-tuple-element.45), channel_id=1, source_target_pairs={{0,4},{4,0},{8,12},{12,8},{16,20},{20,16},{24,28},{28,24},{1,5},{5... | collective-permute-start | bytes 417800 | tf_op jit(solution)/shard_map/ppermute | solution.py:661
  93.8 11.4 %collective-permute-start.7 = (bf16[16,4352]{1,0:T(8,128)(2,1)S(1)}, bf16[16,4352]{1,0:T(8,128)(2,1)S(1)}, u32[]{:S(2)}, u32[]{:S(2)}) collective-permute-start(bf16[16,4352]{1,0:T(8,128)(2,1)S(1)} %get-tuple-element.46), channel_id=1, source_target_pairs={{0,8},{4,12},{8,0},{12,4},{16,24},{20,28},{24,16},{28,20},{1,9},{5... | collective-permute-start | bytes 417800 | tf_op jit(solution)/shard_map/ppermute | solution.py:661
  95.3 27.3 %collective-permute-start.8 = (bf16[16,4352]{1,0:T(8,128)(2,1)S(1)}, bf16[16,4352]{1,0:T(8,128)(2,1)S(1)}, u32[]{:S(2)}, u32[]{:S(2)}) collective-permute-start(bf16[16,4352]{1,0:T(8,128)(2,1)S(1)} %get-tuple-element.47), channel_id=1, source_target_pairs={{0,12},{4,8},{8,4},{12,0},{16,28},{20,24},{24,20},{28,16},{1,13},{... | collective-permute-start | bytes 417800 | tf_op jit(solution)/shard_map/ppermute | solution.py:661
  95.7 27.0 %collective-permute-start.9 = (bf16[16,4352]{1,0:T(8,128)(2,1)S(1)}, bf16[16,4352]{1,0:T(8,128)(2,1)S(1)}, u32[]{:S(2)}, u32[]{:S(2)}) collective-permute-start(bf16[16,4352]{1,0:T(8,128)(2,1)S(1)} %get-tuple-element.48), channel_id=1, source_target_pairs={{0,16},{4,20},{8,24},{12,28},{16,0},{20,4},{24,8},{28,12},{1,17},{... | collective-permute-start | bytes 417800 | tf_op jit(solution)/shard_map/ppermute | solution.py:661
  98.3 24.4 %collective-permute-start.10 = (bf16[16,4352]{1,0:T(8,128)(2,1)S(1)}, bf16[16,4352]{1,0:T(8,128)(2,1)S(1)}, u32[]{:S(2)}, u32[]{:S(2)}) collective-permute-start(bf16[16,4352]{1,0:T(8,128)(2,1)S(1)} %get-tuple-element.49), channel_id=1, source_target_pairs={{0,20},{4,16},{8,28},{12,24},{16,4},{20,0},{24,12},{28,8},{1,21},{... | collective-permute-start | bytes 417800 | tf_op jit(solution)/shard_map/ppermute | solution.py:661
  99.7 23.0 %collective-permute-start.11 = (bf16[16,4352]{1,0:T(8,128)(2,1)}, bf16[16,4352]{1,0:T(8,128)(2,1)S(1)}, u32[]{:S(2)}, u32[]{:S(2)}) collective-permute-start(bf16[16,4352]{1,0:T(8,128)(2,1)} %get-tuple-element.50), channel_id=1, source_target_pairs={{0,24},{4,28},{8,16},{12,20},{16,8},{20,12},{24,0},{28,4},{1,25},{... | collective-permute-start | bytes 417800 | tf_op jit(solution)/shard_map/ppermute | solution.py:661
  105.2 17.5 %collective-permute-start.12 = (bf16[16,4352]{1,0:T(8,128)(2,1)}, bf16[16,4352]{1,0:T(8,128)(2,1)S(1)}, u32[]{:S(2)}, u32[]{:S(2)}) collective-permute-start(bf16[16,4352]{1,0:T(8,128)(2,1)} %get-tuple-element.51), channel_id=1, source_target_pairs={{0,28},{4,24},{8,20},{12,16},{16,12},{20,8},{24,4},{28,0},{1,29},{... | collective-permute-start | bytes 417800 | tf_op jit(solution)/shard_map/ppermute | solution.py:661
  (3 other events, 2.2 us)

commit v8 on v7

--- a/solution.py
+++ b/solution.py
@@ -196,7 +196,7 @@
         self.hbm, self.slots, self.sems, self.step = hbm, slots, sems, step
 
     def copy(self, c):
-        slot = lax.rem(c, WINDOW)
+        slot = lax.rem(c, self.slots.shape[0])
         part = pl.ds(c * self.step, self.step)
         return pltpu.make_async_copy(self.hbm.at[part], self.slots.at[slot], self.sems.at[slot])
 
@@ -220,6 +220,7 @@
     tokens, width = normed_out.shape
     step = gate_w.shape[1]
     blocks = width // step
+    window = gate_w.shape[0]
     gate_ring = Ring(gate_hbm, gate_w, gate_sem, step)
     up_ring = Ring(up_hbm, up_w, up_sem, step)
     half = tokens // 2
@@ -229,7 +230,7 @@
     ]
     for fetch in fetches:
         fetch.start()
-    for c in range(min(WINDOW, blocks)):
+    for c in range(min(window, blocks)):
         gate_ring.copy(c).start()
         up_ring.copy(c).start()
     for fetch in fetches:
@@ -239,7 +240,7 @@
     normed_out[...] = (x * inverse * gain_ref[...]).astype(BF16)
 
     def block(c, first):
-        slot = lax.rem(c, WINDOW)
+        slot = lax.rem(c, window)
         cut = pl.ds(pl.multiple_of(c * step, step), step)
         normed = normed_out[:, cut]
         gate_ring.copy(c).wait()
@@ -249,10 +250,10 @@
         up = jnp.dot(normed, up_w[slot], preferred_element_type=F32)
         up_out[...] = up if first else up_out[...] + up
 
-        @pl.when(c + WINDOW < blocks)
+        @pl.when(c + window < blocks)
         def _():
-            gate_ring.copy(c + WINDOW).start()
-            up_ring.copy(c + WINDOW).start()
+            gate_ring.copy(c + window).start()
+            up_ring.copy(c + window).start()
 
     def more(c, carry):
         block(c, False)
@@ -578,7 +579,7 @@
     halves = (x_half, moved[0], cot_half, moved[1])
     whole = lambda dims: pl.BlockSpec(dims, lambda i: (0,) * len(dims))
     ring = pltpu.SemaphoreType.DMA((WINDOW,))
-    step = min(512, width)
+    step = min(1024, width)
     normed, gate, up = pl.pallas_call(
         forward,
         out_shape=(
@@ -590,11 +591,11 @@
         out_specs=(vmem(), vmem(), vmem()),
         scratch_shapes=[
             pltpu.VMEM((tokens, width), BF16),
-            pltpu.VMEM((WINDOW, step, units), BF16),
-            pltpu.VMEM((WINDOW, step, units), BF16),
+            pltpu.VMEM((2, step, units), BF16),
+            pltpu.VMEM((2, step, units), BF16),
             pltpu.SemaphoreType.DMA((2,)),
-            ring,
-            ring,
+            pltpu.SemaphoreType.DMA((2,)),
+            pltpu.SemaphoreType.DMA((2,)),
         ],
         compiler_params=params(room),
         cost_estimate=pl.CostEstimate(

time: 124 us -> 124 us (level)
  no operation moved by 1% of the time
where the time goes in v8:
time: 124 us; the launch traced here: 123 us
  Pallas kernels  56 us (45%)
  starting transfers between devices  37.2 us (30%)
  waiting for transfers between devices  23 us (19%)
  other arithmetic  3.73 us (3%)
  local copies, waits for them, and re-layouts  2.26 us (2%)
    pallas_call x1, Pallas kernels, local(): pl.pallas_call(lambda *refs: backward(order, cuts, deep_cuts, *refs), out...  21.6 us
    pallas_call x1, Pallas kernels, local(): pl.pallas_call(weight_grads, grid=(width // step,), out_shape=(shape((wid...  16.7 us
    all_to_all x3, waiting for transfers between devices, local(): message = lax.all_to_all(message, everyone, 0, 0, tiled=True)  12.3 us
    ppermute x7, starting transfers between devices, local(): lax.ppermute(by_mask[mask], 'dp', [(i, i ^ mask) for i in range(owners)])  11.8 us
    pallas_call x1, Pallas kernels, local(): pl.pallas_call(forward, out_shape=(shape((tokens, width), BF16), shape((t...  11.8 us
    all_to_all x3, starting transfers between devices, local(): message = lax.all_to_all(message, everyone, 0, 0, tiled=True)  9 us
    ppermute x3, starting transfers between devices, double(): x_far = lax.ppermute(x_half, 'dp', swap)  7.21 us
    ppermute x3, starting transfers between devices, double(): moved[:] = [x_far, lax.ppermute(cot_half, 'dp', swap)]  6.39 us
  transfers between devices with their start and end apart: 17, of which 5 were waited for; matrix products, arithmetic and copies ran while one was open for 3% of the time, Pallas kernels for 27%

profile of v8, /device:TPU:0, one launch (start us, length us, event | category | flops | bytes accessed | tf_op | source)
XLA Modules:
  0.0 123.1 jit_solution(16259643780076005698)
XLA Ops:
  0.6 4.1 %collective-permute-start = (bf16[16,4096]{1,0:T(8,128)(2,1)}, bf16[16,4096]{1,0:T(8,128)(2,1)S(1)}, u32[]{:S(2)}, u32[]{:S(2)}) collective-permute-start(bf16[16,4096]{1,0:T(8,128)(2,1)} %bitcast.13), channel_id=1, source_target_pairs={{0,16},{4,20},{8,24},{12,28},{16,0},{20,4},{24,8},{28,12},{1,17},{... | collective-permute-start | bytes 393224 | tf_op jit(solution)/shard_map/ppermute | solution.py:533
  4.7 1.8 %pack_rows.1 = bf16[32,32,128]{2,1,0:T(8,128)(2,1)} custom-call(bf16[8,4096]{1,0:T(8,128)(2,1)} %query_hbm.1, bf16[8,4096]{1,0:T(8,128)(2,1)} %passage_hbm.1), custom_call_target="tpu_custom_call" | custom-call | tf_op jit(solution)/shard_map/pack_rows/pallas_call | solution.py:507
  6.6 3.8 %all-to-all-start = ((bf16[32,32,128]{2,1,0:T(8,128)(2,1)}), bf16[32,32,128]{2,1,0:T(8,128)(2,1)S(1)}, u32[]{:S(2)}, u32[]{:S(2)}) async-start(bf16[32,32,128]{2,1,0:T(8,128)(2,1)} %pack_rows.1), calls=%async_computation | async-start | bytes 524288 | tf_op jit(solution)/shard_map/all_to_all | solution.py:541
  10.4 2.7 %collective-permute-start.3 = (bf16[16,4096]{1,0:T(8,128)(2,1)}, bf16[16,4096]{1,0:T(8,128)(2,1)S(1)}, u32[]{:S(2)}, u32[]{:S(2)}) collective-permute-start(bf16[16,4096]{1,0:T(8,128)(2,1)} %bitcast.23), channel_id=1, source_target_pairs={{0,16},{4,20},{8,24},{12,28},{16,0},{20,4},{24,8},{28,12},{1,17},{... | collective-permute-start | bytes 393224 | tf_op jit(solution)/shard_map/ppermute | solution.py:536
  14.1 1.6 %collective-permute-start.1 = (bf16[32,4096]{1,0:T(8,128)(2,1)S(1)}, bf16[32,4096]{1,0:T(8,128)(2,1)S(1)}, u32[]{:S(2)}, u32[]{:S(2)}) collective-permute-start(bf16[32,4096]{1,0:T(8,128)(2,1)S(1)} %pad_maximum_fusion.2), channel_id=1, source_target_pairs={{0,8},{4,12},{8,0},{12,4},{16,24},{20,28},{24,16},{28,20},{1,9},{5... | collective-permute-start | bytes 786440 | tf_op jit(solution)/shard_map/ppermute | solution.py:533
  15.6 7.9 %all-to-all-done.rows_ref = bf16[32,32,128]{2,1,0:T(8,128)(2,1)S(1)} async-done(((bf16[32,32,128]{2,1,0:T(8,128)(2,1)}), bf16[32,32,128]{2,1,0:T(8,128)(2,1)S(1)}, u32[]{:S(2)}, u32[]{:S(2)}) %all-to-all-start) | async-done | bytes 262176 | tf_op jit(solution)/shard_map/all_to_all | solution.py:541
  24.5 2.8 %all-to-all-start.1 = ((f32[32,8,256]{2,1,0:T(8,128)}), f32[32,8,256]{2,1,0:T(8,128)S(1)}, u32[]{:S(2)}, u32[]{:S(2)}) async-start(f32[32,8,256]{2,1,0:T(8,128)} %get-tuple-element.35), calls=%async_computation.1 | async-start | bytes 524288 | tf_op jit(solution)/shard_map/all_to_all | solution.py:555
  28.3 1.8 %collective-permute-start.4 = (bf16[32,4096]{1,0:T(8,128)(2,1)S(1)}, bf16[32,4096]{1,0:T(8,128)(2,1)S(1)}, u32[]{:S(2)}, u32[]{:S(2)}) collective-permute-start(bf16[32,4096]{1,0:T(8,128)(2,1)S(1)} %pad_maximum_fusion.3), channel_id=1, source_target_pairs={{0,8},{4,12},{8,0},{12,4},{16,24},{20,28},{24,16},{28,20},{1,9},{5... | collective-permute-start | bytes 786440 | tf_op jit(solution)/shard_map/ppermute | solution.py:536
  31.1 1.5 %collective-permute-start.2 = (bf16[64,4096]{1,0:T(8,128)(2,1)S(1)}, bf16[64,4096]{1,0:T(8,128)(2,1)S(1)}, u32[]{:S(2)}, u32[]{:S(2)}) collective-permute-start(bf16[64,4096]{1,0:T(8,128)(2,1)S(1)} %pad_maximum_fusion.near_hbm.refs_4_), channel_id=1, source_target_pairs={{0,4},{4,0},{8,12},{12,8},{16,20},{20,16},{24,28},{28,24},{1,5},{5... | collective-permute-start | bytes 1572872 | tf_op jit(solution)/shard_map/ppermute | solution.py:533
  32.7 5.2 %all-to-all-done.1.parts_ref = f32[32,8,256]{2,1,0:T(8,128)S(1)} async-done(((f32[32,8,256]{2,1,0:T(8,128)}), f32[32,8,256]{2,1,0:T(8,128)S(1)}, u32[]{:S(2)}, u32[]{:S(2)}) %all-to-all-start.1) | async-done | bytes 262176 | tf_op jit(solution)/shard_map/all_to_all | solution.py:555
  39.5 2.6 %all-to-all-start.2 = ((bf16[32,16,256]{2,1,0:T(8,128)(2,1)}), bf16[32,16,256]{2,1,0:T(8,128)(2,1)S(1)}, u32[]{:S(2)}, u32[]{:S(2)}) async-start(bf16[32,16,256]{2,1,0:T(8,128)(2,1)} %softmax_rows.1), calls=%async_computation.2 | async-start | bytes 524288 | tf_op jit(solution)/shard_map/all_to_all | solution.py:565
  43.1 3.5 %collective-permute-done.2.far_hbm.refs_5_ = bf16[64,4096]{1,0:T(8,128)(2,1)S(1)} collective-permute-done((bf16[64,4096]{1,0:T(8,128)(2,1)S(1)}, bf16[64,4096]{1,0:T(8,128)(2,1)S(1)}, u32[]{:S(2)}, u32[]{:S(2)}) %collective-permute-start.2) | collective-permute-done | bytes 524320 | tf_op jit(solution)/shard_map/ppermute | solution.py:533
  46.5 1.8 %collective-permute-start.5 = (bf16[64,4096]{1,0:T(8,128)(2,1)S(1)}, bf16[64,4096]{1,0:T(8,128)(2,1)S(1)}, u32[]{:S(2)}, u32[]{:S(2)}) collective-permute-start(bf16[64,4096]{1,0:T(8,128)(2,1)S(1)} %pad_maximum_fusion.1.refs_6_), channel_id=1, source_target_pairs={{0,4},{4,0},{8,12},{12,8},{16,20},{20,16},{24,28},{28,24},{1,5},{5... | collective-permute-start | bytes 1572872 | tf_op jit(solution)/shard_map/ppermute | solution.py:536
  48.3 4.4 %all-to-all-done.2.refs_0_ = bf16[32,16,256]{2,1,0:T(8,128)(2,1)S(1)} async-done(((bf16[32,16,256]{2,1,0:T(8,128)(2,1)}), bf16[32,16,256]{2,1,0:T(8,128)(2,1)S(1)}, u32[]{:S(2)}, u32[]{:S(2)}) %all-to-all-start.2) | async-done | bytes 262176 | tf_op jit(solution)/shard_map/all_to_all | solution.py:565
  53.7 2.6 %all-to-all-start.3 = ((bf16[32,32,128]{2,1,0:T(8,128)(2,1)}), bf16[32,32,128]{2,1,0:T(8,128)(2,1)S(1)}, u32[]{:S(2)}, u32[]{:S(2)}) async-start(bf16[32,32,128]{2,1,0:T(8,128)(2,1)} %pair_grads.1), calls=%async_computation.3 | async-start | bytes 524288 | tf_op jit(solution)/shard_map/all_to_all | solution.py:575
  57.1 11.8 %forward.1 = (bf16[128,4096]{1,0:T(8,128)(2,1)}, f32[128,1792]{1,0:T(8,128)}, f32[128,1792]{1,0:T(8,128)}) custom-call(bf16[64,4096]{1,0:T(8,128)(2,1)S(1)} %pad_maximum_fusion.near_hbm.refs_4_, bf16[64,4096]{1,0:T(8,128)(2,1)} %copy-done.6, f32[1,4096]{1,0:T(1,128)S(1)} %copy-done.2, bf16[4096,1792]{1,0:T(8,128)(2,1)} %bitcast.18, bf16[4096,1792]{1,0:T(8,128)(2,1)} %bitcast.20), custom_call_target="tpu_custom_call" | custom-call | flops 3758096384 | bytes 29360128 | tf_op jit(solution)/shard_map/forward/pallas_call | solution.py:583
  69.8 21.6 %backward.1 = (bf16[8,4096]{1,0:T(8,128)(2,1)}, bf16[8,4096]{1,0:T(8,128)(2,1)}, bf16[128,1792]{1,0:T(8,128)(2,1)}, bf16[128,1792]{1,0:T(8,128)(2,1)}, bf16[128,...) custom-call(s32[1]{0:T(128)} %bitcast.refs_0_, ...), custom_call_target="tpu_custom_call" | custom-call | flops 5637144576 | bytes 44040192 | tf_op jit(solution)/shard_map/backward/pallas_call | solution.py:613
  91.5 1.7 %collective-permute-start.6 = (bf16[16,4352]{1,0:T(8,128)(2,1)S(1)}, bf16[16,4352]{1,0:T(8,128)(2,1)S(1)}, u32[]{:S(2)}, u32[]{:S(2)}) collective-permute-start(bf16[16,4352]{1,0:T(8,128)(2,1)S(1)} %get-tuple-element.45), channel_id=1, source_target_pairs={{0,4},{4,0},{8,12},{12,8},{16,20},{20,16},{24,28},{28,24},{1,5},{5... | collective-permute-start | bytes 417800 | tf_op jit(solution)/shard_map/ppermute | solution.py:662
  93.2 1.5 %collective-permute-start.7 = (bf16[16,4352]{1,0:T(8,128)(2,1)S(1)}, bf16[16,4352]{1,0:T(8,128)(2,1)S(1)}, u32[]{:S(2)}, u32[]{:S(2)}) collective-permute-start(bf16[16,4352]{1,0:T(8,128)(2,1)S(1)} %get-tuple-element.46), channel_id=1, source_target_pairs={{0,8},{4,12},{8,0},{12,4},{16,24},{20,28},{24,16},{28,20},{1,9},{5... | collective-permute-start | bytes 417800 | tf_op jit(solution)/shard_map/ppermute | solution.py:662
  95.0 2.7 %collective-permute-start.9 = (bf16[16,4352]{1,0:T(8,128)(2,1)S(1)}, bf16[16,4352]{1,0:T(8,128)(2,1)S(1)}, u32[]{:S(2)}, u32[]{:S(2)}) collective-permute-start(bf16[16,4352]{1,0:T(8,128)(2,1)S(1)} %get-tuple-element.48), channel_id=1, source_target_pairs={{0,16},{4,20},{8,24},{12,28},{16,0},{20,4},{24,8},{28,12},{1,17},{... | collective-permute-start | bytes 417800 | tf_op jit(solution)/shard_map/ppermute | solution.py:662
  97.7 1.3 %collective-permute-start.10 = (bf16[16,4352]{1,0:T(8,128)(2,1)S(1)}, bf16[16,4352]{1,0:T(8,128)(2,1)S(1)}, u32[]{:S(2)}, u32[]{:S(2)}) collective-permute-start(bf16[16,4352]{1,0:T(8,128)(2,1)S(1)} %get-tuple-element.49), channel_id=1, source_target_pairs={{0,20},{4,16},{8,28},{12,24},{16,4},{20,0},{24,12},{28,8},{1,21},{... | collective-permute-start | bytes 417800 | tf_op jit(solution)/shard_map/ppermute | solution.py:662
  99.0 3.5 %collective-permute-start.11 = (bf16[16,4352]{1,0:T(8,128)(2,1)}, bf16[16,4352]{1,0:T(8,128)(2,1)S(1)}, u32[]{:S(2)}, u32[]{:S(2)}) collective-permute-start(bf16[16,4352]{1,0:T(8,128)(2,1)} %get-tuple-element.50), channel_id=1, source_target_pairs={{0,24},{4,28},{8,16},{12,20},{16,8},{20,12},{24,0},{28,4},{1,25},{... | collective-permute-start | bytes 417800 | tf_op jit(solution)/shard_map/ppermute | solution.py:662
  102.5 2.0 %collective-permute-done.7.refs_2_ = bf16[16,4352]{1,0:T(8,128)(2,1)S(1)} collective-permute-done((bf16[16,4352]{1,0:T(8,128)(2,1)S(1)}, bf16[16,4352]{1,0:T(8,128)(2,1)S(1)}, u32[]{:S(2)}, u32[]{:S(2)}) %collective-permute-start.7) | collective-permute-done | bytes 139296 | tf_op jit(solution)/shard_map/ppermute | solution.py:662
  105.3 16.7 %weight_grads.1 = (bf16[4096,1792]{1,0:T(8,128)(2,1)}, bf16[4096,1792]{1,0:T(8,128)(2,1)}, bf16[1792,4096]{1,0:T(8,128)(2,1)}) custom-call(bf16[128,4096]{1,0:T(8,128)(2,1)} %get-tuple-element.54.normed_ref, bf16[128,1792]{1,0:T(8,128)(2,1)} %get-tuple-element.55.d_gate_ref, bf16[128,1792]{1,0:T(8,128)(2,1)} %get-tuple-element.56.d_up_ref, ...), custom_call_target="tpu_custom_call" | custom-call | flops 5637144576 | bytes 44040192 | tf_op jit(solution)/shard_map/weight_grads/pallas_call | solution.py:667
  (42 shorter events, 11.1 us)
Async XLA Ops:
  0.6 12.5 %collective-permute-start = (bf16[16,4096]{1,0:T(8,128)(2,1)}, bf16[16,4096]{1,0:T(8,128)(2,1)S(1)}, u32[]{:S(2)}, u32[]{:S(2)}) collective-permute-start(bf16[16,4096]{1,0:T(8,128)(2,1)} %bitcast.13), channel_id=1, source_target_pairs={{0,16},{4,20},{8,24},{12,28},{16,0},{20,4},{24,8},{28,12},{1,17},{... | collective-permute-start | bytes 393224 | tf_op jit(solution)/shard_map/ppermute | solution.py:533
  6.6 17.0 %all-to-all-start = ((bf16[32,32,128]{2,1,0:T(8,128)(2,1)}), bf16[32,32,128]{2,1,0:T(8,128)(2,1)S(1)}, u32[]{:S(2)}, u32[]{:S(2)}) async-start(bf16[32,32,128]{2,1,0:T(8,128)(2,1)} %pack_rows.1), calls=%async_computation | async-start | bytes 524288 | tf_op jit(solution)/shard_map/all_to_all | solution.py:541
  10.4 17.0 %collective-permute-start.3 = (bf16[16,4096]{1,0:T(8,128)(2,1)}, bf16[16,4096]{1,0:T(8,128)(2,1)S(1)}, u32[]{:S(2)}, u32[]{:S(2)}) collective-permute-start(bf16[16,4096]{1,0:T(8,128)(2,1)} %bitcast.23), channel_id=1, source_target_pairs={{0,16},{4,20},{8,24},{12,28},{16,0},{20,4},{24,8},{28,12},{1,17},{... | collective-permute-start | bytes 393224 | tf_op jit(solution)/shard_map/ppermute | solution.py:536
  14.1 16.1 %collective-permute-start.1 = (bf16[32,4096]{1,0:T(8,128)(2,1)S(1)}, bf16[32,4096]{1,0:T(8,128)(2,1)S(1)}, u32[]{:S(2)}, u32[]{:S(2)}) collective-permute-start(bf16[32,4096]{1,0:T(8,128)(2,1)S(1)} %pad_maximum_fusion.2), channel_id=1, source_target_pairs={{0,8},{4,12},{8,0},{12,4},{16,24},{20,28},{24,16},{28,20},{1,9},{5... | collective-permute-start | bytes 786440 | tf_op jit(solution)/shard_map/ppermute | solution.py:533
  24.5 13.3 %all-to-all-start.1 = ((f32[32,8,256]{2,1,0:T(8,128)}), f32[32,8,256]{2,1,0:T(8,128)S(1)}, u32[]{:S(2)}, u32[]{:S(2)}) async-start(f32[32,8,256]{2,1,0:T(8,128)} %get-tuple-element.35), calls=%async_computation.1 | async-start | bytes 524288 | tf_op jit(solution)/shard_map/all_to_all | solution.py:555
  28.3 13.8 %collective-permute-start.4 = (bf16[32,4096]{1,0:T(8,128)(2,1)S(1)}, bf16[32,4096]{1,0:T(8,128)(2,1)S(1)}, u32[]{:S(2)}, u32[]{:S(2)}) collective-permute-start(bf16[32,4096]{1,0:T(8,128)(2,1)S(1)} %pad_maximum_fusion.3), channel_id=1, source_target_pairs={{0,8},{4,12},{8,0},{12,4},{16,24},{20,28},{24,16},{28,20},{1,9},{5... | collective-permute-start | bytes 786440 | tf_op jit(solution)/shard_map/ppermute | solution.py:536
  31.1 37.8 %copy-start = (bf16[64,4096]{1,0:T(8,128)(2,1)}, bf16[64,4096]{1,0:T(8,128)(2,1)S(1)}, u32[]{:S(2)}) copy-start(bf16[64,4096]{1,0:T(8,128)(2,1)S(1)} %pad_maximum_fusion.near_hbm.refs_4_) | copy-start | bytes 1572868
  31.1 15.4 %collective-permute-start.2 = (bf16[64,4096]{1,0:T(8,128)(2,1)S(1)}, bf16[64,4096]{1,0:T(8,128)(2,1)S(1)}, u32[]{:S(2)}, u32[]{:S(2)}) collective-permute-start(bf16[64,4096]{1,0:T(8,128)(2,1)S(1)} %pad_maximum_fusion.near_hbm.refs_4_), channel_id=1, source_target_pairs={{0,4},{4,0},{8,12},{12,8},{16,20},{20,16},{24,28},{28,24},{1,5},{5... | collective-permute-start | bytes 1572872 | tf_op jit(solution)/shard_map/ppermute | solution.py:533
  39.5 13.2 %all-to-all-start.2 = ((bf16[32,16,256]{2,1,0:T(8,128)(2,1)}), bf16[32,16,256]{2,1,0:T(8,128)(2,1)S(1)}, u32[]{:S(2)}, u32[]{:S(2)}) async-start(bf16[32,16,256]{2,1,0:T(8,128)(2,1)} %softmax_rows.1), calls=%async_computation.2 | async-start | bytes 524288 | tf_op jit(solution)/shard_map/all_to_all | solution.py:565
  43.1 25.8 %copy-start.7 = (bf16[64,4096]{1,0:T(8,128)(2,1)}, bf16[64,4096]{1,0:T(8,128)(2,1)S(1)}, u32[]{:S(2)}) copy-start(bf16[64,4096]{1,0:T(8,128)(2,1)S(1)} %pad_maximum_fusion.1.refs_6_) | copy-start | bytes 1572868
  46.5 9.8 %copy-start.6 = (bf16[64,4096]{1,0:T(8,128)(2,1)}, bf16[64,4096]{1,0:T(8,128)(2,1)S(1)}, u32[]{:S(2)}) copy-start(bf16[64,4096]{1,0:T(8,128)(2,1)S(1)} %collective-permute-done.2.far_hbm.refs_5_) | copy-start | bytes 1572868
  46.5 22.4 %collective-permute-start.5 = (bf16[64,4096]{1,0:T(8,128)(2,1)S(1)}, bf16[64,4096]{1,0:T(8,128)(2,1)S(1)}, u32[]{:S(2)}, u32[]{:S(2)}) collective-permute-start(bf16[64,4096]{1,0:T(8,128)(2,1)S(1)} %pad_maximum_fusion.1.refs_6_), channel_id=1, source_target_pairs={{0,4},{4,0},{8,12},{12,8},{16,20},{20,16},{24,28},{28,24},{1,5},{5... | collective-permute-start | bytes 1572872 | tf_op jit(solution)/shard_map/ppermute | solution.py:536
  53.7 15.2 %all-to-all-start.3 = ((bf16[32,32,128]{2,1,0:T(8,128)(2,1)}), bf16[32,32,128]{2,1,0:T(8,128)(2,1)S(1)}, u32[]{:S(2)}, u32[]{:S(2)}) async-start(bf16[32,32,128]{2,1,0:T(8,128)(2,1)} %pair_grads.1), calls=%async_computation.3 | async-start | bytes 524288 | tf_op jit(solution)/shard_map/all_to_all | solution.py:575
  57.1 12.7 %copy-start.4 = (s32[8]{0:T(128)S(1)}, s32[8]{0:T(128)}, u32[]{:S(2)}) copy-start(s32[8]{0:T(128)} %refs_2_.1) | copy-start | bytes 100
  68.9 0.9 copy-start.8
  91.4 30.6 %copy-start.1 = (bf16[1,16,4096]{2,1,0:T(8,128)(2,1)S(1)}, bf16[1,16,4096]{2,1,0:T(8,128)(2,1)}, u32[]{:S(2)}) copy-start(bf16[1,16,4096]{2,1,0:T(8,128)(2,1)} %param.14) | copy-start | bytes 393220
  91.5 30.6 %copy-start.3 = (f32[1,4096]{1,0:T(1,128)S(1)}, f32[1,4096]{1,0:T(1,128)}, u32[]{:S(2)}) copy-start(f32[1,4096]{1,0:T(1,128)} %refs_10_.1) | copy-start | bytes 49156
  91.5 7.6 %collective-permute-start.6 = (bf16[16,4352]{1,0:T(8,128)(2,1)S(1)}, bf16[16,4352]{1,0:T(8,128)(2,1)S(1)}, u32[]{:S(2)}, u32[]{:S(2)}) collective-permute-start(bf16[16,4352]{1,0:T(8,128)(2,1)S(1)} %get-tuple-element.45), channel_id=1, source_target_pairs={{0,4},{4,0},{8,12},{12,8},{16,20},{20,16},{24,28},{28,24},{1,5},{5... | collective-permute-start | bytes 417800 | tf_op jit(solution)/shard_map/ppermute | solution.py:662
  93.2 11.4 %collective-permute-start.7 = (bf16[16,4352]{1,0:T(8,128)(2,1)S(1)}, bf16[16,4352]{1,0:T(8,128)(2,1)S(1)}, u32[]{:S(2)}, u32[]{:S(2)}) collective-permute-start(bf16[16,4352]{1,0:T(8,128)(2,1)S(1)} %get-tuple-element.46), channel_id=1, source_target_pairs={{0,8},{4,12},{8,0},{12,4},{16,24},{20,28},{24,16},{28,20},{1,9},{5... | collective-permute-start | bytes 417800 | tf_op jit(solution)/shard_map/ppermute | solution.py:662
  94.7 27.3 %collective-permute-start.8 = (bf16[16,4352]{1,0:T(8,128)(2,1)S(1)}, bf16[16,4352]{1,0:T(8,128)(2,1)S(1)}, u32[]{:S(2)}, u32[]{:S(2)}) collective-permute-start(bf16[16,4352]{1,0:T(8,128)(2,1)S(1)} %get-tuple-element.47), channel_id=1, source_target_pairs={{0,12},{4,8},{8,4},{12,0},{16,28},{20,24},{24,20},{28,16},{1,13},{... | collective-permute-start | bytes 417800 | tf_op jit(solution)/shard_map/ppermute | solution.py:662
  95.0 27.0 %collective-permute-start.9 = (bf16[16,4352]{1,0:T(8,128)(2,1)S(1)}, bf16[16,4352]{1,0:T(8,128)(2,1)S(1)}, u32[]{:S(2)}, u32[]{:S(2)}) collective-permute-start(bf16[16,4352]{1,0:T(8,128)(2,1)S(1)} %get-tuple-element.48), channel_id=1, source_target_pairs={{0,16},{4,20},{8,24},{12,28},{16,0},{20,4},{24,8},{28,12},{1,17},{... | collective-permute-start | bytes 417800 | tf_op jit(solution)/shard_map/ppermute | solution.py:662
  97.7 24.4 %collective-permute-start.10 = (bf16[16,4352]{1,0:T(8,128)(2,1)S(1)}, bf16[16,4352]{1,0:T(8,128)(2,1)S(1)}, u32[]{:S(2)}, u32[]{:S(2)}) collective-permute-start(bf16[16,4352]{1,0:T(8,128)(2,1)S(1)} %get-tuple-element.49), channel_id=1, source_target_pairs={{0,20},{4,16},{8,28},{12,24},{16,4},{20,0},{24,12},{28,8},{1,21},{... | collective-permute-start | bytes 417800 | tf_op jit(solution)/shard_map/ppermute | solution.py:662
  99.0 23.0 %collective-permute-start.11 = (bf16[16,4352]{1,0:T(8,128)(2,1)}, bf16[16,4352]{1,0:T(8,128)(2,1)S(1)}, u32[]{:S(2)}, u32[]{:S(2)}) collective-permute-start(bf16[16,4352]{1,0:T(8,128)(2,1)} %get-tuple-element.50), channel_id=1, source_target_pairs={{0,24},{4,28},{8,16},{12,20},{16,8},{20,12},{24,0},{28,4},{1,25},{... | collective-permute-start | bytes 417800 | tf_op jit(solution)/shard_map/ppermute | solution.py:662
  104.5 17.5 %collective-permute-start.12 = (bf16[16,4352]{1,0:T(8,128)(2,1)}, bf16[16,4352]{1,0:T(8,128)(2,1)S(1)}, u32[]{:S(2)}, u32[]{:S(2)}) collective-permute-start(bf16[16,4352]{1,0:T(8,128)(2,1)} %get-tuple-element.51), channel_id=1, source_target_pairs={{0,28},{4,24},{8,20},{12,16},{16,12},{20,8},{24,4},{28,0},{1,29},{... | collective-permute-start | bytes 417800 | tf_op jit(solution)/shard_map/ppermute | solution.py:662
  (3 other events, 2.2 us)
